TPU v7x, 512 devices: a whole 4x8x8 slice. The times are simulated.
512 devices in a mesh: gx: 128 (over x, z, y_lo), gy: 4 (over y_hi, core).
Axes of the slice: x: 4, y: 8 (y_hi: 2, y_lo: 4; y = y_hi * 4 + y_lo), z: 8, core: 2. Of those that a mesh axis runs over, the one named last changes fastest.
Arguments:
- tangent: float32 [8, 5, 512, 16, 128], P(None, None, 'gx', 'gy'), may hold values from -6 to 6
- base_state: float32 [5, 512, 16, 128], P(None, 'gx', 'gy'), may hold values from -0.5 to 4, as said below
- shock_flags: int32 [128, 4, 32], P('gx', 'gy'), may hold values from 0 to 1, as said below
Outputs:
- tangent_out: float32 [8, 5, 512, 16, 128], P(None, None, 'gx', 'gy')
Inputs may be any that keep to these rules, and one draw needn't show every extreme that they name: `base_state`: every node holds a state with density from 0.6 to 1.4 and pressure above 0.5. `shock_flags`: every block of 1 x 1 x 32 elements of one device holds at least one and at most 16 flagged elements; some block holds exactly 16.
All inputs are finite; a program needn't handle non-finite values.
Results may differ from a plain program's by a relative error of at most 0.0001.
Values sent between devices are 32-bit elements; how exact they have to be, the bound alone decides.
No kernel may reach another device: no remote copies, remote signals or barrier semaphores. Data moves between devices by JAX's collectives and lax.ppermute only.
A program may use at most 64 MiB of HBM per device.

v0:
```python
import math

import jax
import jax.numpy as jnp
import numpy as np
from jax import lax
from jax.sharding import PartitionSpec as P

GAMMA_MINUS = 0.4
STEP = 0.1
EPS_TOP = 0.1
SENSOR_MID = -2.3
SENSOR_WIDTH = 0.5
END_PENALTY = 6.0


def extended(value, sides, width):
    for axis, dim in sides:
        size, length = (lax.axis_size(axis), value.shape[dim])
        up = [(i, (i + 1) % size) for i in range(size - 1)]
        down = [(j, i) for i, j in up]
        last = lax.slice_in_dim(value, length - width, length, axis=dim)
        first = lax.slice_in_dim(value, 0, width, axis=dim)
        before = lax.ppermute(last, axis, up)
        after = lax.ppermute(first, axis, down)
        value = jnp.concatenate([before, value, after], axis=dim)
    return value


def legendre_values(x):
    return [1.0, x, 0.5 * (3.0 * x * x - 1.0), 0.5 * (5.0 * x * x * x - 3.0 * x)]


def node_tables():
    inner_point = math.sqrt(0.2)
    points = [-1.0, -inner_point, inner_point, 1.0]
    weights = [1.0 / 6.0, 5.0 / 6.0, 5.0 / 6.0, 1.0 / 6.0]
    barycentric = []
    for j in range(4):
        product = 1.0
        for k in range(4):
            if k != j:
                product = product * (points[j] - points[k])
        barycentric.append(1.0 / product)
    deriv_matrix = [[0.0] * 4 for i in range(4)]
    for i in range(4):
        for j in range(4):
            if j != i:
                deriv_matrix[i][j] = barycentric[j] / barycentric[i] / (points[i] - points[j])
        deriv_matrix[i][i] = -sum((deriv_matrix[i][j] for j in range(4) if j != i))
    norms_discrete = [2.0, 2.0 / 3.0, 2.0 / 5.0, 2.0 / 3.0]
    modal_matrix = [
        [weights[i] * legendre_values(points[i])[k] / norms_discrete[k] for i in range(4)]
        for k in range(4)
    ]
    return (deriv_matrix, modal_matrix)


def block_width(length):
    return 128 if length % 128 == 0 else length


def block_operator(matrix, width):
    table = np.zeros((width, width), np.float32)
    for start in range(0, width, 4):
        for i in range(4):
            for j in range(4):
                table[start + j, start + i] = matrix[i][j]
    return jnp.asarray(table, jnp.float32)


def pick_table(width, node):
    table = np.zeros((width, width // 4), np.float32)
    for element in range(width // 4):
        table[4 * element + node, element] = 1.0
    return jnp.asarray(table, jnp.float32)


def lane_product(f, table):
    leading = f.shape[:-1]
    rows = f.shape[-1] // table.shape[0]
    grouped = f.reshape(leading + (rows, table.shape[0]))
    result = jnp.einsum("...i,ij->...j", grouped, table, precision=lax.Precision.HIGHEST)
    return result.reshape(leading + (rows * table.shape[1],))


def node_slices(f, along):
    return [lax.slice_in_dim(f, j, f.shape[along], 4, along) for j in range(4)]


def face_pair(f, along):
    if along == f.ndim - 1:
        width = block_width(f.shape[-1])
        return (lane_product(f, pick_table(width, 0)), lane_product(f, pick_table(width, 3)))
    node_list = node_slices(f, along)
    return (node_list[0], node_list[3])


def first_slice(f, along):
    return lax.slice_in_dim(f, 0, 1, 1, along)


def last_slice(f, along):
    return lax.slice_in_dim(f, f.shape[along] - 1, f.shape[along], 1, along)


def alternate(pieces, along, full_shape):
    return jnp.stack(pieces, axis=along + 1).reshape(full_shape)


def combine(node_list, matrix, i):
    summed = matrix[i][0] * node_list[0]
    for j in range(1, 4):
        summed = summed + matrix[i][j] * node_list[j]
    return summed


def edge_value(node_list, i, star, matrix):
    value = combine(node_list, matrix, i)
    if i == 0:
        return value - END_PENALTY * (star - node_list[0])
    return value + END_PENALTY * (star - node_list[3])


def derivative(f, along, star_lower, star_upper, matrix):
    if along == f.ndim - 1:
        width = block_width(f.shape[-1])
        volume = lane_product(f, block_operator(matrix, width))
        lower_pick = pick_table(width, 0)
        upper_pick = pick_table(width, 3)
        lower_side = lane_product(f, lower_pick)
        upper_side = lane_product(f, upper_pick)
        volume = volume + lane_product(-END_PENALTY * (star_lower - lower_side), lower_pick.T)
        return volume + lane_product(END_PENALTY * (star_upper - upper_side), upper_pick.T)
    node_list = node_slices(f, along)
    pieces = [
        edge_value(node_list, 0, star_lower, matrix),
        combine(node_list, matrix, 1),
        combine(node_list, matrix, 2),
        edge_value(node_list, 3, star_upper, matrix),
    ]
    return alternate(pieces, along, f.shape)


def transform(f, matrix, along):
    if along == f.ndim - 1:
        return lane_product(f, block_operator(matrix, block_width(f.shape[-1])))
    node_list = node_slices(f, along)
    return alternate([combine(node_list, matrix, i) for i in range(4)], along, f.shape)


def partners(lower_side, upper_side, along, lower_ghost, upper_ghost):
    count = lower_side.shape[along]
    below = jnp.concatenate(
        [lower_ghost, lax.slice_in_dim(upper_side, 0, count - 1, 1, along)], axis=along
    )
    above = jnp.concatenate(
        [lax.slice_in_dim(lower_side, 1, count, 1, along), upper_ghost], axis=along
    )
    return (below, above)


def euler_flux(u, d):
    density = u[0]
    velocity = u[1 + d] / density
    pressure = GAMMA_MINUS * (u[4] - 0.5 * (u[1] * u[1] + u[2] * u[2] + u[3] * u[3]) / density)
    components = [
        u[1 + d],
        u[1] * velocity,
        u[2] * velocity,
        u[3] * velocity,
        (u[4] + pressure) * velocity,
    ]
    components[1 + d] = components[1 + d] + pressure
    return jnp.stack(components)


def tangent_flux(u, t, d):
    return jax.vmap(lambda column: jax.jvp(lambda state: euler_flux(state, d), (u,), (column,))[1])(
        t
    )


def wave_speed(u, d):
    density = u[0]
    pressure = GAMMA_MINUS * (u[4] - 0.5 * (u[1] * u[1] + u[2] * u[2] + u[3] * u[3]) / density)
    return jnp.abs(u[1 + d] / density) + jnp.sqrt(1.4 * pressure / density)


def viscosity(base_state, shock_flags, modal_matrix):
    modal_coefs = base_state[0]
    for along in range(3):
        modal_coefs = transform(modal_coefs, modal_matrix, along)
    blocked = modal_coefs.reshape(
        modal_coefs.shape[0] // 4, 4, modal_coefs.shape[1] // 4, 4, modal_coefs.shape[2] // 4, 4
    )
    squares = blocked * blocked
    top_mask = np.ones((4, 4, 4), np.float32)
    top_mask[:3, :3, :3] = 0.0
    top_mask = jnp.asarray(top_mask, jnp.float32).reshape(1, 4, 1, 4, 1, 4)
    total_energy = jnp.sum(squares, axis=(1, 3, 5))
    top_energy = jnp.sum(squares * top_mask, axis=(1, 3, 5))
    sensor = jnp.log10(top_energy / total_energy + 1e-10)
    return (
        EPS_TOP
        * shock_flags.astype(jnp.float32)
        * jax.nn.sigmoid((sensor - SENSOR_MID) / SENSOR_WIDTH)
    )


def spread_nodes(per_element):
    return jnp.repeat(jnp.repeat(jnp.repeat(per_element, 4, axis=0), 4, axis=1), 4, axis=2)


def section_residual(tangent, base_state, base_faces, coef_nodes, domain_edges, matrix):
    padded = extended(tangent, (("gx", 2), ("gy", 3)), 1)
    rim_values = [
        (padded[:, :, 0:1, 1:-1, :], padded[:, :, -1:, 1:-1, :]),
        (padded[:, :, 1:-1, 0:1, :], padded[:, :, 1:-1, -1:, :]),
    ]
    face_values = []
    averages = []
    for d in range(3):
        along = 2 + d
        tan_lower, tan_upper = face_pair(tangent, along)
        if d < 2:
            ghost_lower = jnp.where(
                domain_edges[2 * d], first_slice(tan_lower, along), rim_values[d][0]
            )
            ghost_upper = jnp.where(
                domain_edges[2 * d + 1], last_slice(tan_upper, along), rim_values[d][1]
            )
        else:
            ghost_lower, ghost_upper = (last_slice(tan_upper, along), first_slice(tan_lower, along))
        tan_below, tan_above = partners(tan_lower, tan_upper, along, ghost_lower, ghost_upper)
        face_values.append((tan_lower, tan_upper, tan_below, tan_above))
        averages.append((0.5 * (tan_lower + tan_below), 0.5 * (tan_upper + tan_above)))
    lifted = tuple(
        (
            coef_nodes * derivative(tangent, 2 + d, averages[d][0], averages[d][1], matrix)
            for d in range(3)
        )
    )
    summed = jnp.zeros_like(tangent)
    for d in range(3):
        along = 2 + d
        lift_lower, lift_upper = face_pair(lifted[d], along)
        if d < 2:
            if d == 0:
                lift_padded = extended(lifted[0], (("gx", 2),), 1)
                raw_lower, raw_upper = (lift_padded[:, :, 0:1], lift_padded[:, :, -1:])
            else:
                lift_padded = extended(lifted[1], (("gy", 3),), 1)
                raw_lower, raw_upper = (lift_padded[:, :, :, 0:1], lift_padded[:, :, :, -1:])
            ghost_lower = jnp.where(domain_edges[2 * d], first_slice(lift_lower, along), raw_lower)
            ghost_upper = jnp.where(
                domain_edges[2 * d + 1], last_slice(lift_upper, along), raw_upper
            )
        else:
            ghost_lower, ghost_upper = (
                last_slice(lift_upper, along),
                first_slice(lift_lower, along),
            )
        lift_below, lift_above = partners(lift_lower, lift_upper, along, ghost_lower, ghost_upper)
        visc_lower = 0.5 * (lift_lower + lift_below)
        visc_upper = 0.5 * (lift_upper + lift_above)
        base_below, base_above, speed_lower, speed_upper = base_faces[d]
        tan_lower, tan_upper, tan_below, tan_above = face_values[d]
        flux = tangent_flux(base_state, tangent, d)
        flux_lower, flux_upper = face_pair(flux, along)
        flux_below = tangent_flux(base_below, tan_below, d)
        flux_above = tangent_flux(base_above, tan_above, d)
        star_lower = 0.5 * (flux_below + flux_lower) - 0.5 * speed_lower * (tan_lower - tan_below)
        star_upper = 0.5 * (flux_upper + flux_above) - 0.5 * speed_upper * (tan_above - tan_upper)
        summed = summed + (
            derivative(lifted[d], along, visc_lower, visc_upper, matrix)
            - derivative(flux, along, star_lower, star_upper, matrix)
        )
    return summed


def per_device(tangent, base_state, shock_flags):
    deriv_matrix, modal_matrix = node_tables()
    index_x = lax.axis_index("gx")
    index_y = lax.axis_index("gy")
    domain_edges = (
        index_x == 0,
        index_x == lax.axis_size("gx") - 1,
        index_y == 0,
        index_y == lax.axis_size("gy") - 1,
    )
    coef_nodes = spread_nodes(viscosity(base_state, shock_flags, modal_matrix))
    padded = extended(base_state, (("gx", 1), ("gy", 2)), 1)
    rim_values = [
        (padded[:, 0:1, 1:-1, :], padded[:, -1:, 1:-1, :]),
        (padded[:, 1:-1, 0:1, :], padded[:, 1:-1, -1:, :]),
    ]
    base_faces = []
    for d in range(3):
        along = 1 + d
        base_lower, base_upper = face_pair(base_state, along)
        if d < 2:
            ghost_lower = jnp.where(
                domain_edges[2 * d], first_slice(base_lower, along), rim_values[d][0]
            )
            ghost_upper = jnp.where(
                domain_edges[2 * d + 1], last_slice(base_upper, along), rim_values[d][1]
            )
        else:
            ghost_lower, ghost_upper = (
                last_slice(base_upper, along),
                first_slice(base_lower, along),
            )
        base_below, base_above = partners(base_lower, base_upper, along, ghost_lower, ghost_upper)
        speed_lower = jnp.maximum(wave_speed(base_lower, d), wave_speed(base_below, d))
        speed_upper = jnp.maximum(wave_speed(base_upper, d), wave_speed(base_above, d))
        base_faces.append((base_below, base_above, speed_lower, speed_upper))

    def evaluate(current):
        return section_residual(
            current, base_state, base_faces, coef_nodes, domain_edges, deriv_matrix
        )

    section_one = tangent + STEP * evaluate(tangent)
    return 0.5 * tangent + 0.5 * (section_one + STEP * evaluate(section_one))


def solution(mesh):
    in_specs = (P(None, None, "gx", "gy", None), P(None, "gx", "gy", None), P("gx", "gy", None))
    out_specs = P(None, None, "gx", "gy", None)
    return jax.shard_map(
        per_device, mesh=mesh, in_specs=in_specs, out_specs=out_specs, check_vma=False
    )
```

profile of v0, /device:TPU:7, one launch (start us, length us, event | category | flops | bytes accessed | tf_op | source)
XLA Modules:
  0.0 177.3 jit_solution(2758402080246245316)
XLA Ops:
  0.0 1.0 fusion.553
  1.7 14.0 %collective-permute-start.1 = (f32[8,5,1,4,128]{4,0,3,1,2:T(8,128)}, f32[8,5,1,4,128]{4,0,3,1,2:T(8,128)}, u32[]{:S(2)}, u32[]{:S(2)}) collective-permute-start(f32[8,5,1,4,128]{4,0,3,1,2:T(8,128)} %copy.1569), channel_id=1, source_target_pairs={{4,0},{8,4},{12,8},{16,12},{20,16},{24,20},{28,24},{32,28},{36,32}... | collective-permute-start | bytes 245768 | tf_op jit(solution)/shard_map/ppermute | solution.py:25
  16.3 1.9 %collective-permute-start.4 = (f32[5,1,4,128]{3,2,1,0:T(4,128)}, f32[5,1,4,128]{3,2,1,0:T(4,128)}, u32[]{:S(2)}, u32[]{:S(2)}) collective-permute-start(f32[5,1,4,128]{3,2,1,0:T(4,128)} %slice.571), channel_id=1, source_target_pairs={{0,4},{4,8},{8,12},{12,16},{16,20},{20,24},{24,28},{28,32},{32,36}... | collective-permute-start | bytes 30728 | tf_op jit(solution)/shard_map/ppermute | solution.py:24
  37.2 8.2 %collective-permute-start.5 = (f32[5,1,4,128]{3,1,2,0:T(1,128)S(1)}, f32[5,1,4,128]{3,1,2,0:T(1,128)S(1)}, u32[]{:S(2)}, u32[]{:S(2)}) collective-permute-start(f32[5,1,4,128]{3,1,2,0:T(1,128)S(1)} %bitcast.2652), channel_id=1, source_target_pairs={{4,0},{8,4},{12,8},{16,12},{20,16},{24,20},{28,24},{32,28},{36,32}... | collective-permute-start | bytes 30728 | tf_op jit(solution)/shard_map/ppermute | solution.py:25
  46.9 6.7 %collective-permute-start.10 = (f32[5,6,1,128]{3,1,2,0:T(8,128)S(1)}, f32[5,6,1,128]{3,1,2,0:T(8,128)S(1)}, u32[]{:S(2)}, u32[]{:S(2)}) collective-permute-start(f32[5,6,1,128]{3,1,2,0:T(8,128)S(1)} %get-tuple-element.217), channel_id=1, source_target_pairs={{0,1},{1,2},{2,3},{4,5},{5,6},{6,7},{8,9},{9,10},{10,11},{12,13},{... | collective-permute-start | bytes 46088 | tf_op jit(solution)/shard_map/ppermute | solution.py:24
  53.6 1.9 %collective-permute-start.11 = (f32[5,6,1,128]{3,1,2,0:T(8,128)S(1)}, f32[5,6,1,128]{3,1,2,0:T(8,128)S(1)}, u32[]{:S(2)}, u32[]{:S(2)}) collective-permute-start(f32[5,6,1,128]{3,1,2,0:T(8,128)S(1)} %get-tuple-element.218), channel_id=1, source_target_pairs={{1,0},{2,1},{3,2},{5,4},{6,5},{7,6},{9,8},{10,9},{11,10},{13,12},{... | collective-permute-start | bytes 46088 | tf_op jit(solution)/shard_map/ppermute | solution.py:25
  55.7 7.0 %collective-permute-done.11 = f32[5,6,1,128]{3,1,2,0:T(8,128)S(1)} collective-permute-done((f32[5,6,1,128]{3,1,2,0:T(8,128)S(1)}, f32[5,6,1,128]{3,1,2,0:T(8,128)S(1)}, u32[]{:S(2)}, u32[]{:S(2)}) %collective-permute-start.11) | collective-permute-done | bytes 15392 | tf_op jit(solution)/shard_map/ppermute | solution.py:25
  62.7 0.9 fusion.243
  63.7 1.9 %collective-permute-start = (f32[8,5,1,4,128]{4,0,3,1,2:T(8,128)S(1)}, f32[8,5,1,4,128]{4,0,3,1,2:T(8,128)S(1)}, u32[]{:S(2)}, u32[]{:S(2)}) collective-permute-start(f32[8,5,1,4,128]{4,0,3,1,2:T(8,128)S(1)} %get-tuple-element.197), channel_id=1, source_target_pairs={{0,4},{4,8},{8,12},{12,16},{16,20},{20,24},{24,28},{28,32},{32,36}... | collective-permute-start | bytes 245768 | tf_op jit(solution)/shard_map/ppermute | solution.py:24
  65.7 8.5 %collective-permute-done = f32[8,5,1,4,128]{4,0,3,1,2:T(8,128)S(1)} collective-permute-done((f32[8,5,1,4,128]{4,0,3,1,2:T(8,128)S(1)}, f32[8,5,1,4,128]{4,0,3,1,2:T(8,128)S(1)}, u32[]{:S(2)}, u32[]{:S(2)}) %collective-permute-start) | collective-permute-done | bytes 81952 | tf_op jit(solution)/shard_map/ppermute | solution.py:24
  75.1 1.9 %collective-permute-start.2 = (f32[8,5,1,4,128]{4,0,3,1,2:T(8,128)S(1)}, f32[8,5,1,4,128]{4,0,3,1,2:T(8,128)S(1)}, u32[]{:S(2)}, u32[]{:S(2)}) collective-permute-start(f32[8,5,1,4,128]{4,0,3,1,2:T(8,128)S(1)} %get-tuple-element.184), channel_id=1, source_target_pairs={{0,4},{4,8},{8,12},{12,16},{16,20},{20,24},{24,28},{28,32},{32,36}... | collective-permute-start | bytes 245768 | tf_op jit(solution)/shard_map/ppermute | solution.py:24
  77.0 8.2 %collective-permute-start.3 = (f32[8,5,1,4,128]{4,0,3,1,2:T(8,128)S(1)}, f32[8,5,1,4,128]{4,0,3,1,2:T(8,128)S(1)}, u32[]{:S(2)}, u32[]{:S(2)}) collective-permute-start(f32[8,5,1,4,128]{4,0,3,1,2:T(8,128)S(1)} %get-tuple-element.186), channel_id=1, source_target_pairs={{4,0},{8,4},{12,8},{16,12},{20,16},{24,20},{28,24},{32,28},{36,32}... | collective-permute-start | bytes 245768 | tf_op jit(solution)/shard_map/ppermute | solution.py:25
  85.2 0.8 pad_maximum_fusion.9
  85.9 3.4 %collective-permute-start.6 = (f32[8,5,6,1,128]{4,0,2,3,1:T(8,128)S(1)}, f32[8,5,6,1,128]{4,0,2,3,1:T(8,128)S(1)}, u32[]{:S(2)}, u32[]{:S(2)}) collective-permute-start(f32[8,5,6,1,128]{4,0,2,3,1:T(8,128)S(1)} %get-tuple-element.109), channel_id=1, source_target_pairs={{0,1},{1,2},{2,3},{4,5},{5,6},{6,7},{8,9},{9,10},{10,11},{12,13},{... | collective-permute-start | bytes 368648 | tf_op jit(solution)/shard_map/ppermute | solution.py:24
  89.4 1.9 %collective-permute-start.7 = (f32[8,5,6,1,128]{4,0,2,3,1:T(8,128)S(1)}, f32[8,5,6,1,128]{4,0,2,3,1:T(8,128)S(1)}, u32[]{:S(2)}, u32[]{:S(2)}) collective-permute-start(f32[8,5,6,1,128]{4,0,2,3,1:T(8,128)S(1)} %get-tuple-element.110), channel_id=1, source_target_pairs={{1,0},{2,1},{3,2},{5,4},{6,5},{7,6},{9,8},{10,9},{11,10},{13,12},{... | collective-permute-start | bytes 368648 | tf_op jit(solution)/shard_map/ppermute | solution.py:25
  91.7 7.8 %collective-permute-done.7 = f32[8,5,6,1,128]{4,0,2,3,1:T(8,128)S(1)} collective-permute-done((f32[8,5,6,1,128]{4,0,2,3,1:T(8,128)S(1)}, f32[8,5,6,1,128]{4,0,2,3,1:T(8,128)S(1)}, u32[]{:S(2)}, u32[]{:S(2)}) %collective-permute-start.7) | collective-permute-done | bytes 122912 | tf_op jit(solution)/shard_map/ppermute | solution.py:25
  99.9 1.9 %collective-permute-start.8 = (f32[8,5,4,1,128]{4,0,2,3,1:T(8,128)S(1)}, f32[8,5,4,1,128]{4,0,2,3,1:T(8,128)S(1)}, u32[]{:S(2)}, u32[]{:S(2)}) collective-permute-start(f32[8,5,4,1,128]{4,0,2,3,1:T(8,128)S(1)} %slice_bitcast_fusion.18), channel_id=1, source_target_pairs={{0,1},{1,2},{2,3},{4,5},{5,6},{6,7},{8,9},{9,10},{10,11},{12,13},{... | collective-permute-start | bytes 245768 | tf_op jit(solution)/shard_map/ppermute | solution.py:24
  101.8 1.4 collective-permute-done.8
  103.4 2.1 %collective-permute-start.9 = (f32[8,5,4,1,128]{4,0,2,1,3:T(8,128)S(1)}, f32[8,5,4,1,128]{4,0,2,1,3:T(8,128)S(1)}, u32[]{:S(2)}, u32[]{:S(2)}) collective-permute-start(f32[8,5,4,1,128]{4,0,2,1,3:T(8,128)S(1)} %get-tuple-element.193), channel_id=1, source_target_pairs={{1,0},{2,1},{3,2},{5,4},{6,5},{7,6},{9,8},{10,9},{11,10},{13,12},{... | collective-permute-start | bytes 245768 | tf_op jit(solution)/shard_map/ppermute | solution.py:25
  105.6 8.1 %collective-permute-done.9 = f32[8,5,4,1,128]{4,0,2,1,3:T(8,128)S(1)} collective-permute-done((f32[8,5,4,1,128]{4,0,2,1,3:T(8,128)S(1)}, f32[8,5,4,1,128]{4,0,2,1,3:T(8,128)S(1)}, u32[]{:S(2)}, u32[]{:S(2)}) %collective-permute-start.9) | collective-permute-done | bytes 81952 | tf_op jit(solution)/shard_map/ppermute | solution.py:25
  119.8 1.9 %collective-permute-start.13 = (f32[8,5,1,4,128]{4,0,3,1,2:T(8,128)S(1)}, f32[8,5,1,4,128]{4,0,3,1,2:T(8,128)S(1)}, u32[]{:S(2)}, u32[]{:S(2)}) collective-permute-start(f32[8,5,1,4,128]{4,0,3,1,2:T(8,128)S(1)} %copy.1581), channel_id=1, source_target_pairs={{4,0},{8,4},{12,8},{16,12},{20,16},{24,20},{28,24},{32,28},{36,32}... | collective-permute-start | bytes 245768 | tf_op jit(solution)/shard_map/ppermute | solution.py:25
  121.8 3.4 %collective-permute-start.12 = (f32[8,5,1,4,128]{4,0,3,1,2:T(8,128)S(1)}, f32[8,5,1,4,128]{4,0,3,1,2:T(8,128)S(1)}, u32[]{:S(2)}, u32[]{:S(2)}) collective-permute-start(f32[8,5,1,4,128]{4,0,3,1,2:T(8,128)S(1)} %copy.1584), channel_id=1, source_target_pairs={{0,4},{4,8},{8,12},{12,16},{16,20},{20,24},{24,28},{28,32},{32,36}... | collective-permute-start | bytes 245768 | tf_op jit(solution)/shard_map/ppermute | solution.py:24
  139.1 1.9 %collective-permute-start.14 = (f32[8,5,1,4,128]{4,0,3,1,2:T(8,128)S(1)}, f32[8,5,1,4,128]{4,0,3,1,2:T(8,128)S(1)}, u32[]{:S(2)}, u32[]{:S(2)}) collective-permute-start(f32[8,5,1,4,128]{4,0,3,1,2:T(8,128)S(1)} %get-tuple-element.143), channel_id=1, source_target_pairs={{0,4},{4,8},{8,12},{12,16},{16,20},{20,24},{24,28},{28,32},{32,36}... | collective-permute-start | bytes 245768 | tf_op jit(solution)/shard_map/ppermute | solution.py:24
  141.0 8.2 %collective-permute-start.15 = (f32[8,5,1,4,128]{4,0,3,1,2:T(8,128)S(1)}, f32[8,5,1,4,128]{4,0,3,1,2:T(8,128)S(1)}, u32[]{:S(2)}, u32[]{:S(2)}) collective-permute-start(f32[8,5,1,4,128]{4,0,3,1,2:T(8,128)S(1)} %get-tuple-element.144), channel_id=1, source_target_pairs={{4,0},{8,4},{12,8},{16,12},{20,16},{24,20},{28,24},{32,28},{36,32}... | collective-permute-start | bytes 245768 | tf_op jit(solution)/shard_map/ppermute | solution.py:25
  149.2 3.0 %collective-permute-start.16 = (f32[8,5,6,1,128]{4,0,2,3,1:T(8,128)S(1)}, f32[8,5,6,1,128]{4,0,2,3,1:T(8,128)S(1)}, u32[]{:S(2)}, u32[]{:S(2)}) collective-permute-start(f32[8,5,6,1,128]{4,0,2,3,1:T(8,128)S(1)} %get-tuple-element.107), channel_id=1, source_target_pairs={{0,1},{1,2},{2,3},{4,5},{5,6},{6,7},{8,9},{9,10},{10,11},{12,13},{... | collective-permute-start | bytes 368648 | tf_op jit(solution)/shard_map/ppermute | solution.py:24
  152.2 1.9 %collective-permute-start.17 = (f32[8,5,6,1,128]{4,0,2,1,3:T(8,128)S(1)}, f32[8,5,6,1,128]{4,0,2,1,3:T(8,128)S(1)}, u32[]{:S(2)}, u32[]{:S(2)}) collective-permute-start(f32[8,5,6,1,128]{4,0,2,1,3:T(8,128)S(1)} %get-tuple-element.108), channel_id=1, source_target_pairs={{1,0},{2,1},{3,2},{5,4},{6,5},{7,6},{9,8},{10,9},{11,10},{13,12},{... | collective-permute-start | bytes 368648 | tf_op jit(solution)/shard_map/ppermute | solution.py:25
  155.3 7.0 %collective-permute-done.17 = f32[8,5,6,1,128]{4,0,2,1,3:T(8,128)S(1)} collective-permute-done((f32[8,5,6,1,128]{4,0,2,1,3:T(8,128)S(1)}, f32[8,5,6,1,128]{4,0,2,1,3:T(8,128)S(1)}, u32[]{:S(2)}, u32[]{:S(2)}) %collective-permute-start.17) | collective-permute-done | bytes 122912 | tf_op jit(solution)/shard_map/ppermute | solution.py:25
  162.7 1.9 %collective-permute-start.19 = (f32[8,5,4,1,128]{4,0,2,3,1:T(8,128)S(1)}, f32[8,5,4,1,128]{4,0,2,3,1:T(8,128)S(1)}, u32[]{:S(2)}, u32[]{:S(2)}) collective-permute-start(f32[8,5,4,1,128]{4,0,2,3,1:T(8,128)S(1)} %get-tuple-element.177), channel_id=1, source_target_pairs={{1,0},{2,1},{3,2},{5,4},{6,5},{7,6},{9,8},{10,9},{11,10},{13,12},{... | collective-permute-start | bytes 245768 | tf_op jit(solution)/shard_map/ppermute | solution.py:25
  164.7 7.7 %collective-permute-done.19 = f32[8,5,4,1,128]{4,0,2,3,1:T(8,128)S(1)} collective-permute-done((f32[8,5,4,1,128]{4,0,2,3,1:T(8,128)S(1)}, f32[8,5,4,1,128]{4,0,2,3,1:T(8,128)S(1)}, u32[]{:S(2)}, u32[]{:S(2)}) %collective-permute-start.19) | collective-permute-done | bytes 81952 | tf_op jit(solution)/shard_map/ppermute | solution.py:25
  172.4 1.9 %collective-permute-start.18 = (f32[8,5,4,1,128]{4,0,2,3,1:T(8,128)S(1)}, f32[8,5,4,1,128]{4,0,2,3,1:T(8,128)S(1)}, u32[]{:S(2)}, u32[]{:S(2)}) collective-permute-start(f32[8,5,4,1,128]{4,0,2,3,1:T(8,128)S(1)} %get-tuple-element.172), channel_id=1, source_target_pairs={{0,1},{1,2},{2,3},{4,5},{5,6},{6,7},{8,9},{9,10},{10,11},{12,13},{... | collective-permute-start | bytes 245768 | tf_op jit(solution)/shard_map/ppermute | solution.py:24
  174.4 1.4 collective-permute-done.18
  176.4 0.9 copy.1526
  (346 shorter events, 44.4 us)
Async XLA Ops:
  0.0 18.2 %copy-start = (f32[8,5,4,4,128]{4,3,2,1,0:T(4,128)S(1)}, f32[8,5,4,4,128]{4,3,2,1,0:T(4,128)}, u32[]{:S(2)}) copy-start(f32[8,5,4,4,128]{4,3,2,1,0:T(4,128)} %param.37) | copy-start | bytes 983044
  1.0 14.6 %copy-start.1 = (f32[5,4,4,128]{3,2,1,0:T(4,128)S(1)}, f32[5,4,4,128]{3,2,1,0:T(4,128)}, u32[]{:S(2)}) copy-start(f32[5,4,4,128]{3,2,1,0:T(4,128)} %param.38) | copy-start | bytes 122884
  1.7 61.0 %collective-permute-start.1 = (f32[8,5,1,4,128]{4,0,3,1,2:T(8,128)}, f32[8,5,1,4,128]{4,0,3,1,2:T(8,128)}, u32[]{:S(2)}, u32[]{:S(2)}) collective-permute-start(f32[8,5,1,4,128]{4,0,3,1,2:T(8,128)} %copy.1569), channel_id=1, source_target_pairs={{4,0},{8,4},{12,8},{16,12},{20,16},{24,20},{28,24},{32,28},{36,32}... | collective-permute-start | bytes 245768 | tf_op jit(solution)/shard_map/ppermute | solution.py:25
  16.3 20.2 %collective-permute-start.4 = (f32[5,1,4,128]{3,2,1,0:T(4,128)}, f32[5,1,4,128]{3,2,1,0:T(4,128)}, u32[]{:S(2)}, u32[]{:S(2)}) collective-permute-start(f32[5,1,4,128]{3,2,1,0:T(4,128)} %slice.571), channel_id=1, source_target_pairs={{0,4},{4,8},{8,12},{12,16},{16,20},{20,24},{24,28},{28,32},{32,36}... | collective-permute-start | bytes 30728 | tf_op jit(solution)/shard_map/ppermute | solution.py:24
  18.2 5.4 %copy-start.46 = (f32[4,4,128]{2,1,0:T(4,128)}, f32[4,4,128]{2,1,0:T(4,128)S(1)}, u32[]{:S(2)}) copy-start(f32[4,4,128]{2,1,0:T(4,128)S(1)} %get-tuple-element.230) | copy-start | bytes 24580
  18.3 5.4 %copy-start.44 = (f32[4,4,128]{2,1,0:T(4,128)}, f32[4,4,128]{2,1,0:T(4,128)S(1)}, u32[]{:S(2)}) copy-start(f32[4,4,128]{2,1,0:T(4,128)S(1)} %get-tuple-element.227) | copy-start | bytes 24580
  18.3 5.4 %copy-start.26 = (f32[4,4,128]{2,1,0:T(4,128)}, f32[4,4,128]{2,1,0:T(4,128)S(1)}, u32[]{:S(2)}) copy-start(f32[4,4,128]{2,1,0:T(4,128)S(1)} %get-tuple-element.223) | copy-start | bytes 24580
  18.3 6.2 %copy-start.48 = (f32[4,4,128]{2,1,0:T(4,128)}, f32[4,4,128]{2,1,0:T(4,128)S(1)}, u32[]{:S(2)}) copy-start(f32[4,4,128]{2,1,0:T(4,128)S(1)} %get-tuple-element.228) | copy-start | bytes 24580
  22.0 5.6 %copy-start.52 = (f32[128]{0:T(128)}, f32[128]{0:T(128)S(1)}, u32[]{:S(2)}) copy-start(f32[128]{0:T(128)S(1)} %broadcast_in_dim.5) | copy-start | bytes 1540
  23.6 5.8 %copy-start.6 = (f32[4,4,128]{2,0,1:T(4,128)}, f32[4,4,128]{2,0,1:T(4,128)S(1)}, u32[]{:S(2)}) copy-start(f32[4,4,128]{2,0,1:T(4,128)S(1)} %copy.1253) | copy-start | bytes 24580
  23.7 5.7 %copy-start.16 = (f32[4,4,128]{2,0,1:T(4,128)}, f32[4,4,128]{2,0,1:T(4,128)S(1)}, u32[]{:S(2)}) copy-start(f32[4,4,128]{2,0,1:T(4,128)S(1)} %copy.1601) | copy-start | bytes 24580
  25.2 4.2 %copy-start.38 = (f32[4,4,128]{2,0,1:T(4,128)}, f32[4,4,128]{2,0,1:T(4,128)S(1)}, u32[]{:S(2)}) copy-start(f32[4,4,128]{2,0,1:T(4,128)S(1)} %copy.1080) | copy-start | bytes 24580
  37.2 9.0 %collective-permute-start.5 = (f32[5,1,4,128]{3,1,2,0:T(1,128)S(1)}, f32[5,1,4,128]{3,1,2,0:T(1,128)S(1)}, u32[]{:S(2)}, u32[]{:S(2)}) collective-permute-start(f32[5,1,4,128]{3,1,2,0:T(1,128)S(1)} %bitcast.2652), channel_id=1, source_target_pairs={{4,0},{8,4},{12,8},{16,12},{20,16},{24,20},{28,24},{32,28},{36,32}... | collective-permute-start | bytes 30728 | tf_op jit(solution)/shard_map/ppermute | solution.py:25
  46.9 8.8 %collective-permute-start.10 = (f32[5,6,1,128]{3,1,2,0:T(8,128)S(1)}, f32[5,6,1,128]{3,1,2,0:T(8,128)S(1)}, u32[]{:S(2)}, u32[]{:S(2)}) collective-permute-start(f32[5,6,1,128]{3,1,2,0:T(8,128)S(1)} %get-tuple-element.217), channel_id=1, source_target_pairs={{0,1},{1,2},{2,3},{4,5},{5,6},{6,7},{8,9},{9,10},{10,11},{12,13},{... | collective-permute-start | bytes 46088 | tf_op jit(solution)/shard_map/ppermute | solution.py:24
  53.6 9.0 %collective-permute-start.11 = (f32[5,6,1,128]{3,1,2,0:T(8,128)S(1)}, f32[5,6,1,128]{3,1,2,0:T(8,128)S(1)}, u32[]{:S(2)}, u32[]{:S(2)}) collective-permute-start(f32[5,6,1,128]{3,1,2,0:T(8,128)S(1)} %get-tuple-element.218), channel_id=1, source_target_pairs={{1,0},{2,1},{3,2},{5,4},{6,5},{7,6},{9,8},{10,9},{11,10},{13,12},{... | collective-permute-start | bytes 46088 | tf_op jit(solution)/shard_map/ppermute | solution.py:25
  63.7 10.5 %collective-permute-start = (f32[8,5,1,4,128]{4,0,3,1,2:T(8,128)S(1)}, f32[8,5,1,4,128]{4,0,3,1,2:T(8,128)S(1)}, u32[]{:S(2)}, u32[]{:S(2)}) collective-permute-start(f32[8,5,1,4,128]{4,0,3,1,2:T(8,128)S(1)} %get-tuple-element.197), channel_id=1, source_target_pairs={{0,4},{4,8},{8,12},{12,16},{16,20},{20,24},{24,28},{28,32},{32,36}... | collective-permute-start | bytes 245768 | tf_op jit(solution)/shard_map/ppermute | solution.py:24
  75.1 16.5 %collective-permute-start.2 = (f32[8,5,1,4,128]{4,0,3,1,2:T(8,128)S(1)}, f32[8,5,1,4,128]{4,0,3,1,2:T(8,128)S(1)}, u32[]{:S(2)}, u32[]{:S(2)}) collective-permute-start(f32[8,5,1,4,128]{4,0,3,1,2:T(8,128)S(1)} %get-tuple-element.184), channel_id=1, source_target_pairs={{0,4},{4,8},{8,12},{12,16},{16,20},{20,24},{24,28},{28,32},{32,36}... | collective-permute-start | bytes 245768 | tf_op jit(solution)/shard_map/ppermute | solution.py:24
  77.0 14.5 %collective-permute-start.3 = (f32[8,5,1,4,128]{4,0,3,1,2:T(8,128)S(1)}, f32[8,5,1,4,128]{4,0,3,1,2:T(8,128)S(1)}, u32[]{:S(2)}, u32[]{:S(2)}) collective-permute-start(f32[8,5,1,4,128]{4,0,3,1,2:T(8,128)S(1)} %get-tuple-element.186), channel_id=1, source_target_pairs={{4,0},{8,4},{12,8},{16,12},{20,16},{24,20},{28,24},{32,28},{36,32}... | collective-permute-start | bytes 245768 | tf_op jit(solution)/shard_map/ppermute | solution.py:25
  85.9 5.7 %collective-permute-start.6 = (f32[8,5,6,1,128]{4,0,2,3,1:T(8,128)S(1)}, f32[8,5,6,1,128]{4,0,2,3,1:T(8,128)S(1)}, u32[]{:S(2)}, u32[]{:S(2)}) collective-permute-start(f32[8,5,6,1,128]{4,0,2,3,1:T(8,128)S(1)} %get-tuple-element.109), channel_id=1, source_target_pairs={{0,1},{1,2},{2,3},{4,5},{5,6},{6,7},{8,9},{9,10},{10,11},{12,13},{... | collective-permute-start | bytes 368648 | tf_op jit(solution)/shard_map/ppermute | solution.py:24
  89.4 10.1 %collective-permute-start.7 = (f32[8,5,6,1,128]{4,0,2,3,1:T(8,128)S(1)}, f32[8,5,6,1,128]{4,0,2,3,1:T(8,128)S(1)}, u32[]{:S(2)}, u32[]{:S(2)}) collective-permute-start(f32[8,5,6,1,128]{4,0,2,3,1:T(8,128)S(1)} %get-tuple-element.110), channel_id=1, source_target_pairs={{1,0},{2,1},{3,2},{5,4},{6,5},{7,6},{9,8},{10,9},{11,10},{13,12},{... | collective-permute-start | bytes 368648 | tf_op jit(solution)/shard_map/ppermute | solution.py:25
  99.9 3.4 %collective-permute-start.8 = (f32[8,5,4,1,128]{4,0,2,3,1:T(8,128)S(1)}, f32[8,5,4,1,128]{4,0,2,3,1:T(8,128)S(1)}, u32[]{:S(2)}, u32[]{:S(2)}) collective-permute-start(f32[8,5,4,1,128]{4,0,2,3,1:T(8,128)S(1)} %slice_bitcast_fusion.18), channel_id=1, source_target_pairs={{0,1},{1,2},{2,3},{4,5},{5,6},{6,7},{8,9},{9,10},{10,11},{12,13},{... | collective-permute-start | bytes 245768 | tf_op jit(solution)/shard_map/ppermute | solution.py:24
  103.4 10.3 %collective-permute-start.9 = (f32[8,5,4,1,128]{4,0,2,1,3:T(8,128)S(1)}, f32[8,5,4,1,128]{4,0,2,1,3:T(8,128)S(1)}, u32[]{:S(2)}, u32[]{:S(2)}) collective-permute-start(f32[8,5,4,1,128]{4,0,2,1,3:T(8,128)S(1)} %get-tuple-element.193), channel_id=1, source_target_pairs={{1,0},{2,1},{3,2},{5,4},{6,5},{7,6},{9,8},{10,9},{11,10},{13,12},{... | collective-permute-start | bytes 245768 | tf_op jit(solution)/shard_map/ppermute | solution.py:25
  105.5 8.2 %copy-start.5 = (f32[8,5,4,1,1,128]{5,0,2,1,4,3:T(8,128)S(1)}, f32[8,5,4,1,1,128]{5,0,2,1,4,3:T(8,128)}, u32[]{:S(2)}) copy-start(f32[8,5,4,1,1,128]{5,0,2,1,4,3:T(8,128)} %get-tuple-element.189) | copy-start | bytes 245764
  119.8 18.9 %collective-permute-start.13 = (f32[8,5,1,4,128]{4,0,3,1,2:T(8,128)S(1)}, f32[8,5,1,4,128]{4,0,3,1,2:T(8,128)S(1)}, u32[]{:S(2)}, u32[]{:S(2)}) collective-permute-start(f32[8,5,1,4,128]{4,0,3,1,2:T(8,128)S(1)} %copy.1581), channel_id=1, source_target_pairs={{4,0},{8,4},{12,8},{16,12},{20,16},{24,20},{28,24},{32,28},{36,32}... | collective-permute-start | bytes 245768 | tf_op jit(solution)/shard_map/ppermute | solution.py:25
  121.7 3.4 %copy-start.25 = (f32[4,4,32]{2,1,0:T(4,128)S(1)}, f32[4,4,32]{2,1,0:T(4,128)}, u32[]{:S(2)}) copy-start(f32[4,4,32]{2,1,0:T(4,128)} %copy-done.24) | copy-start | bytes 6148
  121.8 17.0 %collective-permute-start.12 = (f32[8,5,1,4,128]{4,0,3,1,2:T(8,128)S(1)}, f32[8,5,1,4,128]{4,0,3,1,2:T(8,128)S(1)}, u32[]{:S(2)}, u32[]{:S(2)}) collective-permute-start(f32[8,5,1,4,128]{4,0,3,1,2:T(8,128)S(1)} %copy.1584), channel_id=1, source_target_pairs={{0,4},{4,8},{8,12},{12,16},{16,20},{20,24},{24,28},{28,32},{32,36}... | collective-permute-start | bytes 245768 | tf_op jit(solution)/shard_map/ppermute | solution.py:24
  139.1 15.2 %collective-permute-start.14 = (f32[8,5,1,4,128]{4,0,3,1,2:T(8,128)S(1)}, f32[8,5,1,4,128]{4,0,3,1,2:T(8,128)S(1)}, u32[]{:S(2)}, u32[]{:S(2)}) collective-permute-start(f32[8,5,1,4,128]{4,0,3,1,2:T(8,128)S(1)} %get-tuple-element.143), channel_id=1, source_target_pairs={{0,4},{4,8},{8,12},{12,16},{16,20},{20,24},{24,28},{28,32},{32,36}... | collective-permute-start | bytes 245768 | tf_op jit(solution)/shard_map/ppermute | solution.py:24
  141.0 13.3 %collective-permute-start.15 = (f32[8,5,1,4,128]{4,0,3,1,2:T(8,128)S(1)}, f32[8,5,1,4,128]{4,0,3,1,2:T(8,128)S(1)}, u32[]{:S(2)}, u32[]{:S(2)}) collective-permute-start(f32[8,5,1,4,128]{4,0,3,1,2:T(8,128)S(1)} %get-tuple-element.144), channel_id=1, source_target_pairs={{4,0},{8,4},{12,8},{16,12},{20,16},{24,20},{28,24},{32,28},{36,32}... | collective-permute-start | bytes 245768 | tf_op jit(solution)/shard_map/ppermute | solution.py:25
  149.2 6.0 %collective-permute-start.16 = (f32[8,5,6,1,128]{4,0,2,3,1:T(8,128)S(1)}, f32[8,5,6,1,128]{4,0,2,3,1:T(8,128)S(1)}, u32[]{:S(2)}, u32[]{:S(2)}) collective-permute-start(f32[8,5,6,1,128]{4,0,2,3,1:T(8,128)S(1)} %get-tuple-element.107), channel_id=1, source_target_pairs={{0,1},{1,2},{2,3},{4,5},{5,6},{6,7},{8,9},{9,10},{10,11},{12,13},{... | collective-permute-start | bytes 368648 | tf_op jit(solution)/shard_map/ppermute | solution.py:24
  152.2 10.1 %collective-permute-start.17 = (f32[8,5,6,1,128]{4,0,2,1,3:T(8,128)S(1)}, f32[8,5,6,1,128]{4,0,2,1,3:T(8,128)S(1)}, u32[]{:S(2)}, u32[]{:S(2)}) collective-permute-start(f32[8,5,6,1,128]{4,0,2,1,3:T(8,128)S(1)} %get-tuple-element.108), channel_id=1, source_target_pairs={{1,0},{2,1},{3,2},{5,4},{6,5},{7,6},{9,8},{10,9},{11,10},{13,12},{... | collective-permute-start | bytes 368648 | tf_op jit(solution)/shard_map/ppermute | solution.py:25
  162.7 9.7 %collective-permute-start.19 = (f32[8,5,4,1,128]{4,0,2,3,1:T(8,128)S(1)}, f32[8,5,4,1,128]{4,0,2,3,1:T(8,128)S(1)}, u32[]{:S(2)}, u32[]{:S(2)}) collective-permute-start(f32[8,5,4,1,128]{4,0,2,3,1:T(8,128)S(1)} %get-tuple-element.177), channel_id=1, source_target_pairs={{1,0},{2,1},{3,2},{5,4},{6,5},{7,6},{9,8},{10,9},{11,10},{13,12},{... | collective-permute-start | bytes 245768 | tf_op jit(solution)/shard_map/ppermute | solution.py:25
  172.4 3.4 %collective-permute-start.18 = (f32[8,5,4,1,128]{4,0,2,3,1:T(8,128)S(1)}, f32[8,5,4,1,128]{4,0,2,3,1:T(8,128)S(1)}, u32[]{:S(2)}, u32[]{:S(2)}) collective-permute-start(f32[8,5,4,1,128]{4,0,2,3,1:T(8,128)S(1)} %get-tuple-element.172), channel_id=1, source_target_pairs={{0,1},{1,2},{2,3},{4,5},{5,6},{6,7},{8,9},{9,10},{10,11},{12,13},{... | collective-permute-start | bytes 245768 | tf_op jit(solution)/shard_map/ppermute | solution.py:24
  (47 other events, 33.3 us)
where the time goes:
time: 180 us; the launch traced here: 177 us
  starting transfers between devices  78.2 us (43%)
  waiting for transfers between devices  50.5 us (28%)
  local copies, waits for them, and re-layouts  23.4 us (13%)
  matrix products  14 us (8%)
  other arithmetic  9.25 us (5%)
  between operations  2.08 us (1%)
    ppermute x10, starting transfers between devices, extended(): after = lax.ppermute(first, axis, down)  50.2 us
    ppermute x10, waiting for transfers between devices, extended(): after = lax.ppermute(first, axis, down)  38.4 us
    ppermute x10, starting transfers between devices, extended(): before = lax.ppermute(last, axis, up)  28 us
    unnamed x145, local copies, waits for them, and re-layouts  19.2 us
    dot_general x33, matrix products, lane_product(): jnp.einsum('...i,ij->...j', grouped, table, precision=lax.Precision.HIGHEST)  14 us
    ppermute x10, waiting for transfers between devices, extended(): before = lax.ppermute(last, axis, up)  12.1 us
  transfers between devices with their start and end apart: 20, of which 10 were waited for; matrix products, arithmetic and copies ran while one was open for 11% of the time, Pallas kernels for 0%

commit v1 on v0

v1 whole, which is shorter than its diff:
```python
import math

import jax
import jax.numpy as jnp
import numpy as np
from jax import lax
from jax.experimental import pallas as pl
from jax.experimental.pallas import tpu as pltpu
from jax.sharding import PartitionSpec as P

STEP = 0.1
COLS = 8
LANES = 128
V1, V2, V3, W1, W2, W3, KE, HH, SX, SY, SZ, NU = range(12)
FACE = 160
FACE_NAMES = (V1, V2, V3, KE, HH, NU)
COEF_ROWS = 32


def node_tables():
    inner_point = math.sqrt(0.2)
    points = [-1.0, -inner_point, inner_point, 1.0]
    weights = [1.0 / 6.0, 5.0 / 6.0, 5.0 / 6.0, 1.0 / 6.0]
    barycentric = []
    for j in range(4):
        product = 1.0
        for k in range(4):
            if k != j:
                product = product * (points[j] - points[k])
        barycentric.append(1.0 / product)
    deriv = [[0.0] * 4 for i in range(4)]
    for i in range(4):
        for j in range(4):
            if j != i:
                deriv[i][j] = barycentric[j] / barycentric[i] / (points[i] - points[j])
        deriv[i][i] = -sum((deriv[i][j] for j in range(4) if j != i))
    norms = [2.0, 2.0 / 3.0, 2.0 / 5.0, 2.0 / 3.0]
    legendre = [
        lambda x: 1.0,
        lambda x: x,
        lambda x: 0.5 * (3.0 * x * x - 1.0),
        lambda x: 0.5 * (5.0 * x * x * x - 3.0 * x),
    ]
    modal = [[weights[i] * legendre[k](points[i]) / norms[k] for i in range(4)] for k in range(4)]
    return deriv, modal


DERIV, MODAL = node_tables()


def span_table():
    m = np.zeros((LANES, LANES), np.float64)
    for e in range(LANES // 4):
        for i in range(4):
            for j in range(4):
                if i != j:
                    m[4 * e + j, 4 * e + i] = DERIV[i][j]
        m[4 * e, 4 * e] = DERIV[0][0] + 3.0
        m[4 * e + 3, 4 * e + 3] = DERIV[3][3] - 3.0
        m[(4 * e + 4) % LANES, 4 * e + 3] += 3.0
        m[(4 * e - 1) % LANES, 4 * e] -= 3.0
    m = m.astype(np.float32)
    hi = m.astype(jnp.bfloat16)
    lo = (m - hi.astype(np.float32)).astype(jnp.bfloat16)
    zero = np.zeros_like(lo)
    return np.block([[hi, lo], [hi, zero]])


def row(f, x, y):
    return (f * 16 + x * 4 + y) * COLS


def face_row(f, n):
    return (f * 4 + n) * COLS


def tan_in(ref, f, x, y):
    return ref[pl.ds(f * 16 + x * 4 + y, COLS, stride=80), :]


def coef(ref, name, x, y):
    r = name * 16 + x * 4 + y
    return ref[r : r + 1, :]


def group_transform(f, matrix, axis, index, step):
    size = f.shape[axis]
    total = None
    for offset in range(-3, 4):
        c = jnp.zeros_like(f)
        for i in range(4):
            if 0 <= i + offset < 4:
                c = jnp.where(index == i, matrix[i][i + offset], c)
        moved = f if offset == 0 else pltpu.roll(f, (-offset * step) % size, axis)
        term = c * moved
        total = term if total is None else total + term
    return total


def base_coefs(base_ref, flags_ref, coef_ref):
    u = [base_ref[f * 16 : (f + 1) * 16, :] for f in range(5)]
    inv = 1.0 / u[0]
    v = [u[1 + d] * inv for d in range(3)]
    ke = 0.5 * (v[0] * v[0] + v[1] * v[1] + v[2] * v[2])
    pressure = 0.4 * (u[4] - ke * u[0])
    sound = jnp.sqrt(1.4 * pressure * inv)
    speed = [jnp.abs(v[d]) + sound for d in range(3)]
    lane = lax.broadcasted_iota(jnp.int32, (16, LANES), 1)
    sub = lax.broadcasted_iota(jnp.int32, (16, LANES), 0)
    zi, yi, xi = lane % 4, sub % 4, sub // 4
    near = jnp.where(
        zi == 3, pltpu.roll(speed[2], LANES - 1, 1), pltpu.roll(speed[2], 1, 1)
    )
    sz = jnp.where((zi == 0) | (zi == 3), 3.0 * jnp.maximum(speed[2], near), 0.0)
    modal = group_transform(u[0], MODAL, 1, zi, 1)
    modal = group_transform(modal, MODAL, 0, yi, 1)
    modal = group_transform(modal, MODAL, 0, xi, 4)
    squares = modal * modal
    edge = jnp.where((zi == 3) | (yi == 3) | (xi == 3), squares, 0.0)
    ones = [[1.0] * 4] * 4
    sums = []
    for s in (squares, edge):
        s = jnp.broadcast_to(jnp.sum(s, axis=0, keepdims=True), (8, LANES))
        sums.append(group_transform(s, ones, 1, zi[:8], 1))
    sensor = jnp.log(sums[1] / sums[0] + 1e-10) * (1.0 / math.log(10.0))
    shape = 1.0 / (1.0 + jnp.exp(-(sensor + 2.3) * 2.0))
    spread = jnp.where(
        lax.broadcasted_iota(jnp.int32, (32, LANES), 1) // 4
        == lax.broadcasted_iota(jnp.int32, (32, LANES), 0),
        1.0,
        0.0,
    )
    flags = jnp.broadcast_to(flags_ref[...].astype(jnp.float32), (8, 32))
    flags = jnp.dot(flags, spread, preferred_element_type=jnp.float32)
    nu = 0.1 * flags * shape
    nu = jnp.concatenate([nu, nu], axis=0)
    table = {
        V1: v[0], V2: v[1], V3: v[2],
        W1: 0.4 * v[0], W2: 0.4 * v[1], W3: 0.4 * v[2],
        KE: 0.4 * ke, HH: (u[4] + pressure) * inv,
        SX: speed[0], SY: speed[1], SZ: sz, NU: nu,
    }
    for name, value in table.items():
        coef_ref[name * 16 : (name + 1) * 16, :] = value


def pack_faces(load, outs, odd_x, odd_y):
    for axis, (near, far), odd in ((0, outs[:2], odd_x), (1, outs[2:], odd_y)):
        for f in range(5):
            for n in range(4):
                line = [load(f, k, n) if axis == 0 else load(f, n, k) for k in range(4)]
                lower = line[0] * DERIV[0][0]
                upper = line[3] * DERIV[3][3]
                for k in range(1, 4):
                    lower = lower + DERIV[0][k] * line[k]
                    upper = upper + DERIV[3][3 - k] * line[3 - k]
                r = face_row(f, n)
                near[r : r + 8, :] = jnp.where(odd, line[0], line[3])
                far[r : r + 8, :] = jnp.where(odd, line[3], line[0])
                near[FACE + r : FACE + r + 8, :] = jnp.where(odd, lower, upper)
                far[FACE + r : FACE + r + 8, :] = jnp.where(odd, upper, lower)


def pack_kernel(t_ref, base_ref, flags_ref, coef_ref, xn, xf, yn, yf):
    odd_x = lax.axis_index("gx") % 2 == 1
    odd_y = lax.axis_index("gy") % 2 == 1
    base_coefs(base_ref, flags_ref, coef_ref)
    pack_faces(lambda f, x, y: tan_in(t_ref, f, x, y), (xn, xf, yn, yf), odd_x, odd_y)
    for axis, (near, far), odd in ((0, (xn, xf), odd_x), (1, (yn, yf), odd_y)):
        for place, name in enumerate(FACE_NAMES + (SX + axis,)):
            first = name * 16
            if axis == 0:
                lower = coef_ref[first : first + 4, :]
                upper = coef_ref[first + 12 : first + 16, :]
            else:
                lower = coef_ref[pl.ds(first, 4, stride=4), :]
                upper = coef_ref[pl.ds(first + 3, 4, stride=4), :]
            r = 2 * FACE + 4 * place
            near[r : r + 4, :] = jnp.where(odd, lower, upper)
            far[r : r + 4, :] = jnp.where(odd, upper, lower)
        r = 2 * FACE + 28
        near[r : r + 4, :] = jnp.zeros((4, LANES), jnp.float32)
        far[r : r + 4, :] = jnp.zeros((4, LANES), jnp.float32)


def flux(d, t, v, dp, e, hh):
    u = t[1 + d] - v[d] * t[0]
    out = [t[1 + d]]
    for i in range(3):
        value = v[d] * t[1 + i] + v[i] * u
        out.append(value + dp if i == d else value)
    out.append(v[d] * e + hh * u)
    return out


def section(load, coef_ref, recv, coef_recv, odd_x, odd_y, wm_ref, acc, ops, aux, finish):
    nodes = [(x, y) for x in range(4) for y in range(4)]
    zi = lax.broadcasted_iota(jnp.int32, (COLS, LANES), 1) % 4
    top_lane = zi == 3

    def split(r, value):
        hi = value.astype(jnp.bfloat16)
        lo = (value - hi.astype(jnp.float32)).astype(jnp.bfloat16)
        return hi, lo

    def put(f, x, y, pair):
        r = row(f, x, y)
        ops[r : r + 16, :LANES] = pair[0]
        ops[r : r + 16, LANES:] = pair[1]

    for x in range(4):
        for f in range(5):
            for y in (0, 2):
                value = jnp.concatenate([load(f, x, y), load(f, x, y + 1)], axis=0)
                put(f, x, y, split(0, value))
    chunk = 128
    for c in range(640 // chunk):
        both = jnp.dot(
            ops[c * chunk : (c + 1) * chunk, :], wm_ref[...], preferred_element_type=jnp.float32
        )
        acc[c * chunk : (c + 1) * chunk, :] = both[:, :LANES] + both[:, LANES:]

    for x in range(4):
        for y in (0, 2):
            parts = []
            for yy in (y, y + 1):
                t = [load(f, x, yy) for f in range(5)]
                v = [coef(coef_ref, V1 + d, x, yy) for d in range(3)]
                w = [coef(coef_ref, W1 + d, x, yy) for d in range(3)]
                dp = 0.4 * t[4] + coef(coef_ref, KE, x, yy) * t[0]
                for d in range(3):
                    dp = dp - w[d] * t[1 + d]
                e = t[4] + dp
                k = (x * 4 + yy) * 16
                aux[k : k + 8, :] = dp
                aux[k + 8 : k + 16, :] = e
                g = flux(2, t, v, dp, e, coef(coef_ref, HH, x, yy))
                nu = coef(coef_ref, NU, x, yy)
                out = []
                for f in range(5):
                    r = row(f, x, yy)
                    out.append(nu * acc[r : r + 8, :] - g[f])
                parts.append(out)
            for f in range(5):
                value = jnp.concatenate([parts[0][f], parts[1][f]], axis=0)
                put(f, x, y, split(0, value))
    for c in range(640 // chunk):
        both = jnp.dot(
            ops[c * chunk : (c + 1) * chunk, :], wm_ref[...], preferred_element_type=jnp.float32
        )
        acc[c * chunk : (c + 1) * chunk, :] = both[:, :LANES] + both[:, LANES:]

    for axis, odd in ((0, odd_x), (1, odd_y)):
        near, far = recv[2 * axis : 2 * axis + 2]
        (near_c, near_at), (far_c, far_at) = coef_recv[2 * axis : 2 * axis + 2]

        def pick(low, r, rows=8):
            a, b = near[r : r + rows, :], far[r : r + rows, :]
            return jnp.where(odd, a, b) if low else jnp.where(odd, b, a)

        def pick_coef(low, place, n):
            r = 4 * place + n
            a = near_c[near_at + r : near_at + r + 1, :]
            b = far_c[far_at + r : far_at + r + 1, :]
            return jnp.where(odd, a, b) if low else jnp.where(odd, b, a)

        for n in range(4):
            line = [(k, n) if axis == 0 else (n, k) for k in range(4)]
            t = [[load(f, x, y) for f in range(5)] for x, y in line]
            g = []
            for k, (x, y) in enumerate(line):
                v = [coef(coef_ref, V1 + d, x, y) for d in range(3)]
                r = (x * 4 + y) * 16
                g.append(
                    flux(axis, t[k], v, aux[r : r + 8, :], aux[r + 8 : r + 16, :],
                         coef(coef_ref, HH, x, y))
                )
            nu = coef(coef_ref, NU, *line[0])
            sides = []
            for low in (True, False):
                mine = t[0] if low else t[3]
                far_t = [pick(low, face_row(f, n)) for f in range(5)]
                v = [pick_coef(low, d, n) for d in range(3)]
                dp = 0.4 * far_t[4] + pick_coef(low, 3, n) * far_t[0]
                for d in range(3):
                    dp = dp - (0.4 * v[d]) * far_t[1 + d]
                far_g = flux(axis, far_t, v, dp, far_t[4] + dp, pick_coef(low, 4, n))
                far_nu = pick_coef(low, 5, n)
                own_s = coef(coef_ref, SX + axis, *(line[0] if low else line[3]))
                s3 = 3.0 * jnp.maximum(own_s, pick_coef(low, 6, n))
                far_f, jump, mean = [], [], []
                for f in range(5):
                    step3 = 3.0 * (far_t[f] - mine[f])
                    far_d = pick(low, FACE + face_row(f, n))
                    far_q = far_d - step3 if low else far_d + step3
                    value = 3.0 * (far_nu * far_q - far_g[f])
                    far_f.append(-value if low else value)
                    jump.append(s3 * (far_t[f] - mine[f]))
                    mean.append(3.0 * far_t[f])
                sides.append((far_f, jump, mean))
            for f in range(5):
                tt = [t[k][f] for k in range(4)]
                fl = []
                for i in range(4):
                    q = None
                    for k in range(4):
                        if k != i:
                            term = DERIV[i][k] * tt[k]
                            q = term if q is None else q + term
                    if i == 0:
                        q = q - sides[0][2][f]
                    if i == 3:
                        q = q + sides[1][2][f]
                    fl.append(nu * q - g[i][f])
                for i, (x, y) in enumerate(line):
                    total = None
                    for k in range(4):
                        if k != i:
                            term = DERIV[i][k] * fl[k]
                            total = term if total is None else total + term
                    if i == 0:
                        total = total + (sides[0][0][f] + sides[0][1][f])
                    if i == 3:
                        total = total + (sides[1][0][f] + sides[1][1][f])
                    r = row(f, x, y)
                    total = total + acc[r : r + 8, :]
                    if axis == 0:
                        tz = tt[i]
                        other = jnp.where(
                            top_lane, pltpu.roll(tz, LANES - 1, 1), pltpu.roll(tz, 1, 1)
                        )
                        total = total + coef(coef_ref, SZ, x, y) * (other - tz)
                        acc[r : r + 8, :] = total
                    else:
                        finish(f, x, y, tt[i], total)


def first_kernel(
    t_ref, coef_ref, wm_ref, rxn, rxf, ryn, ryf, s_ref, xn, xf, yn, yf, acc, ops, aux
):
    odd_x = lax.axis_index("gx") % 2 == 1
    odd_y = lax.axis_index("gy") % 2 == 1

    def finish(f, x, y, t, total):
        r = row(f, x, y)
        s_ref[r : r + 8, :] = t + STEP * total

    faces = (rxn, rxf, ryn, ryf)
    section(
        lambda f, x, y: tan_in(t_ref, f, x, y), coef_ref, faces,
        [(ref, 2 * FACE) for ref in faces], odd_x, odd_y, wm_ref, acc, ops, aux, finish,
    )

    def load(f, x, y):
        r = row(f, x, y)
        return s_ref[r : r + 8, :]

    pack_faces(load, (xn, xf, yn, yf), odd_x, odd_y)


def second_kernel(
    t_ref, s_ref, coef_ref, wm_ref, cxn, cxf, cyn, cyf, rxn, rxf, ryn, ryf, out_ref, acc, ops, aux
):
    odd_x = lax.axis_index("gx") % 2 == 1
    odd_y = lax.axis_index("gy") % 2 == 1

    def load(f, x, y):
        r = row(f, x, y)
        return s_ref[r : r + 8, :]

    def finish(f, x, y, s, total):
        value = 0.5 * tan_in(t_ref, f, x, y) + (0.5 * s + (0.5 * STEP) * total)
        out_ref[pl.ds(f * 16 + x * 4 + y, COLS, stride=80), :] = value

    section(
        load, coef_ref, (rxn, rxf, ryn, ryf),
        [(ref, 2 * FACE) for ref in (cxn, cxf, cyn, cyf)],
        odd_x, odd_y, wm_ref, acc, ops, aux, finish,
    )


def call(kernel, shapes, scratch, args, cost):
    vmem = pl.BlockSpec(memory_space=pltpu.VMEM)
    return pl.pallas_call(
        kernel,
        out_shape=[jax.ShapeDtypeStruct(s, jnp.float32) for s in shapes],
        in_specs=[vmem] * len(args),
        out_specs=[vmem] * len(shapes),
        scratch_shapes=scratch,
        compiler_params=pltpu.CompilerParams(vmem_limit_bytes=32 * 1024 * 1024),
        cost_estimate=pl.CostEstimate(flops=cost, bytes_accessed=1000000, transcendentals=0),
    )(*args)


def exchange(messages):
    size_x, size_y = lax.axis_size("gx"), lax.axis_size("gy")

    def pairs(size, first):
        out = []
        for i in range(first, size - 1, 2):
            out += [(i, i + 1), (i + 1, i)]
        if first == 1:
            out += [(0, 0)]
            if size % 2 == 0:
                out += [(size - 1, size - 1)]
        return out

    xn, xf, yn, yf = messages
    got_xn = lax.ppermute(xn, "gx", pairs(size_x, 0))
    got_yn = lax.ppermute(yn, "gy", pairs(size_y, 0))
    got_xf = lax.ppermute(xf, "gx", pairs(size_x, 1))
    got_yf = lax.ppermute(yf, "gy", pairs(size_y, 1))
    return got_xn, got_xf, got_yn, got_yf


def per_device(tangent, base_state, shock_flags):
    t = tangent.reshape(640, LANES)
    base = base_state.reshape(80, LANES)
    flags = shock_flags.reshape(1, 32)
    wm = jnp.asarray(span_table())
    message = (2 * FACE + COEF_ROWS, LANES)
    short = (2 * FACE, LANES)
    scratch = [
        pltpu.VMEM((640, LANES), jnp.float32),
        pltpu.VMEM((640, 2 * LANES), jnp.bfloat16),
        pltpu.VMEM((256, LANES), jnp.float32),
    ]
    coefs, *faces = call(
        pack_kernel, [(192, LANES)] + [message] * 4, [], [t, base, flags], 1000000
    )
    got = exchange(faces)
    s, *faces = call(
        first_kernel, [(640, LANES)] + [short] * 4, scratch, [t, coefs, wm, *got], 10000000
    )
    again = exchange(faces)
    (out,) = call(
        second_kernel, [(640, LANES)], scratch, [t, s, coefs, wm, *got, *again], 10000000
    )
    return out.reshape(tangent.shape)


def solution(mesh):
    in_specs = (P(None, None, "gx", "gy", None), P(None, "gx", "gy", None), P("gx", "gy", None))
    out_specs = P(None, None, "gx", "gy", None)
    return jax.shard_map(
        per_device, mesh=mesh, in_specs=in_specs, out_specs=out_specs, check_vma=False
    )
```

time: 180 us -> 54.7 us (0.30)
  the two profiles are of different devices: /device:TPU:7 before, /device:TPU:23 now
where the time goes in v1:
time: 54.7 us; the launch traced here: 54.3 us
  starting transfers between devices  37.9 us (69%)
  waiting for transfers between devices  10.4 us (19%)
  Pallas kernels  3.44 us (6%)
  local copies, waits for them, and re-layouts  2.41 us (4%)
    ppermute x2, starting transfers between devices, exchange(): got_yf = lax.ppermute(yf, 'gy', pairs(size_y, 1))  12.7 us
    ppermute x2, starting transfers between devices, exchange(): got_xf = lax.ppermute(xf, 'gx', pairs(size_x, 1))  10.4 us
    ppermute x2, waiting for transfers between devices, exchange(): got_yf = lax.ppermute(yf, 'gy', pairs(size_y, 1))  10.4 us
    ppermute x2, starting transfers between devices, exchange(): got_xn = lax.ppermute(xn, 'gx', pairs(size_x, 0))  10.1 us
    ppermute x2, starting transfers between devices, exchange(): got_yn = lax.ppermute(yn, 'gy', pairs(size_y, 0))  4.78 us
    pallas_call x3, Pallas kernels, call(): pl.pallas_call(kernel, out_shape=[jax.ShapeDtypeStruct(s, jnp.float32) fo...  3.44 us
    unnamed x8, local copies, waits for them, and re-layouts  2.41 us
  transfers between devices with their start and end apart: 8, of which 2 were waited for; matrix products, arithmetic and copies ran while one was open for 0% of the time, Pallas kernels for 0%

profile of v1, /device:TPU:23, one launch (start us, length us, event | category | flops | bytes accessed | tf_op | source)
XLA Modules:
  0.0 54.3 jit_solution(5246640366211617768)
XLA Ops:
  0.0 0.0 copy-start.3
  0.0 0.7 %copy-done.3 = s32[1,1,32]{2,1,0:T(1,128)S(1)} copy-done((s32[1,1,32]{2,1,0:T(1,128)S(1)}, s32[1,1,32]{2,1,0:T(1,128)}, u32[]{:S(2)}) %copy-start.3) | copy-done | bytes 152
  0.7 0.0 copy-start
  0.7 1.0 %copy-done = f32[8,5,4,4,128]{4,3,2,1,0:T(4,128)S(1)} copy-done((f32[8,5,4,4,128]{4,3,2,1,0:T(4,128)S(1)}, f32[8,5,4,4,128]{4,3,2,1,0:T(4,128)}, u32[]{:S(2)}) %copy-start) | copy-done | bytes 327704
  1.6 0.0 copy-start.2
  1.6 0.8 %copy-done.2 = f32[5,4,4,128]{3,2,1,0:T(4,128)S(1)} copy-done((f32[5,4,4,128]{3,2,1,0:T(4,128)S(1)}, f32[5,4,4,128]{3,2,1,0:T(4,128)}, u32[]{:S(2)}) %copy-start.2) | copy-done | bytes 40984
  2.4 0.0 copy-start.1
  2.4 0.3 shard_map.46
  2.8 3.2 %collective-permute-start = (f32[352,128]{1,0:T(8,128)S(1)}, f32[352,128]{1,0:T(8,128)S(1)}, u32[]{:S(2)}, u32[]{:S(2)}) collective-permute-start(f32[352,128]{1,0:T(8,128)S(1)} %get-tuple-element.16), channel_id=1, source_target_pairs={{0,4},{4,0},{8,12},{12,8},{16,20},{20,16},{24,28},{28,24},{32,36},... | collective-permute-start | bytes 540680 | tf_op jit(solution)/shard_map/ppermute | solution.py:409
  6.0 1.9 %collective-permute-start.1 = (f32[352,128]{1,0:T(8,128)S(1)}, f32[352,128]{1,0:T(8,128)S(1)}, u32[]{:S(2)}, u32[]{:S(2)}) collective-permute-start(f32[352,128]{1,0:T(8,128)S(1)} %get-tuple-element.17), channel_id=1, source_target_pairs={{4,8},{8,4},{12,16},{16,12},{20,24},{24,20},{28,32},{32,28},{36,40... | collective-permute-start | bytes 540680 | tf_op jit(solution)/shard_map/ppermute | solution.py:411
  7.9 2.9 %collective-permute-start.2 = (f32[352,128]{1,0:T(8,128)S(1)}, f32[352,128]{1,0:T(8,128)S(1)}, u32[]{:S(2)}, u32[]{:S(2)}) collective-permute-start(f32[352,128]{1,0:T(8,128)S(1)} %get-tuple-element.18), channel_id=1, source_target_pairs={{0,1},{1,0},{2,3},{3,2},{4,5},{5,4},{6,7},{7,6},{8,9},{9,8},{10,11... | collective-permute-start | bytes 540680 | tf_op jit(solution)/shard_map/ppermute | solution.py:410
  10.8 6.7 %collective-permute-start.3 = (f32[352,128]{1,0:T(8,128)S(1)}, f32[352,128]{1,0:T(8,128)S(1)}, u32[]{:S(2)}, u32[]{:S(2)}) collective-permute-start(f32[352,128]{1,0:T(8,128)S(1)} %get-tuple-element.19), channel_id=1, source_target_pairs={{1,2},{2,1},{0,0},{3,3},{5,6},{6,5},{4,4},{7,7},{9,10},{10,9},{8,8... | collective-permute-start | bytes 540680 | tf_op jit(solution)/shard_map/ppermute | solution.py:412
  17.4 0.0 collective-permute-done.rxn.cxn
  17.4 0.0 collective-permute-done.1.rxf.cxf
  17.5 0.0 collective-permute-done.2.ryn.cyn
  17.5 4.1 %collective-permute-done.3.ryf.cyf = f32[352,128]{1,0:T(8,128)S(1)} collective-permute-done((f32[352,128]{1,0:T(8,128)S(1)}, f32[352,128]{1,0:T(8,128)S(1)}, u32[]{:S(2)}, u32[]{:S(2)}) %collective-permute-start.3) | collective-permute-done | bytes 180256 | tf_op jit(solution)/shard_map/ppermute | solution.py:412
  21.6 0.0 copy-done.1
  21.6 1.3 %shard_map.47 = (f32[640,128]{1,0:T(8,128)S(1)}, f32[320,128]{1,0:T(8,128)S(1)}, f32[320,128]{1,0:T(8,128)S(1)}, f32[320,128]{1,0:T(8,128)S(1)}, f32[320,128]{1,0:T(8,128)S(1)}) custom-call(f32[640,128]{1,0:T(8,128)S(1)} %bitcast.5, f32[192,128]{1,0:T(8,128)S(1)} %get-tuple-element.15.coef_ref, bf16[256,256]{1,0:T(8,128)(2,1)S(1)} %copy-done.1, ...), custom_call_target="tpu_custom_call" | custom-call | flops 10000000 | bytes 1000000 | tf_op jit(solution)/shard_map/pallas_call | solution.py:384
  22.9 6.9 %collective-permute-start.4 = (f32[320,128]{1,0:T(8,128)S(1)}, f32[320,128]{1,0:T(8,128)S(1)}, u32[]{:S(2)}, u32[]{:S(2)}) collective-permute-start(f32[320,128]{1,0:T(8,128)S(1)} %get-tuple-element.21), channel_id=1, source_target_pairs={{0,4},{4,0},{8,12},{12,8},{16,20},{20,16},{24,28},{28,24},{32,36},... | collective-permute-start | bytes 491528 | tf_op jit(solution)/shard_map/ppermute | solution.py:409
  29.8 8.5 %collective-permute-start.5 = (f32[320,128]{1,0:T(8,128)S(1)}, f32[320,128]{1,0:T(8,128)S(1)}, u32[]{:S(2)}, u32[]{:S(2)}) collective-permute-start(f32[320,128]{1,0:T(8,128)S(1)} %get-tuple-element.22), channel_id=1, source_target_pairs={{4,8},{8,4},{12,16},{16,12},{20,24},{24,20},{28,32},{32,28},{36,40... | collective-permute-start | bytes 491528 | tf_op jit(solution)/shard_map/ppermute | solution.py:411
  38.2 1.9 %collective-permute-start.6 = (f32[320,128]{1,0:T(8,128)S(1)}, f32[320,128]{1,0:T(8,128)S(1)}, u32[]{:S(2)}, u32[]{:S(2)}) collective-permute-start(f32[320,128]{1,0:T(8,128)S(1)} %get-tuple-element.23), channel_id=1, source_target_pairs={{0,1},{1,0},{2,3},{3,2},{4,5},{5,4},{6,7},{7,6},{8,9},{9,8},{10,11... | collective-permute-start | bytes 491528 | tf_op jit(solution)/shard_map/ppermute | solution.py:410
  40.2 6.0 %collective-permute-start.7 = (f32[320,128]{1,0:T(8,128)S(1)}, f32[320,128]{1,0:T(8,128)S(1)}, u32[]{:S(2)}, u32[]{:S(2)}) collective-permute-start(f32[320,128]{1,0:T(8,128)S(1)} %get-tuple-element.24), channel_id=1, source_target_pairs={{1,2},{2,1},{0,0},{3,3},{5,6},{6,5},{4,4},{7,7},{9,10},{10,9},{8,8... | collective-permute-start | bytes 491528 | tf_op jit(solution)/shard_map/ppermute | solution.py:412
  46.2 0.0 collective-permute-done.4.rxn
  46.2 0.0 collective-permute-done.5.rxf
  46.2 0.0 collective-permute-done.6.ryn
  46.2 6.3 %collective-permute-done.7.ryf = f32[320,128]{1,0:T(8,128)S(1)} collective-permute-done((f32[320,128]{1,0:T(8,128)S(1)}, f32[320,128]{1,0:T(8,128)S(1)}, u32[]{:S(2)}, u32[]{:S(2)}) %collective-permute-start.7) | collective-permute-done | bytes 163872 | tf_op jit(solution)/shard_map/ppermute | solution.py:412
  52.5 1.8 %shard_map.48 = f32[640,128]{1,0:T(8,128)} custom-call(f32[640,128]{1,0:T(8,128)S(1)} %bitcast.6, f32[640,128]{1,0:T(8,128)S(1)} %get-tuple-element.20.s_ref, f32[192,128]{1,0:T(8,128)S(1)} %get-tuple-element.15.coef_ref, bf16[256,256]{1,0:T(8,128)(2,1)S(1)} %copy-done.1, f32[352,128]{1,0:T(8,128)S(1)} %collective-permute-done.rxn.cxn, ...), custom_call_target="tpu_custom_call" | custom-call | flops 10000000 | bytes 1000000 | tf_op jit(solution)/shard_map/pallas_call | solution.py:384
Async XLA Ops:
  0.0 0.7 %copy-start.3 = (s32[1,1,32]{2,1,0:T(1,128)S(1)}, s32[1,1,32]{2,1,0:T(1,128)}, u32[]{:S(2)}) copy-start(s32[1,1,32]{2,1,0:T(1,128)} %param.6) | copy-start | bytes 388
  0.7 1.0 %copy-start = (f32[8,5,4,4,128]{4,3,2,1,0:T(4,128)S(1)}, f32[8,5,4,4,128]{4,3,2,1,0:T(4,128)}, u32[]{:S(2)}) copy-start(f32[8,5,4,4,128]{4,3,2,1,0:T(4,128)} %param.4) | copy-start | bytes 983044
  1.6 0.8 %copy-start.2 = (f32[5,4,4,128]{3,2,1,0:T(4,128)S(1)}, f32[5,4,4,128]{3,2,1,0:T(4,128)}, u32[]{:S(2)}) copy-start(f32[5,4,4,128]{3,2,1,0:T(4,128)} %param.5) | copy-start | bytes 122884
  2.4 19.2 %copy-start.1 = (bf16[256,256]{1,0:T(8,128)(2,1)S(1)}, bf16[256,256]{1,0:T(8,128)(2,1)}, u32[]{:S(2)}) copy-start(bf16[256,256]{1,0:T(8,128)(2,1)} %constant.2.clone.wm_ref) | copy-start | bytes 393220
  2.8 14.7 %collective-permute-start = (f32[352,128]{1,0:T(8,128)S(1)}, f32[352,128]{1,0:T(8,128)S(1)}, u32[]{:S(2)}, u32[]{:S(2)}) collective-permute-start(f32[352,128]{1,0:T(8,128)S(1)} %get-tuple-element.16), channel_id=1, source_target_pairs={{0,4},{4,0},{8,12},{12,8},{16,20},{20,16},{24,28},{28,24},{32,36},... | collective-permute-start | bytes 540680 | tf_op jit(solution)/shard_map/ppermute | solution.py:409
  6.0 11.5 %collective-permute-start.1 = (f32[352,128]{1,0:T(8,128)S(1)}, f32[352,128]{1,0:T(8,128)S(1)}, u32[]{:S(2)}, u32[]{:S(2)}) collective-permute-start(f32[352,128]{1,0:T(8,128)S(1)} %get-tuple-element.17), channel_id=1, source_target_pairs={{4,8},{8,4},{12,16},{16,12},{20,24},{24,20},{28,32},{32,28},{36,40... | collective-permute-start | bytes 540680 | tf_op jit(solution)/shard_map/ppermute | solution.py:411
  7.9 9.6 %collective-permute-start.2 = (f32[352,128]{1,0:T(8,128)S(1)}, f32[352,128]{1,0:T(8,128)S(1)}, u32[]{:S(2)}, u32[]{:S(2)}) collective-permute-start(f32[352,128]{1,0:T(8,128)S(1)} %get-tuple-element.18), channel_id=1, source_target_pairs={{0,1},{1,0},{2,3},{3,2},{4,5},{5,4},{6,7},{7,6},{8,9},{9,8},{10,11... | collective-permute-start | bytes 540680 | tf_op jit(solution)/shard_map/ppermute | solution.py:410
  10.8 10.8 %collective-permute-start.3 = (f32[352,128]{1,0:T(8,128)S(1)}, f32[352,128]{1,0:T(8,128)S(1)}, u32[]{:S(2)}, u32[]{:S(2)}) collective-permute-start(f32[352,128]{1,0:T(8,128)S(1)} %get-tuple-element.19), channel_id=1, source_target_pairs={{1,2},{2,1},{0,0},{3,3},{5,6},{6,5},{4,4},{7,7},{9,10},{10,9},{8,8... | collective-permute-start | bytes 540680 | tf_op jit(solution)/shard_map/ppermute | solution.py:412
  22.9 23.3 %collective-permute-start.4 = (f32[320,128]{1,0:T(8,128)S(1)}, f32[320,128]{1,0:T(8,128)S(1)}, u32[]{:S(2)}, u32[]{:S(2)}) collective-permute-start(f32[320,128]{1,0:T(8,128)S(1)} %get-tuple-element.21), channel_id=1, source_target_pairs={{0,4},{4,0},{8,12},{12,8},{16,20},{20,16},{24,28},{28,24},{32,36},... | collective-permute-start | bytes 491528 | tf_op jit(solution)/shard_map/ppermute | solution.py:409
  29.8 16.4 %collective-permute-start.5 = (f32[320,128]{1,0:T(8,128)S(1)}, f32[320,128]{1,0:T(8,128)S(1)}, u32[]{:S(2)}, u32[]{:S(2)}) collective-permute-start(f32[320,128]{1,0:T(8,128)S(1)} %get-tuple-element.22), channel_id=1, source_target_pairs={{4,8},{8,4},{12,16},{16,12},{20,24},{24,20},{28,32},{32,28},{36,40... | collective-permute-start | bytes 491528 | tf_op jit(solution)/shard_map/ppermute | solution.py:411
  38.2 8.0 %collective-permute-start.6 = (f32[320,128]{1,0:T(8,128)S(1)}, f32[320,128]{1,0:T(8,128)S(1)}, u32[]{:S(2)}, u32[]{:S(2)}) collective-permute-start(f32[320,128]{1,0:T(8,128)S(1)} %get-tuple-element.23), channel_id=1, source_target_pairs={{0,1},{1,0},{2,3},{3,2},{4,5},{5,4},{6,7},{7,6},{8,9},{9,8},{10,11... | collective-permute-start | bytes 491528 | tf_op jit(solution)/shard_map/ppermute | solution.py:410
  40.2 12.3 %collective-permute-start.7 = (f32[320,128]{1,0:T(8,128)S(1)}, f32[320,128]{1,0:T(8,128)S(1)}, u32[]{:S(2)}, u32[]{:S(2)}) collective-permute-start(f32[320,128]{1,0:T(8,128)S(1)} %get-tuple-element.24), channel_id=1, source_target_pairs={{1,2},{2,1},{0,0},{3,3},{5,6},{6,5},{4,4},{7,7},{9,10},{10,9},{8,8... | collective-permute-start | bytes 491528 | tf_op jit(solution)/shard_map/ppermute | solution.py:412

commit v2 on v1

--- a/solution.py
+++ b/solution.py
@@ -15,6 +15,7 @@
 FACE = 160
 FACE_NAMES = (V1, V2, V3, KE, HH, NU)
 COEF_ROWS = 32
+ORDER = (1, 3, 0, 2)
 
 
 def node_tables():
@@ -161,7 +162,12 @@
                 far[FACE + r : FACE + r + 8, :] = jnp.where(odd, upper, lower)
 
 
-def pack_kernel(t_ref, base_ref, flags_ref, coef_ref, xn, xf, yn, yf):
+def by_face(refs):
+    return tuple(refs[ORDER.index(face)] for face in range(4))
+
+
+def pack_kernel(t_ref, base_ref, flags_ref, coef_ref, *sent):
+    xn, xf, yn, yf = by_face(sent)
     odd_x = lax.axis_index("gx") % 2 == 1
     odd_y = lax.axis_index("gy") % 2 == 1
     base_coefs(base_ref, flags_ref, coef_ref)
@@ -335,46 +341,44 @@
                         finish(f, x, y, tt[i], total)
 
 
-def first_kernel(
-    t_ref, coef_ref, wm_ref, rxn, rxf, ryn, ryf, s_ref, xn, xf, yn, yf, acc, ops, aux
+def first_kernel(t_ref, coef_ref, wm_ref, r0, r1, r2, r3, s_ref, m0, m1, m2, m3, acc, ops, aux):
+    odd_x = lax.axis_index("gx") % 2 == 1
+    odd_y = lax.axis_index("gy") % 2 == 1
+
+    def finish(f, x, y, t, total):
+        r = row(f, x, y)
+        s_ref[r : r + 8, :] = t + STEP * total
+
+    faces = by_face((r0, r1, r2, r3))
+    section(
+        lambda f, x, y: tan_in(t_ref, f, x, y), coef_ref, faces,
+        [(ref, 2 * FACE) for ref in faces], odd_x, odd_y, wm_ref, acc, ops, aux, finish,
+    )
+
+    def load(f, x, y):
+        r = row(f, x, y)
+        return s_ref[r : r + 8, :]
+
+    pack_faces(load, by_face((m0, m1, m2, m3)), odd_x, odd_y)
+
+
+def second_kernel(
+    t_ref, s_ref, coef_ref, wm_ref, c0, c1, c2, c3, r0, r1, r2, r3, out_ref, acc, ops, aux
 ):
     odd_x = lax.axis_index("gx") % 2 == 1
     odd_y = lax.axis_index("gy") % 2 == 1
 
-    def finish(f, x, y, t, total):
-        r = row(f, x, y)
-        s_ref[r : r + 8, :] = t + STEP * total
-
-    faces = (rxn, rxf, ryn, ryf)
-    section(
-        lambda f, x, y: tan_in(t_ref, f, x, y), coef_ref, faces,
-        [(ref, 2 * FACE) for ref in faces], odd_x, odd_y, wm_ref, acc, ops, aux, finish,
-    )
-
     def load(f, x, y):
         r = row(f, x, y)
         return s_ref[r : r + 8, :]
 
-    pack_faces(load, (xn, xf, yn, yf), odd_x, odd_y)
-
-
-def second_kernel(
-    t_ref, s_ref, coef_ref, wm_ref, cxn, cxf, cyn, cyf, rxn, rxf, ryn, ryf, out_ref, acc, ops, aux
-):
-    odd_x = lax.axis_index("gx") % 2 == 1
-    odd_y = lax.axis_index("gy") % 2 == 1
-
-    def load(f, x, y):
-        r = row(f, x, y)
-        return s_ref[r : r + 8, :]
-
     def finish(f, x, y, s, total):
         value = 0.5 * tan_in(t_ref, f, x, y) + (0.5 * s + (0.5 * STEP) * total)
         out_ref[pl.ds(f * 16 + x * 4 + y, COLS, stride=80), :] = value
 
     section(
-        load, coef_ref, (rxn, rxf, ryn, ryf),
-        [(ref, 2 * FACE) for ref in (cxn, cxf, cyn, cyf)],
+        load, coef_ref, by_face((r0, r1, r2, r3)),
+        [(ref, 2 * FACE) for ref in by_face((c0, c1, c2, c3))],
         odd_x, odd_y, wm_ref, acc, ops, aux, finish,
     )
 
@@ -405,12 +409,13 @@
                 out += [(size - 1, size - 1)]
         return out
 
-    xn, xf, yn, yf = messages
-    got_xn = lax.ppermute(xn, "gx", pairs(size_x, 0))
-    got_yn = lax.ppermute(yn, "gy", pairs(size_y, 0))
-    got_xf = lax.ppermute(xf, "gx", pairs(size_x, 1))
-    got_yf = lax.ppermute(yf, "gy", pairs(size_y, 1))
-    return got_xn, got_xf, got_yn, got_yf
+    plan = (
+        ("gx", pairs(size_x, 0)),
+        ("gx", pairs(size_x, 1)),
+        ("gy", pairs(size_y, 0)),
+        ("gy", pairs(size_y, 1)),
+    )
+    return [lax.ppermute(m, *plan[face]) for m, face in zip(messages, ORDER)]
 
 
 def per_device(tangent, base_state, shock_flags):

time: 54.7 us -> 50.1 us (0.916)
  the two profiles are of different devices: /device:TPU:23 before, /device:TPU:7 now
where the time goes in v2:
time: 50.1 us; the launch traced here: 49.7 us
  starting transfers between devices  38.2 us (76%)
  waiting for transfers between devices  5.49 us (11%)
  Pallas kernels  3.44 us (7%)
  local copies, waits for them, and re-layouts  2.41 us (5%)
    ppermute x8, starting transfers between devices, exchange(): return [lax.ppermute(m, *plan[face]) for m, face in zip(messages, ORDER)]  38.2 us
    ppermute x8, waiting for transfers between devices, exchange(): return [lax.ppermute(m, *plan[face]) for m, face in zip(messages, ORDER)]  5.49 us
    pallas_call x3, Pallas kernels, call(): pl.pallas_call(kernel, out_shape=[jax.ShapeDtypeStruct(s, jnp.float32) fo...  3.44 us
    unnamed x8, local copies, waits for them, and re-layouts  2.41 us
  transfers between devices with their start and end apart: 8, of which 2 were waited for; matrix products, arithmetic and copies ran while one was open for 0% of the time, Pallas kernels for 0%

profile of v2, /device:TPU:7, one launch (start us, length us, event | category | flops | bytes accessed | tf_op | source)
XLA Modules:
  0.0 49.7 jit_solution(10264697447480584596)
XLA Ops:
  0.0 0.0 copy-start.3
  0.0 0.7 %copy-done.3 = s32[1,1,32]{2,1,0:T(1,128)S(1)} copy-done((s32[1,1,32]{2,1,0:T(1,128)S(1)}, s32[1,1,32]{2,1,0:T(1,128)}, u32[]{:S(2)}) %copy-start.3) | copy-done | bytes 152
  0.7 0.0 copy-start
  0.7 1.0 %copy-done = f32[8,5,4,4,128]{4,3,2,1,0:T(4,128)S(1)} copy-done((f32[8,5,4,4,128]{4,3,2,1,0:T(4,128)S(1)}, f32[8,5,4,4,128]{4,3,2,1,0:T(4,128)}, u32[]{:S(2)}) %copy-start) | copy-done | bytes 327704
  1.6 0.0 copy-start.2
  1.6 0.8 %copy-done.2 = f32[5,4,4,128]{3,2,1,0:T(4,128)S(1)} copy-done((f32[5,4,4,128]{3,2,1,0:T(4,128)S(1)}, f32[5,4,4,128]{3,2,1,0:T(4,128)}, u32[]{:S(2)}) %copy-start.2) | copy-done | bytes 40984
  2.4 0.0 copy-start.1
  2.4 0.3 shard_map.46
  2.8 14.0 %collective-permute-start = (f32[352,128]{1,0:T(8,128)S(1)}, f32[352,128]{1,0:T(8,128)S(1)}, u32[]{:S(2)}, u32[]{:S(2)}) collective-permute-start(f32[352,128]{1,0:T(8,128)S(1)} %get-tuple-element.16), channel_id=1, source_target_pairs={{4,8},{8,4},{12,16},{16,12},{20,24},{24,20},{28,32},{32,28},{36,40... | collective-permute-start | bytes 540680 | tf_op jit(solution)/shard_map/ppermute | solution.py:418
  16.7 5.6 %collective-permute-start.1 = (f32[352,128]{1,0:T(8,128)S(1)}, f32[352,128]{1,0:T(8,128)S(1)}, u32[]{:S(2)}, u32[]{:S(2)}) collective-permute-start(f32[352,128]{1,0:T(8,128)S(1)} %get-tuple-element.17), channel_id=1, source_target_pairs={{1,2},{2,1},{0,0},{3,3},{5,6},{6,5},{4,4},{7,7},{9,10},{10,9},{8,8... | collective-permute-start | bytes 540680 | tf_op jit(solution)/shard_map/ppermute | solution.py:418
  22.3 1.9 %collective-permute-start.2 = (f32[352,128]{1,0:T(8,128)S(1)}, f32[352,128]{1,0:T(8,128)S(1)}, u32[]{:S(2)}, u32[]{:S(2)}) collective-permute-start(f32[352,128]{1,0:T(8,128)S(1)} %get-tuple-element.18), channel_id=1, source_target_pairs={{0,4},{4,0},{8,12},{12,8},{16,20},{20,16},{24,28},{28,24},{32,36},... | collective-permute-start | bytes 540680 | tf_op jit(solution)/shard_map/ppermute | solution.py:418
  24.3 1.9 %collective-permute-start.3 = (f32[352,128]{1,0:T(8,128)S(1)}, f32[352,128]{1,0:T(8,128)S(1)}, u32[]{:S(2)}, u32[]{:S(2)}) collective-permute-start(f32[352,128]{1,0:T(8,128)S(1)} %get-tuple-element.19), channel_id=1, source_target_pairs={{0,1},{1,0},{2,3},{3,2},{4,5},{5,4},{6,7},{7,6},{8,9},{9,8},{10,11... | collective-permute-start | bytes 540680 | tf_op jit(solution)/shard_map/ppermute | solution.py:418
  26.2 0.0 collective-permute-done.r0.c0
  26.2 2.9 %collective-permute-done.1.r1.c1 = f32[352,128]{1,0:T(8,128)S(1)} collective-permute-done((f32[352,128]{1,0:T(8,128)S(1)}, f32[352,128]{1,0:T(8,128)S(1)}, u32[]{:S(2)}, u32[]{:S(2)}) %collective-permute-start.1) | collective-permute-done | bytes 180256 | tf_op jit(solution)/shard_map/ppermute | solution.py:418
  29.1 0.0 collective-permute-done.2.r2.c2
  29.1 0.0 collective-permute-done.3.r3.c3
  29.1 0.0 copy-done.1
  29.1 1.3 %shard_map.47 = (f32[640,128]{1,0:T(8,128)S(1)}, f32[320,128]{1,0:T(8,128)S(1)}, f32[320,128]{1,0:T(8,128)S(1)}, f32[320,128]{1,0:T(8,128)S(1)}, f32[320,128]{1,0:T(8,128)S(1)}) custom-call(f32[640,128]{1,0:T(8,128)S(1)} %bitcast.5, f32[192,128]{1,0:T(8,128)S(1)} %get-tuple-element.15.coef_ref, bf16[256,256]{1,0:T(8,128)(2,1)S(1)} %copy-done.1, ...), custom_call_target="tpu_custom_call" | custom-call | flops 10000000 | bytes 1000000 | tf_op jit(solution)/shard_map/pallas_call | solution.py:388
  30.4 5.4 %collective-permute-start.4 = (f32[320,128]{1,0:T(8,128)S(1)}, f32[320,128]{1,0:T(8,128)S(1)}, u32[]{:S(2)}, u32[]{:S(2)}) collective-permute-start(f32[320,128]{1,0:T(8,128)S(1)} %get-tuple-element.21), channel_id=1, source_target_pairs={{4,8},{8,4},{12,16},{16,12},{20,24},{24,20},{28,32},{32,28},{36,40... | collective-permute-start | bytes 491528 | tf_op jit(solution)/shard_map/ppermute | solution.py:418
  35.8 5.6 %collective-permute-start.5 = (f32[320,128]{1,0:T(8,128)S(1)}, f32[320,128]{1,0:T(8,128)S(1)}, u32[]{:S(2)}, u32[]{:S(2)}) collective-permute-start(f32[320,128]{1,0:T(8,128)S(1)} %get-tuple-element.22), channel_id=1, source_target_pairs={{1,2},{2,1},{0,0},{3,3},{5,6},{6,5},{4,4},{7,7},{9,10},{10,9},{8,8... | collective-permute-start | bytes 491528 | tf_op jit(solution)/shard_map/ppermute | solution.py:418
  41.4 1.9 %collective-permute-start.6 = (f32[320,128]{1,0:T(8,128)S(1)}, f32[320,128]{1,0:T(8,128)S(1)}, u32[]{:S(2)}, u32[]{:S(2)}) collective-permute-start(f32[320,128]{1,0:T(8,128)S(1)} %get-tuple-element.23), channel_id=1, source_target_pairs={{0,4},{4,0},{8,12},{12,8},{16,20},{20,16},{24,28},{28,24},{32,36},... | collective-permute-start | bytes 491528 | tf_op jit(solution)/shard_map/ppermute | solution.py:418
  43.3 1.9 %collective-permute-start.7 = (f32[320,128]{1,0:T(8,128)S(1)}, f32[320,128]{1,0:T(8,128)S(1)}, u32[]{:S(2)}, u32[]{:S(2)}) collective-permute-start(f32[320,128]{1,0:T(8,128)S(1)} %get-tuple-element.24), channel_id=1, source_target_pairs={{0,1},{1,0},{2,3},{3,2},{4,5},{5,4},{6,7},{7,6},{8,9},{9,8},{10,11... | collective-permute-start | bytes 491528 | tf_op jit(solution)/shard_map/ppermute | solution.py:418
  45.3 0.0 collective-permute-done.4.r0
  45.3 2.6 %collective-permute-done.5.r1 = f32[320,128]{1,0:T(8,128)S(1)} collective-permute-done((f32[320,128]{1,0:T(8,128)S(1)}, f32[320,128]{1,0:T(8,128)S(1)}, u32[]{:S(2)}, u32[]{:S(2)}) %collective-permute-start.5) | collective-permute-done | bytes 163872 | tf_op jit(solution)/shard_map/ppermute | solution.py:418
  47.9 0.0 collective-permute-done.6.r2
  47.9 0.0 collective-permute-done.7.r3
  47.9 1.8 %shard_map.48 = f32[640,128]{1,0:T(8,128)} custom-call(f32[640,128]{1,0:T(8,128)S(1)} %bitcast.6, f32[640,128]{1,0:T(8,128)S(1)} %get-tuple-element.20.s_ref, f32[192,128]{1,0:T(8,128)S(1)} %get-tuple-element.15.coef_ref, bf16[256,256]{1,0:T(8,128)(2,1)S(1)} %copy-done.1, f32[352,128]{1,0:T(8,128)S(1)} %collective-permute-done.r0.c0, ...), custom_call_target="tpu_custom_call" | custom-call | flops 10000000 | bytes 1000000 | tf_op jit(solution)/shard_map/pallas_call | solution.py:388
Async XLA Ops:
  0.0 0.7 %copy-start.3 = (s32[1,1,32]{2,1,0:T(1,128)S(1)}, s32[1,1,32]{2,1,0:T(1,128)}, u32[]{:S(2)}) copy-start(s32[1,1,32]{2,1,0:T(1,128)} %param.6) | copy-start | bytes 388
  0.7 1.0 %copy-start = (f32[8,5,4,4,128]{4,3,2,1,0:T(4,128)S(1)}, f32[8,5,4,4,128]{4,3,2,1,0:T(4,128)}, u32[]{:S(2)}) copy-start(f32[8,5,4,4,128]{4,3,2,1,0:T(4,128)} %param.4) | copy-start | bytes 983044
  1.6 0.8 %copy-start.2 = (f32[5,4,4,128]{3,2,1,0:T(4,128)S(1)}, f32[5,4,4,128]{3,2,1,0:T(4,128)}, u32[]{:S(2)}) copy-start(f32[5,4,4,128]{3,2,1,0:T(4,128)} %param.5) | copy-start | bytes 122884
  2.4 26.7 %copy-start.1 = (bf16[256,256]{1,0:T(8,128)(2,1)S(1)}, bf16[256,256]{1,0:T(8,128)(2,1)}, u32[]{:S(2)}) copy-start(bf16[256,256]{1,0:T(8,128)(2,1)} %constant.2.clone.wm_ref) | copy-start | bytes 393220
  2.8 23.4 %collective-permute-start = (f32[352,128]{1,0:T(8,128)S(1)}, f32[352,128]{1,0:T(8,128)S(1)}, u32[]{:S(2)}, u32[]{:S(2)}) collective-permute-start(f32[352,128]{1,0:T(8,128)S(1)} %get-tuple-element.16), channel_id=1, source_target_pairs={{4,8},{8,4},{12,16},{16,12},{20,24},{24,20},{28,32},{32,28},{36,40... | collective-permute-start | bytes 540680 | tf_op jit(solution)/shard_map/ppermute | solution.py:418
  16.7 12.4 %collective-permute-start.1 = (f32[352,128]{1,0:T(8,128)S(1)}, f32[352,128]{1,0:T(8,128)S(1)}, u32[]{:S(2)}, u32[]{:S(2)}) collective-permute-start(f32[352,128]{1,0:T(8,128)S(1)} %get-tuple-element.17), channel_id=1, source_target_pairs={{1,2},{2,1},{0,0},{3,3},{5,6},{6,5},{4,4},{7,7},{9,10},{10,9},{8,8... | collective-permute-start | bytes 540680 | tf_op jit(solution)/shard_map/ppermute | solution.py:418
  22.3 6.8 %collective-permute-start.2 = (f32[352,128]{1,0:T(8,128)S(1)}, f32[352,128]{1,0:T(8,128)S(1)}, u32[]{:S(2)}, u32[]{:S(2)}) collective-permute-start(f32[352,128]{1,0:T(8,128)S(1)} %get-tuple-element.18), channel_id=1, source_target_pairs={{0,4},{4,0},{8,12},{12,8},{16,20},{20,16},{24,28},{28,24},{32,36},... | collective-permute-start | bytes 540680 | tf_op jit(solution)/shard_map/ppermute | solution.py:418
  24.3 4.9 %collective-permute-start.3 = (f32[352,128]{1,0:T(8,128)S(1)}, f32[352,128]{1,0:T(8,128)S(1)}, u32[]{:S(2)}, u32[]{:S(2)}) collective-permute-start(f32[352,128]{1,0:T(8,128)S(1)} %get-tuple-element.19), channel_id=1, source_target_pairs={{0,1},{1,0},{2,3},{3,2},{4,5},{5,4},{6,7},{7,6},{8,9},{9,8},{10,11... | collective-permute-start | bytes 540680 | tf_op jit(solution)/shard_map/ppermute | solution.py:418
  30.4 14.9 %collective-permute-start.4 = (f32[320,128]{1,0:T(8,128)S(1)}, f32[320,128]{1,0:T(8,128)S(1)}, u32[]{:S(2)}, u32[]{:S(2)}) collective-permute-start(f32[320,128]{1,0:T(8,128)S(1)} %get-tuple-element.21), channel_id=1, source_target_pairs={{4,8},{8,4},{12,16},{16,12},{20,24},{24,20},{28,32},{32,28},{36,40... | collective-permute-start | bytes 491528 | tf_op jit(solution)/shard_map/ppermute | solution.py:418
  35.8 12.1 %collective-permute-start.5 = (f32[320,128]{1,0:T(8,128)S(1)}, f32[320,128]{1,0:T(8,128)S(1)}, u32[]{:S(2)}, u32[]{:S(2)}) collective-permute-start(f32[320,128]{1,0:T(8,128)S(1)} %get-tuple-element.22), channel_id=1, source_target_pairs={{1,2},{2,1},{0,0},{3,3},{5,6},{6,5},{4,4},{7,7},{9,10},{10,9},{8,8... | collective-permute-start | bytes 491528 | tf_op jit(solution)/shard_map/ppermute | solution.py:418
  41.4 6.4 %collective-permute-start.6 = (f32[320,128]{1,0:T(8,128)S(1)}, f32[320,128]{1,0:T(8,128)S(1)}, u32[]{:S(2)}, u32[]{:S(2)}) collective-permute-start(f32[320,128]{1,0:T(8,128)S(1)} %get-tuple-element.23), channel_id=1, source_target_pairs={{0,4},{4,0},{8,12},{12,8},{16,20},{20,16},{24,28},{28,24},{32,36},... | collective-permute-start | bytes 491528 | tf_op jit(solution)/shard_map/ppermute | solution.py:418
  43.3 4.5 %collective-permute-start.7 = (f32[320,128]{1,0:T(8,128)S(1)}, f32[320,128]{1,0:T(8,128)S(1)}, u32[]{:S(2)}, u32[]{:S(2)}) collective-permute-start(f32[320,128]{1,0:T(8,128)S(1)} %get-tuple-element.24), channel_id=1, source_target_pairs={{0,1},{1,0},{2,3},{3,2},{4,5},{5,4},{6,7},{7,6},{8,9},{9,8},{10,11... | collective-permute-start | bytes 491528 | tf_op jit(solution)/shard_map/ppermute | solution.py:418

commit v3 on v2

--- a/solution.py
+++ b/solution.py
@@ -15,7 +15,8 @@
 FACE = 160
 FACE_NAMES = (V1, V2, V3, KE, HH, NU)
 COEF_ROWS = 32
-ORDER = (1, 3, 0, 2)
+ORDER_1 = (0, 1, 3, 2)
+ORDER_2 = (1, 3, 0, 2)
 
 
 def node_tables():
@@ -49,22 +50,23 @@
 DERIV, MODAL = node_tables()
 
 
-def span_table():
-    m = np.zeros((LANES, LANES), np.float64)
-    for e in range(LANES // 4):
-        for i in range(4):
-            for j in range(4):
-                if i != j:
-                    m[4 * e + j, 4 * e + i] = DERIV[i][j]
-        m[4 * e, 4 * e] = DERIV[0][0] + 3.0
-        m[4 * e + 3, 4 * e + 3] = DERIV[3][3] - 3.0
-        m[(4 * e + 4) % LANES, 4 * e + 3] += 3.0
-        m[(4 * e - 1) % LANES, 4 * e] -= 3.0
-    m = m.astype(np.float32)
-    hi = m.astype(jnp.bfloat16)
-    lo = (m - hi.astype(np.float32)).astype(jnp.bfloat16)
-    zero = np.zeros_like(lo)
-    return np.block([[hi, lo], [hi, zero]])
+def span_table(wm_ref):
+    k = lax.broadcasted_iota(jnp.int32, (LANES, LANES), 0)
+    n = lax.broadcasted_iota(jnp.int32, (LANES, LANES), 1)
+    place = (n % 4) * LANES + ((k - n) & (LANES - 1))
+    hi = jnp.zeros((LANES, LANES), jnp.float32)
+    lo = hi
+    entries = [(i, j - i, DERIV[i][j]) for i in range(4) for j in range(4) if i != j]
+    for i, offset, value in entries + [(0, -1, -3.0), (3, 1, 3.0)]:
+        head = float(np.float32(value).astype(jnp.bfloat16))
+        here = place == i * LANES + (offset & (LANES - 1))
+        hi = jnp.where(here, head, hi)
+        lo = jnp.where(here, value - head, lo)
+    hi, lo = hi.astype(jnp.bfloat16), lo.astype(jnp.bfloat16)
+    wm_ref[:LANES, :LANES] = hi
+    wm_ref[LANES:, :LANES] = hi
+    wm_ref[:LANES, LANES:] = lo
+    wm_ref[LANES:, LANES:] = jnp.zeros_like(lo)
 
 
 def row(f, x, y):
@@ -162,15 +164,27 @@
                 far[FACE + r : FACE + r + 8, :] = jnp.where(odd, upper, lower)
 
 
-def by_face(refs):
-    return tuple(refs[ORDER.index(face)] for face in range(4))
-
-
-def pack_kernel(t_ref, base_ref, flags_ref, coef_ref, *sent):
-    xn, xf, yn, yf = by_face(sent)
+def by_face(refs, order):
+    return tuple(refs[order.index(face)] for face in range(4))
+
+
+def pack_kernel(t_hbm, base_hbm, flags_hbm, coef_ref, *refs):
+    xn, xf, yn, yf = by_face(refs[:4], ORDER_1)
+    t_ref, base_ref, flags_ref, sems = refs[4:]
+    copies = [
+        pltpu.make_async_copy(src, dst, sems.at[k])
+        for k, (src, dst) in enumerate(
+            ((base_hbm, base_ref), (flags_hbm, flags_ref), (t_hbm, t_ref))
+        )
+    ]
+    for copy in copies:
+        copy.start()
     odd_x = lax.axis_index("gx") % 2 == 1
     odd_y = lax.axis_index("gy") % 2 == 1
+    copies[0].wait()
+    copies[1].wait()
     base_coefs(base_ref, flags_ref, coef_ref)
+    copies[2].wait()
     pack_faces(lambda f, x, y: tan_in(t_ref, f, x, y), (xn, xf, yn, yf), odd_x, odd_y)
     for axis, (near, far), odd in ((0, (xn, xf), odd_x), (1, (yn, yf), odd_y)):
         for place, name in enumerate(FACE_NAMES + (SX + axis,)):
@@ -199,32 +213,30 @@
     return out
 
 
-def section(load, coef_ref, recv, coef_recv, odd_x, odd_y, wm_ref, acc, ops, aux, finish):
-    nodes = [(x, y) for x in range(4) for y in range(4)]
-    zi = lax.broadcasted_iota(jnp.int32, (COLS, LANES), 1) % 4
-    top_lane = zi == 3
-
-    def split(r, value):
+def volume(load, coef_ref, wm_ref, acc, ops, aux):
+    top_lane = lax.broadcasted_iota(jnp.int32, (COLS, LANES), 1) % 4 == 3
+    chunk = 128
+
+    def put(f, x, y, value):
         hi = value.astype(jnp.bfloat16)
-        lo = (value - hi.astype(jnp.float32)).astype(jnp.bfloat16)
-        return hi, lo
-
-    def put(f, x, y, pair):
         r = row(f, x, y)
-        ops[r : r + 16, :LANES] = pair[0]
-        ops[r : r + 16, LANES:] = pair[1]
+        ops[r : r + 16, :LANES] = hi
+        ops[r : r + 16, LANES:] = (value - hi.astype(jnp.float32)).astype(jnp.bfloat16)
+
+    def span_product():
+        for c in range(640 // chunk):
+            both = jnp.dot(
+                ops[c * chunk : (c + 1) * chunk, :],
+                wm_ref[...],
+                preferred_element_type=jnp.float32,
+            )
+            acc[c * chunk : (c + 1) * chunk, :] = both[:, :LANES] + both[:, LANES:]
 
     for x in range(4):
         for f in range(5):
             for y in (0, 2):
-                value = jnp.concatenate([load(f, x, y), load(f, x, y + 1)], axis=0)
-                put(f, x, y, split(0, value))
-    chunk = 128
-    for c in range(640 // chunk):
-        both = jnp.dot(
-            ops[c * chunk : (c + 1) * chunk, :], wm_ref[...], preferred_element_type=jnp.float32
-        )
-        acc[c * chunk : (c + 1) * chunk, :] = both[:, :LANES] + both[:, LANES:]
+                put(f, x, y, jnp.concatenate([load(f, x, y), load(f, x, y + 1)], axis=0))
+    span_product()
 
     for x in range(4):
         for y in (0, 2):
@@ -248,28 +260,10 @@
                     out.append(nu * acc[r : r + 8, :] - g[f])
                 parts.append(out)
             for f in range(5):
-                value = jnp.concatenate([parts[0][f], parts[1][f]], axis=0)
-                put(f, x, y, split(0, value))
-    for c in range(640 // chunk):
-        both = jnp.dot(
-            ops[c * chunk : (c + 1) * chunk, :], wm_ref[...], preferred_element_type=jnp.float32
-        )
-        acc[c * chunk : (c + 1) * chunk, :] = both[:, :LANES] + both[:, LANES:]
-
-    for axis, odd in ((0, odd_x), (1, odd_y)):
-        near, far = recv[2 * axis : 2 * axis + 2]
-        (near_c, near_at), (far_c, far_at) = coef_recv[2 * axis : 2 * axis + 2]
-
-        def pick(low, r, rows=8):
-            a, b = near[r : r + rows, :], far[r : r + rows, :]
-            return jnp.where(odd, a, b) if low else jnp.where(odd, b, a)
-
-        def pick_coef(low, place, n):
-            r = 4 * place + n
-            a = near_c[near_at + r : near_at + r + 1, :]
-            b = far_c[far_at + r : far_at + r + 1, :]
-            return jnp.where(odd, a, b) if low else jnp.where(odd, b, a)
-
+                put(f, x, y, jnp.concatenate([parts[0][f], parts[1][f]], axis=0))
+    span_product()
+
+    for axis in range(2):
         for n in range(4):
             line = [(k, n) if axis == 0 else (n, k) for k in range(4)]
             t = [[load(f, x, y) for f in range(5)] for x, y in line]
@@ -282,9 +276,51 @@
                          coef(coef_ref, HH, x, y))
                 )
             nu = coef(coef_ref, NU, *line[0])
-            sides = []
+            for f in range(5):
+                tt = [t[k][f] for k in range(4)]
+                fl = []
+                for i in range(4):
+                    fl.append(nu * row_product(i, tt) - g[i][f])
+                for i, (x, y) in enumerate(line):
+                    r = row(f, x, y)
+                    total = acc[r : r + 8, :] + row_product(i, fl)
+                    if axis == 0:
+                        other = jnp.where(
+                            top_lane, pltpu.roll(tt[i], LANES - 1, 1), pltpu.roll(tt[i], 1, 1)
+                        )
+                        total = total + coef(coef_ref, SZ, x, y) * (other - tt[i])
+                    acc[r : r + 8, :] = total
+
+
+def row_product(i, values):
+    total = None
+    for k in range(4):
+        if k != i:
+            term = DERIV[i][k] * values[k]
+            total = term if total is None else total + term
+    return total
+
+
+def add_faces(load, coef_ref, recv, coef_recv, odd_x, odd_y, acc, work, finish):
+    for axis, odd in ((0, odd_x), (1, odd_y)):
+        near, far = recv[2 * axis : 2 * axis + 2]
+        near_c, far_c = coef_recv[2 * axis : 2 * axis + 2]
+
+        def pick(low, r, rows=8):
+            a, b = near[r : r + rows, :], far[r : r + rows, :]
+            return jnp.where(odd, a, b) if low else jnp.where(odd, b, a)
+
+        def pick_coef(low, place, n):
+            r = 2 * FACE + 4 * place + n
+            a, b = near_c[r : r + 1, :], far_c[r : r + 1, :]
+            return jnp.where(odd, a, b) if low else jnp.where(odd, b, a)
+
+        for n in range(4):
+            line = [(k, n) if axis == 0 else (n, k) for k in range(4)]
+            nu3 = 3.0 * coef(coef_ref, NU, *line[0])
+            shift, extra = [], []
             for low in (True, False):
-                mine = t[0] if low else t[3]
+                place = line[0] if low else line[3]
                 far_t = [pick(low, face_row(f, n)) for f in range(5)]
                 v = [pick_coef(low, d, n) for d in range(3)]
                 dp = 0.4 * far_t[4] + pick_coef(low, 3, n) * far_t[0]
@@ -292,111 +328,100 @@
                     dp = dp - (0.4 * v[d]) * far_t[1 + d]
                 far_g = flux(axis, far_t, v, dp, far_t[4] + dp, pick_coef(low, 4, n))
                 far_nu = pick_coef(low, 5, n)
-                own_s = coef(coef_ref, SX + axis, *(line[0] if low else line[3]))
-                s3 = 3.0 * jnp.maximum(own_s, pick_coef(low, 6, n))
-                far_f, jump, mean = [], [], []
+                s3 = 3.0 * jnp.maximum(
+                    coef(coef_ref, SX + axis, *place), pick_coef(low, 6, n)
+                )
+                moved, added = [], []
                 for f in range(5):
-                    step3 = 3.0 * (far_t[f] - mine[f])
+                    gap = far_t[f] - load(f, *place)
                     far_d = pick(low, FACE + face_row(f, n))
-                    far_q = far_d - step3 if low else far_d + step3
+                    far_q = far_d - 3.0 * gap if low else far_d + 3.0 * gap
                     value = 3.0 * (far_nu * far_q - far_g[f])
-                    far_f.append(-value if low else value)
-                    jump.append(s3 * (far_t[f] - mine[f]))
-                    mean.append(3.0 * far_t[f])
-                sides.append((far_f, jump, mean))
+                    added.append(s3 * gap - value if low else s3 * gap + value)
+                    moved.append(-(nu3 * far_t[f]) if low else nu3 * far_t[f])
+                shift.append(moved)
+                extra.append(added)
             for f in range(5):
-                tt = [t[k][f] for k in range(4)]
-                fl = []
-                for i in range(4):
-                    q = None
-                    for k in range(4):
-                        if k != i:
-                            term = DERIV[i][k] * tt[k]
-                            q = term if q is None else q + term
+                for i, (x, y) in enumerate(line):
+                    r = row(f, x, y)
+                    total = (acc if axis == 0 else work)[r : r + 8, :]
+                    if i != 0:
+                        total = total + DERIV[i][0] * shift[0][f]
+                    if i != 3:
+                        total = total + DERIV[i][3] * shift[1][f]
                     if i == 0:
-                        q = q - sides[0][2][f]
+                        total = total + extra[0][f]
                     if i == 3:
-                        q = q + sides[1][2][f]
-                    fl.append(nu * q - g[i][f])
-                for i, (x, y) in enumerate(line):
-                    total = None
-                    for k in range(4):
-                        if k != i:
-                            term = DERIV[i][k] * fl[k]
-                            total = term if total is None else total + term
-                    if i == 0:
-                        total = total + (sides[0][0][f] + sides[0][1][f])
-                    if i == 3:
-                        total = total + (sides[1][0][f] + sides[1][1][f])
-                    r = row(f, x, y)
-                    total = total + acc[r : r + 8, :]
+                        total = total + extra[1][f]
                     if axis == 0:
-                        tz = tt[i]
-                        other = jnp.where(
-                            top_lane, pltpu.roll(tz, LANES - 1, 1), pltpu.roll(tz, 1, 1)
-                        )
-                        total = total + coef(coef_ref, SZ, x, y) * (other - tz)
-                        acc[r : r + 8, :] = total
+                        work[r : r + 8, :] = total
                     else:
-                        finish(f, x, y, tt[i], total)
-
-
-def first_kernel(t_ref, coef_ref, wm_ref, r0, r1, r2, r3, s_ref, m0, m1, m2, m3, acc, ops, aux):
+                        finish(f, x, y, total)
+
+
+def loader(ref):
+    def load(f, x, y):
+        r = row(f, x, y)
+        return ref[r : r + 8, :]
+
+    return load
+
+
+def first_volume(t_ref, coef_ref, acc, wm_ref, ops, aux):
+    span_table(wm_ref)
+    volume(lambda f, x, y: tan_in(t_ref, f, x, y), coef_ref, wm_ref, acc, ops, aux)
+
+
+def second_volume(s_ref, coef_ref, wm_ref, acc, ops, aux):
+    volume(loader(s_ref), coef_ref, wm_ref, acc, ops, aux)
+
+
+def first_faces(t_ref, coef_ref, acc, r0, r1, r2, r3, s_ref, m0, m1, m2, m3, work):
     odd_x = lax.axis_index("gx") % 2 == 1
     odd_y = lax.axis_index("gy") % 2 == 1
-
-    def finish(f, x, y, t, total):
+    load = lambda f, x, y: tan_in(t_ref, f, x, y)
+
+    def finish(f, x, y, total):
         r = row(f, x, y)
-        s_ref[r : r + 8, :] = t + STEP * total
-
-    faces = by_face((r0, r1, r2, r3))
-    section(
-        lambda f, x, y: tan_in(t_ref, f, x, y), coef_ref, faces,
-        [(ref, 2 * FACE) for ref in faces], odd_x, odd_y, wm_ref, acc, ops, aux, finish,
-    )
-
-    def load(f, x, y):
-        r = row(f, x, y)
-        return s_ref[r : r + 8, :]
-
-    pack_faces(load, by_face((m0, m1, m2, m3)), odd_x, odd_y)
-
-
-def second_kernel(
-    t_ref, s_ref, coef_ref, wm_ref, c0, c1, c2, c3, r0, r1, r2, r3, out_ref, acc, ops, aux
+        s_ref[r : r + 8, :] = load(f, x, y) + STEP * total
+
+    faces = by_face((r0, r1, r2, r3), ORDER_1)
+    add_faces(load, coef_ref, faces, faces, odd_x, odd_y, acc, work, finish)
+    pack_faces(loader(s_ref), by_face((m0, m1, m2, m3), ORDER_2), odd_x, odd_y)
+
+
+def second_faces(
+    t_ref, s_ref, coef_ref, acc, c0, c1, c2, c3, r0, r1, r2, r3, out_ref, work
 ):
     odd_x = lax.axis_index("gx") % 2 == 1
     odd_y = lax.axis_index("gy") % 2 == 1
-
-    def load(f, x, y):
-        r = row(f, x, y)
-        return s_ref[r : r + 8, :]
-
-    def finish(f, x, y, s, total):
-        value = 0.5 * tan_in(t_ref, f, x, y) + (0.5 * s + (0.5 * STEP) * total)
+    load = loader(s_ref)
+
+    def finish(f, x, y, total):
+        value = 0.5 * tan_in(t_ref, f, x, y) + (0.5 * load(f, x, y) + (0.5 * STEP) * total)
         out_ref[pl.ds(f * 16 + x * 4 + y, COLS, stride=80), :] = value
 
-    section(
-        load, coef_ref, by_face((r0, r1, r2, r3)),
-        [(ref, 2 * FACE) for ref in by_face((c0, c1, c2, c3))],
-        odd_x, odd_y, wm_ref, acc, ops, aux, finish,
-    )
-
-
-def call(kernel, shapes, scratch, args, cost):
-    vmem = pl.BlockSpec(memory_space=pltpu.VMEM)
+    add_faces(
+        load, coef_ref, by_face((r0, r1, r2, r3), ORDER_2),
+        by_face((c0, c1, c2, c3), ORDER_1), odd_x, odd_y, acc, work, finish,
+    )
+
+
+def call(kernel, shapes, scratch, args, flops, space=pltpu.VMEM, limit=16):
     return pl.pallas_call(
         kernel,
-        out_shape=[jax.ShapeDtypeStruct(s, jnp.float32) for s in shapes],
-        in_specs=[vmem] * len(args),
-        out_specs=[vmem] * len(shapes),
+        out_shape=[
+            s if hasattr(s, "dtype") else jax.ShapeDtypeStruct(s, jnp.float32) for s in shapes
+        ],
+        in_specs=[pl.BlockSpec(memory_space=space)] * len(args),
+        out_specs=[pl.BlockSpec(memory_space=pltpu.VMEM)] * len(shapes),
         scratch_shapes=scratch,
-        compiler_params=pltpu.CompilerParams(vmem_limit_bytes=32 * 1024 * 1024),
-        cost_estimate=pl.CostEstimate(flops=cost, bytes_accessed=1000000, transcendentals=0),
+        compiler_params=pltpu.CompilerParams(vmem_limit_bytes=limit * 1024 * 1024),
+        cost_estimate=pl.CostEstimate(flops=flops, bytes_accessed=1000000, transcendentals=0),
     )(*args)
 
 
-def exchange(messages):
+def exchange(messages, order):
     size_x, size_y = lax.axis_size("gx"), lax.axis_size("gy")
 
     def pairs(size, first):
@@ -415,32 +440,42 @@
         ("gy", pairs(size_y, 0)),
         ("gy", pairs(size_y, 1)),
     )
-    return [lax.ppermute(m, *plan[face]) for m, face in zip(messages, ORDER)]
+    return [lax.ppermute(m, *plan[face]) for m, face in zip(messages, order)]
 
 
 def per_device(tangent, base_state, shock_flags):
     t = tangent.reshape(640, LANES)
     base = base_state.reshape(80, LANES)
     flags = shock_flags.reshape(1, 32)
-    wm = jnp.asarray(span_table())
     message = (2 * FACE + COEF_ROWS, LANES)
     short = (2 * FACE, LANES)
-    scratch = [
-        pltpu.VMEM((640, LANES), jnp.float32),
+    whole = (640, LANES)
+    volume_scratch = [
         pltpu.VMEM((640, 2 * LANES), jnp.bfloat16),
         pltpu.VMEM((256, LANES), jnp.float32),
     ]
+    work = [pltpu.VMEM(whole, jnp.float32)]
+    staging = [
+        pltpu.VMEM(whole, jnp.float32),
+        pltpu.VMEM(base.shape, jnp.float32),
+        pltpu.VMEM(flags.shape, jnp.int32),
+        pltpu.SemaphoreType.DMA((3,)),
+    ]
     coefs, *faces = call(
-        pack_kernel, [(192, LANES)] + [message] * 4, [], [t, base, flags], 1000000
-    )
-    got = exchange(faces)
+        pack_kernel, [(192, LANES)] + [message] * 4, staging, [t, base, flags], 1000000,
+        space=pltpu.HBM, limit=56,
+    )
+    got = exchange(faces, ORDER_1)
+    inner, wm = call(
+        first_volume, [whole, jax.ShapeDtypeStruct((256, 256), jnp.bfloat16)], volume_scratch, [t, coefs],
+        10000000,
+    )
     s, *faces = call(
-        first_kernel, [(640, LANES)] + [short] * 4, scratch, [t, coefs, wm, *got], 10000000
-    )
-    again = exchange(faces)
-    (out,) = call(
-        second_kernel, [(640, LANES)], scratch, [t, s, coefs, wm, *got, *again], 10000000
-    )
+        first_faces, [whole] + [short] * 4, work, [t, coefs, inner, *got], 1000000
+    )
+    again = exchange(faces, ORDER_2)
+    (inner,) = call(second_volume, [whole], volume_scratch, [s, coefs, wm], 10000000)
+    (out,) = call(second_faces, [whole], work, [t, s, coefs, inner, *got, *again], 1000000)
     return out.reshape(tangent.shape)
 
 

time: 50.1 us -> 46.7 us (0.932)
  waiting for transfers between devices: 5.49 us -> 1.99 us
  Pallas kernels: 3.44 us -> 5.69 us
  local copies, waits for them, and re-layouts: 2.41 us -> 0.89 us
  starting transfers between devices: 38.2 us -> 37.6 us
    ppermute x8, waiting for transfers between devices: 5.49 us -> 1.99 us  [exchange(): return [lax.ppermute(m, *plan[face]) for m, face in zip(messages, order)]]
    pallas_call x3 -> x5, Pallas kernels: 3.44 us -> 5.69 us  [call(): pl.pallas_call(kernel, out_shape=[s if hasattr(s, 'dtype') else jax.Shape...]
    unnamed x8 -> x4, local copies, waits for them, and re-layouts: 2.41 us -> 0.89 us
    ppermute x8, starting transfers between devices: 38.2 us -> 37.6 us  [exchange(): return [lax.ppermute(m, *plan[face]) for m, face in zip(messages, order)]]
  transfers between devices with their start and end apart: 8 -> 8, of which waited for: 2 -> 2; matrix products, arithmetic and copies ran while one was open for 0% -> 0% of each run, Pallas kernels for 0% -> 4%
where the time goes in v3:
time: 46.7 us; the launch traced here: 46.3 us
  starting transfers between devices  37.6 us (81%)
  Pallas kernels  5.69 us (12%)
  waiting for transfers between devices  1.99 us (4%)
  local copies, waits for them, and re-layouts  0.89 us (2%)
    ppermute x8, starting transfers between devices, exchange(): return [lax.ppermute(m, *plan[face]) for m, face in zip(messages, order)]  37.6 us
    pallas_call x5, Pallas kernels, call(): pl.pallas_call(kernel, out_shape=[s if hasattr(s, 'dtype') else jax.Shape...  5.69 us
    ppermute x8, waiting for transfers between devices, exchange(): return [lax.ppermute(m, *plan[face]) for m, face in zip(messages, order)]  1.99 us
  transfers between devices with their start and end apart: 8, of which 2 were waited for; matrix products, arithmetic and copies ran while one was open for 0% of the time, Pallas kernels for 4%

profile of v3, /device:TPU:7, one launch (start us, length us, event | category | flops | bytes accessed | tf_op | source)
XLA Modules:
  0.0 46.3 jit_solution(11534116687690513591)
XLA Ops:
  0.0 0.0 copy-start
  0.0 2.2 %shard_map.37 = (f32[192,128]{1,0:T(8,128)}, f32[352,128]{1,0:T(8,128)}, f32[352,128]{1,0:T(8,128)}, f32[352,128]{1,0:T(8,128)}, f32[352,128]{1,0:T(8,128)}) custom-call(f32[640,128]{1,0:T(8,128)} %bitcast.4, f32[80,128]{1,0:T(8,128)} %bitcast.8, s32[1,32]{1,0:T(1,128)} %bitcast.9), custom_call_target="tpu_custom_call" | custom-call | flops 1000000 | bytes 1000000 | tf_op jit(solution)/shard_map/pallas_call | solution.py:411
  2.2 3.2 %collective-permute-start = (f32[352,128]{1,0:T(8,128)}, f32[352,128]{1,0:T(8,128)S(1)}, u32[]{:S(2)}, u32[]{:S(2)}) collective-permute-start(f32[352,128]{1,0:T(8,128)} %get-tuple-element.19), channel_id=1, source_target_pairs={{0,4},{4,0},{8,12},{12,8},{16,20},{20,16},{24,28},{28,24},{32,36},... | collective-permute-start | bytes 540680 | tf_op jit(solution)/shard_map/ppermute | solution.py:443
  5.4 12.8 %collective-permute-start.1 = (f32[352,128]{1,0:T(8,128)}, f32[352,128]{1,0:T(8,128)S(1)}, u32[]{:S(2)}, u32[]{:S(2)}) collective-permute-start(f32[352,128]{1,0:T(8,128)} %get-tuple-element.20), channel_id=1, source_target_pairs={{4,8},{8,4},{12,16},{16,12},{20,24},{24,20},{28,32},{32,28},{36,40... | collective-permute-start | bytes 540680 | tf_op jit(solution)/shard_map/ppermute | solution.py:443
  18.2 6.8 %collective-permute-start.2 = (f32[352,128]{1,0:T(8,128)}, f32[352,128]{1,0:T(8,128)S(1)}, u32[]{:S(2)}, u32[]{:S(2)}) collective-permute-start(f32[352,128]{1,0:T(8,128)} %get-tuple-element.21), channel_id=1, source_target_pairs={{1,2},{2,1},{0,0},{3,3},{5,6},{6,5},{4,4},{7,7},{9,10},{10,9},{8,8... | collective-permute-start | bytes 540680 | tf_op jit(solution)/shard_map/ppermute | solution.py:443
  25.0 1.9 %collective-permute-start.3 = (f32[352,128]{1,0:T(8,128)}, f32[352,128]{1,0:T(8,128)S(1)}, u32[]{:S(2)}, u32[]{:S(2)}) collective-permute-start(f32[352,128]{1,0:T(8,128)} %get-tuple-element.22), channel_id=1, source_target_pairs={{0,1},{1,0},{2,3},{3,2},{4,5},{5,4},{6,7},{7,6},{8,9},{9,8},{10,11... | collective-permute-start | bytes 540680 | tf_op jit(solution)/shard_map/ppermute | solution.py:443
  27.0 0.0 copy-done
  27.0 0.0 copy-start.1
  27.0 0.9 %copy-done.1 = f32[192,128]{1,0:T(8,128)S(1)} copy-done((f32[192,128]{1,0:T(8,128)S(1)}, f32[192,128]{1,0:T(8,128)}, u32[]{:S(2)}) %copy-start.1) | copy-done | bytes 98328
  27.9 1.1 %shard_map.38 = (f32[640,128]{1,0:T(8,128)S(1)}, bf16[256,256]{1,0:T(8,128)(2,1)S(1)}) custom-call(f32[640,128]{1,0:T(8,128)S(1)} %bitcast.5, f32[192,128]{1,0:T(8,128)S(1)} %copy-done.1), custom_call_target="tpu_custom_call" | custom-call | flops 10000000 | bytes 1000000 | tf_op jit(solution)/shard_map/pallas_call | solution.py:411
  29.0 0.0 collective-permute-done.r0.c0
  29.0 0.0 collective-permute-done.1.r1.c1
  29.0 0.2 collective-permute-done.2.r2.c2
  29.2 0.0 collective-permute-done.3.r3.c3
  29.2 0.5 %shard_map.39 = (f32[640,128]{1,0:T(8,128)S(1)}, f32[320,128]{1,0:T(8,128)S(1)}, f32[320,128]{1,0:T(8,128)S(1)}, f32[320,128]{1,0:T(8,128)S(1)}, f32[320,128]{1,0:T(8,128)S(1)}) custom-call(f32[640,128]{1,0:T(8,128)S(1)} %bitcast.6, f32[192,128]{1,0:T(8,128)S(1)} %copy-done.1, f32[640,128]{1,0:T(8,128)S(1)} %get-tuple-element.18.acc, ...), custom_call_target="tpu_custom_call" | custom-call | flops 1000000 | bytes 1000000 | tf_op jit(solution)/shard_map/pallas_call | solution.py:411
  29.8 4.0 %collective-permute-start.4 = (f32[320,128]{1,0:T(8,128)S(1)}, f32[320,128]{1,0:T(8,128)S(1)}, u32[]{:S(2)}, u32[]{:S(2)}) collective-permute-start(f32[320,128]{1,0:T(8,128)S(1)} %get-tuple-element.25), channel_id=1, source_target_pairs={{4,8},{8,4},{12,16},{16,12},{20,24},{24,20},{28,32},{32,28},{36,40... | collective-permute-start | bytes 491528 | tf_op jit(solution)/shard_map/ppermute | solution.py:443
  33.8 5.0 %collective-permute-start.5 = (f32[320,128]{1,0:T(8,128)S(1)}, f32[320,128]{1,0:T(8,128)S(1)}, u32[]{:S(2)}, u32[]{:S(2)}) collective-permute-start(f32[320,128]{1,0:T(8,128)S(1)} %get-tuple-element.26), channel_id=1, source_target_pairs={{1,2},{2,1},{0,0},{3,3},{5,6},{6,5},{4,4},{7,7},{9,10},{10,9},{8,8... | collective-permute-start | bytes 491528 | tf_op jit(solution)/shard_map/ppermute | solution.py:443
  38.8 1.9 %collective-permute-start.6 = (f32[320,128]{1,0:T(8,128)S(1)}, f32[320,128]{1,0:T(8,128)S(1)}, u32[]{:S(2)}, u32[]{:S(2)}) collective-permute-start(f32[320,128]{1,0:T(8,128)S(1)} %get-tuple-element.27), channel_id=1, source_target_pairs={{0,4},{4,0},{8,12},{12,8},{16,20},{20,16},{24,28},{28,24},{32,36},... | collective-permute-start | bytes 491528 | tf_op jit(solution)/shard_map/ppermute | solution.py:443
  40.7 1.9 %collective-permute-start.7 = (f32[320,128]{1,0:T(8,128)S(1)}, f32[320,128]{1,0:T(8,128)S(1)}, u32[]{:S(2)}, u32[]{:S(2)}) collective-permute-start(f32[320,128]{1,0:T(8,128)S(1)} %get-tuple-element.28), channel_id=1, source_target_pairs={{0,1},{1,0},{2,3},{3,2},{4,5},{5,4},{6,7},{7,6},{8,9},{9,8},{10,11... | collective-permute-start | bytes 491528 | tf_op jit(solution)/shard_map/ppermute | solution.py:443
  42.6 0.7 %shard_map.40.acc = f32[640,128]{1,0:T(8,128)S(1)} custom-call(f32[640,128]{1,0:T(8,128)S(1)} %get-tuple-element.23.s_ref, f32[192,128]{1,0:T(8,128)S(1)} %copy-done.1, bf16[256,256]{1,0:T(8,128)(2,1)S(1)} %get-tuple-element.24.wm_ref), custom_call_target="tpu_custom_call" | custom-call | flops 10000000 | bytes 1000000 | tf_op jit(solution)/shard_map/pallas_call | solution.py:411
  43.4 0.0 collective-permute-done.4.r0
  43.4 1.7 %collective-permute-done.5.r1 = f32[320,128]{1,0:T(8,128)S(1)} collective-permute-done((f32[320,128]{1,0:T(8,128)S(1)}, f32[320,128]{1,0:T(8,128)S(1)}, u32[]{:S(2)}, u32[]{:S(2)}) %collective-permute-start.5) | collective-permute-done | bytes 163872 | tf_op jit(solution)/shard_map/ppermute | solution.py:443
  45.1 0.0 collective-permute-done.6.r2
  45.1 0.0 collective-permute-done.7.r3
  45.1 1.2 %shard_map.41 = f32[640,128]{1,0:T(8,128)} custom-call(f32[640,128]{1,0:T(8,128)S(1)} %bitcast.7, f32[640,128]{1,0:T(8,128)S(1)} %get-tuple-element.23.s_ref, f32[192,128]{1,0:T(8,128)S(1)} %copy-done.1, f32[640,128]{1,0:T(8,128)S(1)} %shard_map.40.acc, f32[352,128]{1,0:T(8,128)S(1)} %collective-permute-done.r0.c0, ...), custom_call_target="tpu_custom_call" | custom-call | flops 1000000 | bytes 1000000 | tf_op jit(solution)/shard_map/pallas_call | solution.py:411
Async XLA Ops:
  0.0 27.0 %copy-start = (f32[8,5,4,4,128]{4,3,2,1,0:T(4,128)S(1)}, f32[8,5,4,4,128]{4,3,2,1,0:T(4,128)}, u32[]{:S(2)}) copy-start(f32[8,5,4,4,128]{4,3,2,1,0:T(4,128)} %param.3) | copy-start | bytes 983044
  2.2 26.8 %collective-permute-start = (f32[352,128]{1,0:T(8,128)}, f32[352,128]{1,0:T(8,128)S(1)}, u32[]{:S(2)}, u32[]{:S(2)}) collective-permute-start(f32[352,128]{1,0:T(8,128)} %get-tuple-element.19), channel_id=1, source_target_pairs={{0,4},{4,0},{8,12},{12,8},{16,20},{20,16},{24,28},{28,24},{32,36},... | collective-permute-start | bytes 540680 | tf_op jit(solution)/shard_map/ppermute | solution.py:443
  5.4 23.6 %collective-permute-start.1 = (f32[352,128]{1,0:T(8,128)}, f32[352,128]{1,0:T(8,128)S(1)}, u32[]{:S(2)}, u32[]{:S(2)}) collective-permute-start(f32[352,128]{1,0:T(8,128)} %get-tuple-element.20), channel_id=1, source_target_pairs={{4,8},{8,4},{12,16},{16,12},{20,24},{24,20},{28,32},{32,28},{36,40... | collective-permute-start | bytes 540680 | tf_op jit(solution)/shard_map/ppermute | solution.py:443
  18.2 11.0 %collective-permute-start.2 = (f32[352,128]{1,0:T(8,128)}, f32[352,128]{1,0:T(8,128)S(1)}, u32[]{:S(2)}, u32[]{:S(2)}) collective-permute-start(f32[352,128]{1,0:T(8,128)} %get-tuple-element.21), channel_id=1, source_target_pairs={{1,2},{2,1},{0,0},{3,3},{5,6},{6,5},{4,4},{7,7},{9,10},{10,9},{8,8... | collective-permute-start | bytes 540680 | tf_op jit(solution)/shard_map/ppermute | solution.py:443
  25.0 4.2 %collective-permute-start.3 = (f32[352,128]{1,0:T(8,128)}, f32[352,128]{1,0:T(8,128)S(1)}, u32[]{:S(2)}, u32[]{:S(2)}) collective-permute-start(f32[352,128]{1,0:T(8,128)} %get-tuple-element.22), channel_id=1, source_target_pairs={{0,1},{1,0},{2,3},{3,2},{4,5},{5,4},{6,7},{7,6},{8,9},{9,8},{10,11... | collective-permute-start | bytes 540680 | tf_op jit(solution)/shard_map/ppermute | solution.py:443
  27.0 0.9 %copy-start.1 = (f32[192,128]{1,0:T(8,128)S(1)}, f32[192,128]{1,0:T(8,128)}, u32[]{:S(2)}) copy-start(f32[192,128]{1,0:T(8,128)} %get-tuple-element.17.coef_ref) | copy-start | bytes 294916
  29.8 13.6 %collective-permute-start.4 = (f32[320,128]{1,0:T(8,128)S(1)}, f32[320,128]{1,0:T(8,128)S(1)}, u32[]{:S(2)}, u32[]{:S(2)}) collective-permute-start(f32[320,128]{1,0:T(8,128)S(1)} %get-tuple-element.25), channel_id=1, source_target_pairs={{4,8},{8,4},{12,16},{16,12},{20,24},{24,20},{28,32},{32,28},{36,40... | collective-permute-start | bytes 491528 | tf_op jit(solution)/shard_map/ppermute | solution.py:443
  33.8 11.3 %collective-permute-start.5 = (f32[320,128]{1,0:T(8,128)S(1)}, f32[320,128]{1,0:T(8,128)S(1)}, u32[]{:S(2)}, u32[]{:S(2)}) collective-permute-start(f32[320,128]{1,0:T(8,128)S(1)} %get-tuple-element.26), channel_id=1, source_target_pairs={{1,2},{2,1},{0,0},{3,3},{5,6},{6,5},{4,4},{7,7},{9,10},{10,9},{8,8... | collective-permute-start | bytes 491528 | tf_op jit(solution)/shard_map/ppermute | solution.py:443
  38.8 6.3 %collective-permute-start.6 = (f32[320,128]{1,0:T(8,128)S(1)}, f32[320,128]{1,0:T(8,128)S(1)}, u32[]{:S(2)}, u32[]{:S(2)}) collective-permute-start(f32[320,128]{1,0:T(8,128)S(1)} %get-tuple-element.27), channel_id=1, source_target_pairs={{0,4},{4,0},{8,12},{12,8},{16,20},{20,16},{24,28},{28,24},{32,36},... | collective-permute-start | bytes 491528 | tf_op jit(solution)/shard_map/ppermute | solution.py:443
  40.7 4.4 %collective-permute-start.7 = (f32[320,128]{1,0:T(8,128)S(1)}, f32[320,128]{1,0:T(8,128)S(1)}, u32[]{:S(2)}, u32[]{:S(2)}) collective-permute-start(f32[320,128]{1,0:T(8,128)S(1)} %get-tuple-element.28), channel_id=1, source_target_pairs={{0,1},{1,0},{2,3},{3,2},{4,5},{5,4},{6,7},{7,6},{8,9},{9,8},{10,11... | collective-permute-start | bytes 491528 | tf_op jit(solution)/shard_map/ppermute | solution.py:443

commit v4 on v3

--- a/solution.py
+++ b/solution.py
@@ -13,8 +13,11 @@
 LANES = 128
 V1, V2, V3, W1, W2, W3, KE, HH, SX, SY, SZ, NU = range(12)
 FACE = 160
+HALF = 80
 FACE_NAMES = (V1, V2, V3, KE, HH, NU)
 COEF_ROWS = 32
+COEF_AT = FACE + HALF
+PLACE_AT = 12 * 16
 ORDER_1 = (0, 1, 3, 2)
 ORDER_2 = (1, 3, 0, 2)
 
@@ -133,8 +136,17 @@
         1.0,
         0.0,
     )
-    flags = jnp.broadcast_to(flags_ref[...].astype(jnp.float32), (8, 32))
-    flags = jnp.dot(flags, spread, preferred_element_type=jnp.float32)
+    element_flags = jnp.broadcast_to(flags_ref[...].astype(jnp.float32), (8, 32))
+    flags = jnp.dot(element_flags, spread, preferred_element_type=jnp.float32)
+    ahead = jnp.where(
+        lax.broadcasted_iota(jnp.int32, (32, LANES), 1) // 4
+        > lax.broadcasted_iota(jnp.int32, (32, LANES), 0),
+        1.0,
+        0.0,
+    )
+    rank = jnp.dot(element_flags, ahead, preferred_element_type=jnp.float32)
+    place = 4.0 * rank + zi[:8].astype(jnp.float32)
+    coef_ref[PLACE_AT : PLACE_AT + 8, :] = jnp.where(flags > 0.5, place, -1000.0)
     nu = 0.1 * flags * shape
     nu = jnp.concatenate([nu, nu], axis=0)
     table = {
@@ -147,7 +159,29 @@
         coef_ref[name * 16 : (name + 1) * 16, :] = value
 
 
-def pack_faces(load, outs, odd_x, odd_y):
+def selection(place):
+    m = lax.broadcasted_iota(jnp.int32, (LANES, LANES), 0).astype(jnp.float32)
+    lower = jnp.where(m == place, 1.0, 0.0).astype(jnp.bfloat16)
+    upper = jnp.where(m == place + 64.0, 1.0, 0.0).astype(jnp.bfloat16)
+    return jnp.concatenate([lower, upper], axis=1)
+
+
+def select(value, chosen, dims):
+    hi = value.astype(jnp.bfloat16)
+    lo = (value - hi.astype(jnp.float32)).astype(jnp.bfloat16)
+    return sum(
+        lax.dot_general(part, chosen, (dims, ((), ())), preferred_element_type=jnp.float32)
+        for part in (hi, lo)
+    )
+
+
+def wide_at(face, f, n):
+    item = f * 4 + n
+    r, c = face * HALF + (item % 10) * 8, (item // 10) * LANES
+    return slice(r, r + 8), slice(c, c + LANES)
+
+
+def pack_faces(load, coef_ref, outs, odd_x, odd_y, wide):
     for axis, (near, far), odd in ((0, outs[:2], odd_x), (1, outs[2:], odd_y)):
         for f in range(5):
             for n in range(4):
@@ -160,8 +194,12 @@
                 r = face_row(f, n)
                 near[r : r + 8, :] = jnp.where(odd, line[0], line[3])
                 far[r : r + 8, :] = jnp.where(odd, line[3], line[0])
-                near[FACE + r : FACE + r + 8, :] = jnp.where(odd, lower, upper)
-                far[FACE + r : FACE + r + 8, :] = jnp.where(odd, upper, lower)
+                wide[wide_at(2 * axis, f, n)] = jnp.where(odd, lower, upper)
+                wide[wide_at(2 * axis + 1, f, n)] = jnp.where(odd, upper, lower)
+    chosen = selection(coef_ref[PLACE_AT : PLACE_AT + 1, :])
+    for face in range(4):
+        rows = wide[face * HALF : (face + 1) * HALF, :]
+        outs[face][FACE:COEF_AT, :] = select(rows, chosen, ((1,), (1,)))
 
 
 def by_face(refs, order):
@@ -170,7 +208,7 @@
 
 def pack_kernel(t_hbm, base_hbm, flags_hbm, coef_ref, *refs):
     xn, xf, yn, yf = by_face(refs[:4], ORDER_1)
-    t_ref, base_ref, flags_ref, sems = refs[4:]
+    t_ref, base_ref, flags_ref, wide, sems = refs[4:]
     copies = [
         pltpu.make_async_copy(src, dst, sems.at[k])
         for k, (src, dst) in enumerate(
@@ -185,7 +223,9 @@
     copies[1].wait()
     base_coefs(base_ref, flags_ref, coef_ref)
     copies[2].wait()
-    pack_faces(lambda f, x, y: tan_in(t_ref, f, x, y), (xn, xf, yn, yf), odd_x, odd_y)
+    faces = (xn, xf, yn, yf)
+    load = lambda f, x, y: tan_in(t_ref, f, x, y)
+    pack_faces(load, coef_ref, faces, odd_x, odd_y, wide)
     for axis, (near, far), odd in ((0, (xn, xf), odd_x), (1, (yn, yf), odd_y)):
         for place, name in enumerate(FACE_NAMES + (SX + axis,)):
             first = name * 16
@@ -195,12 +235,12 @@
             else:
                 lower = coef_ref[pl.ds(first, 4, stride=4), :]
                 upper = coef_ref[pl.ds(first + 3, 4, stride=4), :]
-            r = 2 * FACE + 4 * place
+            r = COEF_AT + 4 * place
             near[r : r + 4, :] = jnp.where(odd, lower, upper)
             far[r : r + 4, :] = jnp.where(odd, upper, lower)
-        r = 2 * FACE + 28
-        near[r : r + 4, :] = jnp.zeros((4, LANES), jnp.float32)
-        far[r : r + 4, :] = jnp.zeros((4, LANES), jnp.float32)
+        r = COEF_AT + 28
+        near[r : r + 4, :] = coef_ref[PLACE_AT : PLACE_AT + 4, :]
+        far[r : r + 4, :] = coef_ref[PLACE_AT : PLACE_AT + 4, :]
 
 
 def flux(d, t, v, dp, e, hh):
@@ -301,7 +341,13 @@
     return total
 
 
-def add_faces(load, coef_ref, recv, coef_recv, odd_x, odd_y, acc, work, finish):
+def add_faces(load, coef_ref, recv, coef_recv, odd_x, odd_y, acc, work, wide, finish):
+    for face in range(4):
+        r = COEF_AT + 28
+        chosen = selection(coef_recv[face][r : r + 1, :])
+        wide[face * HALF : (face + 1) * HALF, :] = select(
+            recv[face][FACE:COEF_AT, :], chosen, ((1,), (0,))
+        )
     for axis, odd in ((0, odd_x), (1, odd_y)):
         near, far = recv[2 * axis : 2 * axis + 2]
         near_c, far_c = coef_recv[2 * axis : 2 * axis + 2]
@@ -311,7 +357,7 @@
             return jnp.where(odd, a, b) if low else jnp.where(odd, b, a)
 
         def pick_coef(low, place, n):
-            r = 2 * FACE + 4 * place + n
+            r = COEF_AT + 4 * place + n
             a, b = near_c[r : r + 1, :], far_c[r : r + 1, :]
             return jnp.where(odd, a, b) if low else jnp.where(odd, b, a)
 
@@ -334,7 +380,9 @@
                 moved, added = [], []
                 for f in range(5):
                     gap = far_t[f] - load(f, *place)
-                    far_d = pick(low, FACE + face_row(f, n))
+                    a = wide[wide_at(2 * axis, f, n)]
+                    b = wide[wide_at(2 * axis + 1, f, n)]
+                    far_d = jnp.where(odd, a, b) if low else jnp.where(odd, b, a)
                     far_q = far_d - 3.0 * gap if low else far_d + 3.0 * gap
                     value = 3.0 * (far_nu * far_q - far_g[f])
                     added.append(s3 * gap - value if low else s3 * gap + value)
@@ -376,7 +424,7 @@
     volume(loader(s_ref), coef_ref, wm_ref, acc, ops, aux)
 
 
-def first_faces(t_ref, coef_ref, acc, r0, r1, r2, r3, s_ref, m0, m1, m2, m3, work):
+def first_faces(t_ref, coef_ref, acc, r0, r1, r2, r3, s_ref, m0, m1, m2, m3, work, wide):
     odd_x = lax.axis_index("gx") % 2 == 1
     odd_y = lax.axis_index("gy") % 2 == 1
     load = lambda f, x, y: tan_in(t_ref, f, x, y)
@@ -386,12 +434,13 @@
         s_ref[r : r + 8, :] = load(f, x, y) + STEP * total
 
     faces = by_face((r0, r1, r2, r3), ORDER_1)
-    add_faces(load, coef_ref, faces, faces, odd_x, odd_y, acc, work, finish)
-    pack_faces(loader(s_ref), by_face((m0, m1, m2, m3), ORDER_2), odd_x, odd_y)
+    add_faces(load, coef_ref, faces, faces, odd_x, odd_y, acc, work, wide, finish)
+    sent = by_face((m0, m1, m2, m3), ORDER_2)
+    pack_faces(loader(s_ref), coef_ref, sent, odd_x, odd_y, wide)
 
 
 def second_faces(
-    t_ref, s_ref, coef_ref, acc, c0, c1, c2, c3, r0, r1, r2, r3, out_ref, work
+    t_ref, s_ref, coef_ref, acc, c0, c1, c2, c3, r0, r1, r2, r3, out_ref, work, wide
 ):
     odd_x = lax.axis_index("gx") % 2 == 1
     odd_y = lax.axis_index("gy") % 2 == 1
@@ -403,7 +452,7 @@
 
     add_faces(
         load, coef_ref, by_face((r0, r1, r2, r3), ORDER_2),
-        by_face((c0, c1, c2, c3), ORDER_1), odd_x, odd_y, acc, work, finish,
+        by_face((c0, c1, c2, c3), ORDER_1), odd_x, odd_y, acc, work, wide, finish,
     )
 
 
@@ -447,22 +496,24 @@
     t = tangent.reshape(640, LANES)
     base = base_state.reshape(80, LANES)
     flags = shock_flags.reshape(1, 32)
-    message = (2 * FACE + COEF_ROWS, LANES)
-    short = (2 * FACE, LANES)
+    message = (COEF_AT + COEF_ROWS, LANES)
+    short = (COEF_AT, LANES)
     whole = (640, LANES)
     volume_scratch = [
         pltpu.VMEM((640, 2 * LANES), jnp.bfloat16),
         pltpu.VMEM((256, LANES), jnp.float32),
     ]
-    work = [pltpu.VMEM(whole, jnp.float32)]
+    wide = pltpu.VMEM((4 * HALF, 2 * LANES), jnp.float32)
+    work = [pltpu.VMEM(whole, jnp.float32), wide]
     staging = [
         pltpu.VMEM(whole, jnp.float32),
         pltpu.VMEM(base.shape, jnp.float32),
         pltpu.VMEM(flags.shape, jnp.int32),
+        wide,
         pltpu.SemaphoreType.DMA((3,)),
     ]
     coefs, *faces = call(
-        pack_kernel, [(192, LANES)] + [message] * 4, staging, [t, base, flags], 1000000,
+        pack_kernel, [(PLACE_AT + 8, LANES)] + [message] * 4, staging, [t, base, flags], 1000000,
         space=pltpu.HBM, limit=56,
     )
     got = exchange(faces, ORDER_1)

time: 46.7 us -> 45.8 us (0.981)
  waiting for transfers between devices: 1.99 us -> 0.97 us
  Pallas kernels: 5.69 us -> 6.32 us
  starting transfers between devices: 37.6 us -> 37.1 us
    ppermute x8, waiting for transfers between devices: 1.99 us -> 0.97 us  [exchange(): return [lax.ppermute(m, *plan[face]) for m, face in zip(messages, order)]]
    pallas_call x5, Pallas kernels: 5.69 us -> 6.32 us  [call(): pl.pallas_call(kernel, out_shape=[s if hasattr(s, 'dtype') else jax.Shape...]
    ppermute x8, starting transfers between devices: 37.6 us -> 37.1 us  [exchange(): return [lax.ppermute(m, *plan[face]) for m, face in zip(messages, order)]]
  transfers between devices with their start and end apart: 8 -> 8, of which waited for: 2 -> 1; matrix products, arithmetic and copies ran while one was open for 0% -> 0% of each run, Pallas kernels for 4% -> 4%
where the time goes in v4:
time: 45.8 us; the launch traced here: 45.4 us
  starting transfers between devices  37.1 us (81%)
  Pallas kernels  6.32 us (14%)
  waiting for transfers between devices  0.97 us (2%)
  local copies, waits for them, and re-layouts  0.89 us (2%)
    ppermute x8, starting transfers between devices, exchange(): return [lax.ppermute(m, *plan[face]) for m, face in zip(messages, order)]  37.1 us
    pallas_call x5, Pallas kernels, call(): pl.pallas_call(kernel, out_shape=[s if hasattr(s, 'dtype') else jax.Shape...  6.32 us
    ppermute x8, waiting for transfers between devices, exchange(): return [lax.ppermute(m, *plan[face]) for m, face in zip(messages, order)]  0.97 us
  transfers between devices with their start and end apart: 8, of which 1 were waited for; matrix products, arithmetic and copies ran while one was open for 0% of the time, Pallas kernels for 4%

profile of v4, /device:TPU:7, one launch (start us, length us, event | category | flops | bytes accessed | tf_op | source)
XLA Modules:
  0.0 45.4 jit_solution(8933977582828096337)
XLA Ops:
  0.0 0.0 copy-start
  0.0 2.2 %shard_map.37 = (f32[200,128]{1,0:T(8,128)}, f32[272,128]{1,0:T(8,128)}, f32[272,128]{1,0:T(8,128)}, f32[272,128]{1,0:T(8,128)}, f32[272,128]{1,0:T(8,128)}) custom-call(f32[640,128]{1,0:T(8,128)} %bitcast.4, f32[80,128]{1,0:T(8,128)} %bitcast.8, s32[1,32]{1,0:T(1,128)} %bitcast.9), custom_call_target="tpu_custom_call" | custom-call | flops 1000000 | bytes 1000000 | tf_op jit(solution)/shard_map/pallas_call | solution.py:460
  2.2 3.2 %collective-permute-start = (f32[272,128]{1,0:T(8,128)}, f32[272,128]{1,0:T(8,128)S(1)}, u32[]{:S(2)}, u32[]{:S(2)}) collective-permute-start(f32[272,128]{1,0:T(8,128)} %get-tuple-element.19), channel_id=1, source_target_pairs={{0,4},{4,0},{8,12},{12,8},{16,20},{20,16},{24,28},{28,24},{32,36},... | collective-permute-start | bytes 417800 | tf_op jit(solution)/shard_map/ppermute | solution.py:492
  5.4 12.8 %collective-permute-start.1 = (f32[272,128]{1,0:T(8,128)}, f32[272,128]{1,0:T(8,128)S(1)}, u32[]{:S(2)}, u32[]{:S(2)}) collective-permute-start(f32[272,128]{1,0:T(8,128)} %get-tuple-element.20), channel_id=1, source_target_pairs={{4,8},{8,4},{12,16},{16,12},{20,24},{24,20},{28,32},{32,28},{36,40... | collective-permute-start | bytes 417800 | tf_op jit(solution)/shard_map/ppermute | solution.py:492
  18.3 6.8 %collective-permute-start.2 = (f32[272,128]{1,0:T(8,128)}, f32[272,128]{1,0:T(8,128)S(1)}, u32[]{:S(2)}, u32[]{:S(2)}) collective-permute-start(f32[272,128]{1,0:T(8,128)} %get-tuple-element.21), channel_id=1, source_target_pairs={{1,2},{2,1},{0,0},{3,3},{5,6},{6,5},{4,4},{7,7},{9,10},{10,9},{8,8... | collective-permute-start | bytes 417800 | tf_op jit(solution)/shard_map/ppermute | solution.py:492
  25.1 1.9 %collective-permute-start.3 = (f32[272,128]{1,0:T(8,128)}, f32[272,128]{1,0:T(8,128)S(1)}, u32[]{:S(2)}, u32[]{:S(2)}) collective-permute-start(f32[272,128]{1,0:T(8,128)} %get-tuple-element.22), channel_id=1, source_target_pairs={{0,1},{1,0},{2,3},{3,2},{4,5},{5,4},{6,7},{7,6},{8,9},{9,8},{10,11... | collective-permute-start | bytes 417800 | tf_op jit(solution)/shard_map/ppermute | solution.py:492
  27.0 0.0 copy-done
  27.0 0.0 copy-start.1
  27.0 0.9 %copy-done.1 = f32[200,128]{1,0:T(8,128)S(1)} copy-done((f32[200,128]{1,0:T(8,128)S(1)}, f32[200,128]{1,0:T(8,128)}, u32[]{:S(2)}) %copy-start.1) | copy-done | bytes 102424
  27.9 1.1 %shard_map.38 = (f32[640,128]{1,0:T(8,128)S(1)}, bf16[256,256]{1,0:T(8,128)(2,1)S(1)}) custom-call(f32[640,128]{1,0:T(8,128)S(1)} %bitcast.5, f32[200,128]{1,0:T(8,128)S(1)} %copy-done.1), custom_call_target="tpu_custom_call" | custom-call | flops 10000000 | bytes 1000000 | tf_op jit(solution)/shard_map/pallas_call | solution.py:460
  29.0 0.0 collective-permute-done.r0.c0
  29.0 0.0 collective-permute-done.1.r1.c1
  29.0 0.0 collective-permute-done.2.r2.c2
  29.0 0.0 collective-permute-done.3.r3.c3
  29.1 0.9 %shard_map.39 = (f32[640,128]{1,0:T(8,128)S(1)}, f32[240,128]{1,0:T(8,128)S(1)}, f32[240,128]{1,0:T(8,128)S(1)}, f32[240,128]{1,0:T(8,128)S(1)}, f32[240,128]{1,0:T(8,128)S(1)}) custom-call(f32[640,128]{1,0:T(8,128)S(1)} %bitcast.6, f32[200,128]{1,0:T(8,128)S(1)} %copy-done.1, f32[640,128]{1,0:T(8,128)S(1)} %get-tuple-element.18.acc, ...), custom_call_target="tpu_custom_call" | custom-call | flops 1000000 | bytes 1000000 | tf_op jit(solution)/shard_map/pallas_call | solution.py:460
  29.9 1.9 %collective-permute-start.4 = (f32[240,128]{1,0:T(8,128)S(1)}, f32[240,128]{1,0:T(8,128)S(1)}, u32[]{:S(2)}, u32[]{:S(2)}) collective-permute-start(f32[240,128]{1,0:T(8,128)S(1)} %get-tuple-element.25), channel_id=1, source_target_pairs={{4,8},{8,4},{12,16},{16,12},{20,24},{24,20},{28,32},{32,28},{36,40... | collective-permute-start | bytes 368648 | tf_op jit(solution)/shard_map/ppermute | solution.py:492
  31.8 6.6 %collective-permute-start.5 = (f32[240,128]{1,0:T(8,128)S(1)}, f32[240,128]{1,0:T(8,128)S(1)}, u32[]{:S(2)}, u32[]{:S(2)}) collective-permute-start(f32[240,128]{1,0:T(8,128)S(1)} %get-tuple-element.26), channel_id=1, source_target_pairs={{1,2},{2,1},{0,0},{3,3},{5,6},{6,5},{4,4},{7,7},{9,10},{10,9},{8,8... | collective-permute-start | bytes 368648 | tf_op jit(solution)/shard_map/ppermute | solution.py:492
  38.4 1.9 %collective-permute-start.6 = (f32[240,128]{1,0:T(8,128)S(1)}, f32[240,128]{1,0:T(8,128)S(1)}, u32[]{:S(2)}, u32[]{:S(2)}) collective-permute-start(f32[240,128]{1,0:T(8,128)S(1)} %get-tuple-element.27), channel_id=1, source_target_pairs={{0,4},{4,0},{8,12},{12,8},{16,20},{20,16},{24,28},{28,24},{32,36},... | collective-permute-start | bytes 368648 | tf_op jit(solution)/shard_map/ppermute | solution.py:492
  40.4 1.9 %collective-permute-start.7 = (f32[240,128]{1,0:T(8,128)S(1)}, f32[240,128]{1,0:T(8,128)S(1)}, u32[]{:S(2)}, u32[]{:S(2)}) collective-permute-start(f32[240,128]{1,0:T(8,128)S(1)} %get-tuple-element.28), channel_id=1, source_target_pairs={{0,1},{1,0},{2,3},{3,2},{4,5},{5,4},{6,7},{7,6},{8,9},{9,8},{10,11... | collective-permute-start | bytes 368648 | tf_op jit(solution)/shard_map/ppermute | solution.py:492
  42.3 0.8 %shard_map.40.acc = f32[640,128]{1,0:T(8,128)S(1)} custom-call(f32[640,128]{1,0:T(8,128)S(1)} %get-tuple-element.23.s_ref, f32[200,128]{1,0:T(8,128)S(1)} %copy-done.1, bf16[256,256]{1,0:T(8,128)(2,1)S(1)} %get-tuple-element.24.wm_ref), custom_call_target="tpu_custom_call" | custom-call | flops 10000000 | bytes 1000000 | tf_op jit(solution)/shard_map/pallas_call | solution.py:460
  43.1 0.0 collective-permute-done.4.r0
  43.1 0.0 collective-permute-done.5.r1
  43.1 0.9 %collective-permute-done.6.r2 = f32[240,128]{1,0:T(8,128)S(1)} collective-permute-done((f32[240,128]{1,0:T(8,128)S(1)}, f32[240,128]{1,0:T(8,128)S(1)}, u32[]{:S(2)}, u32[]{:S(2)}) %collective-permute-start.6) | collective-permute-done | bytes 122912 | tf_op jit(solution)/shard_map/ppermute | solution.py:492
  44.1 0.0 collective-permute-done.7.r3
  44.1 1.4 %shard_map.41 = f32[640,128]{1,0:T(8,128)} custom-call(f32[640,128]{1,0:T(8,128)S(1)} %bitcast.7, f32[640,128]{1,0:T(8,128)S(1)} %get-tuple-element.23.s_ref, f32[200,128]{1,0:T(8,128)S(1)} %copy-done.1, f32[640,128]{1,0:T(8,128)S(1)} %shard_map.40.acc, f32[272,128]{1,0:T(8,128)S(1)} %collective-permute-done.r0.c0, ...), custom_call_target="tpu_custom_call" | custom-call | flops 1000000 | bytes 1000000 | tf_op jit(solution)/shard_map/pallas_call | solution.py:460
Async XLA Ops:
  0.0 27.0 %copy-start = (f32[8,5,4,4,128]{4,3,2,1,0:T(4,128)S(1)}, f32[8,5,4,4,128]{4,3,2,1,0:T(4,128)}, u32[]{:S(2)}) copy-start(f32[8,5,4,4,128]{4,3,2,1,0:T(4,128)} %param.3) | copy-start | bytes 983044
  2.2 26.8 %collective-permute-start = (f32[272,128]{1,0:T(8,128)}, f32[272,128]{1,0:T(8,128)S(1)}, u32[]{:S(2)}, u32[]{:S(2)}) collective-permute-start(f32[272,128]{1,0:T(8,128)} %get-tuple-element.19), channel_id=1, source_target_pairs={{0,4},{4,0},{8,12},{12,8},{16,20},{20,16},{24,28},{28,24},{32,36},... | collective-permute-start | bytes 417800 | tf_op jit(solution)/shard_map/ppermute | solution.py:492
  5.4 23.6 %collective-permute-start.1 = (f32[272,128]{1,0:T(8,128)}, f32[272,128]{1,0:T(8,128)S(1)}, u32[]{:S(2)}, u32[]{:S(2)}) collective-permute-start(f32[272,128]{1,0:T(8,128)} %get-tuple-element.20), channel_id=1, source_target_pairs={{4,8},{8,4},{12,16},{16,12},{20,24},{24,20},{28,32},{32,28},{36,40... | collective-permute-start | bytes 417800 | tf_op jit(solution)/shard_map/ppermute | solution.py:492
  18.3 10.8 %collective-permute-start.2 = (f32[272,128]{1,0:T(8,128)}, f32[272,128]{1,0:T(8,128)S(1)}, u32[]{:S(2)}, u32[]{:S(2)}) collective-permute-start(f32[272,128]{1,0:T(8,128)} %get-tuple-element.21), channel_id=1, source_target_pairs={{1,2},{2,1},{0,0},{3,3},{5,6},{6,5},{4,4},{7,7},{9,10},{10,9},{8,8... | collective-permute-start | bytes 417800 | tf_op jit(solution)/shard_map/ppermute | solution.py:492
  25.1 4.0 %collective-permute-start.3 = (f32[272,128]{1,0:T(8,128)}, f32[272,128]{1,0:T(8,128)S(1)}, u32[]{:S(2)}, u32[]{:S(2)}) collective-permute-start(f32[272,128]{1,0:T(8,128)} %get-tuple-element.22), channel_id=1, source_target_pairs={{0,1},{1,0},{2,3},{3,2},{4,5},{5,4},{6,7},{7,6},{8,9},{9,8},{10,11... | collective-permute-start | bytes 417800 | tf_op jit(solution)/shard_map/ppermute | solution.py:492
  27.0 0.9 %copy-start.1 = (f32[200,128]{1,0:T(8,128)S(1)}, f32[200,128]{1,0:T(8,128)}, u32[]{:S(2)}) copy-start(f32[200,128]{1,0:T(8,128)} %get-tuple-element.17.coef_ref) | copy-start | bytes 307204
  29.9 13.2 %collective-permute-start.4 = (f32[240,128]{1,0:T(8,128)S(1)}, f32[240,128]{1,0:T(8,128)S(1)}, u32[]{:S(2)}, u32[]{:S(2)}) collective-permute-start(f32[240,128]{1,0:T(8,128)S(1)} %get-tuple-element.25), channel_id=1, source_target_pairs={{4,8},{8,4},{12,16},{16,12},{20,24},{24,20},{28,32},{32,28},{36,40... | collective-permute-start | bytes 368648 | tf_op jit(solution)/shard_map/ppermute | solution.py:492
  31.8 11.3 %collective-permute-start.5 = (f32[240,128]{1,0:T(8,128)S(1)}, f32[240,128]{1,0:T(8,128)S(1)}, u32[]{:S(2)}, u32[]{:S(2)}) collective-permute-start(f32[240,128]{1,0:T(8,128)S(1)} %get-tuple-element.26), channel_id=1, source_target_pairs={{1,2},{2,1},{0,0},{3,3},{5,6},{6,5},{4,4},{7,7},{9,10},{10,9},{8,8... | collective-permute-start | bytes 368648 | tf_op jit(solution)/shard_map/ppermute | solution.py:492
  38.4 5.6 %collective-permute-start.6 = (f32[240,128]{1,0:T(8,128)S(1)}, f32[240,128]{1,0:T(8,128)S(1)}, u32[]{:S(2)}, u32[]{:S(2)}) collective-permute-start(f32[240,128]{1,0:T(8,128)S(1)} %get-tuple-element.27), channel_id=1, source_target_pairs={{0,4},{4,0},{8,12},{12,8},{16,20},{20,16},{24,28},{28,24},{32,36},... | collective-permute-start | bytes 368648 | tf_op jit(solution)/shard_map/ppermute | solution.py:492
  40.4 3.7 %collective-permute-start.7 = (f32[240,128]{1,0:T(8,128)S(1)}, f32[240,128]{1,0:T(8,128)S(1)}, u32[]{:S(2)}, u32[]{:S(2)}) collective-permute-start(f32[240,128]{1,0:T(8,128)S(1)} %get-tuple-element.28), channel_id=1, source_target_pairs={{0,1},{1,0},{2,3},{3,2},{4,5},{5,4},{6,7},{7,6},{8,9},{9,8},{10,11... | collective-permute-start | bytes 368648 | tf_op jit(solution)/shard_map/ppermute | solution.py:492

commit v5 on v4

--- a/solution.py
+++ b/solution.py
@@ -18,7 +18,7 @@
 COEF_ROWS = 32
 COEF_AT = FACE + HALF
 PLACE_AT = 12 * 16
-ORDER_1 = (0, 1, 3, 2)
+ORDER_1 = (1, 3, 0, 2)
 ORDER_2 = (1, 3, 0, 2)
 
 
@@ -169,10 +169,14 @@
 def select(value, chosen, dims):
     hi = value.astype(jnp.bfloat16)
     lo = (value - hi.astype(jnp.float32)).astype(jnp.bfloat16)
-    return sum(
-        lax.dot_general(part, chosen, (dims, ((), ())), preferred_element_type=jnp.float32)
-        for part in (hi, lo)
-    )
+    both = lax.dot_general(
+        jnp.concatenate([hi, lo], axis=0),
+        chosen,
+        (dims, ((), ())),
+        preferred_element_type=jnp.float32,
+    )
+    rows = value.shape[0]
+    return both[:rows] + both[rows:]
 
 
 def wide_at(face, f, n):
@@ -197,9 +201,9 @@
                 wide[wide_at(2 * axis, f, n)] = jnp.where(odd, lower, upper)
                 wide[wide_at(2 * axis + 1, f, n)] = jnp.where(odd, upper, lower)
     chosen = selection(coef_ref[PLACE_AT : PLACE_AT + 1, :])
+    packed = select(wide[...], chosen, ((1,), (1,)))
     for face in range(4):
-        rows = wide[face * HALF : (face + 1) * HALF, :]
-        outs[face][FACE:COEF_AT, :] = select(rows, chosen, ((1,), (1,)))
+        outs[face][FACE:COEF_AT, :] = packed[face * HALF : (face + 1) * HALF]
 
 
 def by_face(refs, order):

time: 45.8 us -> 45.6 us (level)
  starting transfers between devices: 37.1 us -> 36.6 us
  waiting for transfers between devices: 0.97 us -> 1.44 us
    ppermute x8, starting transfers between devices: 37.1 us -> 36.6 us  [exchange(): return [lax.ppermute(m, *plan[face]) for m, face in zip(messages, order)]]
    ppermute x8, waiting for transfers between devices: 0.97 us -> 1.44 us  [exchange(): return [lax.ppermute(m, *plan[face]) for m, face in zip(messages, order)]]
  transfers between devices with their start and end apart: 8 -> 8, of which waited for: 1 -> 2; matrix products, arithmetic and copies ran while one was open for 0% -> 0% of each run, Pallas kernels for 4% -> 4%
where the time goes in v5:
time: 45.6 us; the launch traced here: 45.3 us
  starting transfers between devices  36.6 us (80%)
  Pallas kernels  6.23 us (14%)
  waiting for transfers between devices  1.44 us (3%)
  local copies, waits for them, and re-layouts  0.89 us (2%)
    ppermute x8, starting transfers between devices, exchange(): return [lax.ppermute(m, *plan[face]) for m, face in zip(messages, order)]  36.6 us
    pallas_call x5, Pallas kernels, call(): pl.pallas_call(kernel, out_shape=[s if hasattr(s, 'dtype') else jax.Shape...  6.23 us
    ppermute x8, waiting for transfers between devices, exchange(): return [lax.ppermute(m, *plan[face]) for m, face in zip(messages, order)]  1.44 us
  transfers between devices with their start and end apart: 8, of which 2 were waited for; matrix products, arithmetic and copies ran while one was open for 0% of the time, Pallas kernels for 4%

profile of v5, /device:TPU:7, one launch (start us, length us, event | category | flops | bytes accessed | tf_op | source)
XLA Modules:
  0.0 45.3 jit_solution(4317392213709915728)
XLA Ops:
  0.0 0.0 copy-start
  0.0 2.2 %shard_map.37 = (f32[200,128]{1,0:T(8,128)}, f32[272,128]{1,0:T(8,128)}, f32[272,128]{1,0:T(8,128)}, f32[272,128]{1,0:T(8,128)}, f32[272,128]{1,0:T(8,128)}) custom-call(f32[640,128]{1,0:T(8,128)} %bitcast.4, f32[80,128]{1,0:T(8,128)} %bitcast.8, s32[1,32]{1,0:T(1,128)} %bitcast.9), custom_call_target="tpu_custom_call" | custom-call | flops 1000000 | bytes 1000000 | tf_op jit(solution)/shard_map/pallas_call | solution.py:464
  2.2 14.0 %collective-permute-start = (f32[272,128]{1,0:T(8,128)}, f32[272,128]{1,0:T(8,128)S(1)}, u32[]{:S(2)}, u32[]{:S(2)}) collective-permute-start(f32[272,128]{1,0:T(8,128)} %get-tuple-element.19), channel_id=1, source_target_pairs={{4,8},{8,4},{12,16},{16,12},{20,24},{24,20},{28,32},{32,28},{36,40... | collective-permute-start | bytes 417800 | tf_op jit(solution)/shard_map/ppermute | solution.py:496
  16.2 5.6 %collective-permute-start.1 = (f32[272,128]{1,0:T(8,128)}, f32[272,128]{1,0:T(8,128)S(1)}, u32[]{:S(2)}, u32[]{:S(2)}) collective-permute-start(f32[272,128]{1,0:T(8,128)} %get-tuple-element.20), channel_id=1, source_target_pairs={{1,2},{2,1},{0,0},{3,3},{5,6},{6,5},{4,4},{7,7},{9,10},{10,9},{8,8... | collective-permute-start | bytes 417800 | tf_op jit(solution)/shard_map/ppermute | solution.py:496
  21.8 1.9 %collective-permute-start.2 = (f32[272,128]{1,0:T(8,128)}, f32[272,128]{1,0:T(8,128)S(1)}, u32[]{:S(2)}, u32[]{:S(2)}) collective-permute-start(f32[272,128]{1,0:T(8,128)} %get-tuple-element.21), channel_id=1, source_target_pairs={{0,4},{4,0},{8,12},{12,8},{16,20},{20,16},{24,28},{28,24},{32,36},... | collective-permute-start | bytes 417800 | tf_op jit(solution)/shard_map/ppermute | solution.py:496
  23.7 1.9 %collective-permute-start.3 = (f32[272,128]{1,0:T(8,128)}, f32[272,128]{1,0:T(8,128)S(1)}, u32[]{:S(2)}, u32[]{:S(2)}) collective-permute-start(f32[272,128]{1,0:T(8,128)} %get-tuple-element.22), channel_id=1, source_target_pairs={{0,1},{1,0},{2,3},{3,2},{4,5},{5,4},{6,7},{7,6},{8,9},{9,8},{10,11... | collective-permute-start | bytes 417800 | tf_op jit(solution)/shard_map/ppermute | solution.py:496
  25.6 0.0 copy-done
  25.6 0.0 copy-start.1
  25.6 0.9 %copy-done.1 = f32[200,128]{1,0:T(8,128)S(1)} copy-done((f32[200,128]{1,0:T(8,128)S(1)}, f32[200,128]{1,0:T(8,128)}, u32[]{:S(2)}) %copy-start.1) | copy-done | bytes 102424
  26.5 1.1 %shard_map.38 = (f32[640,128]{1,0:T(8,128)S(1)}, bf16[256,256]{1,0:T(8,128)(2,1)S(1)}) custom-call(f32[640,128]{1,0:T(8,128)S(1)} %bitcast.5, f32[200,128]{1,0:T(8,128)S(1)} %copy-done.1), custom_call_target="tpu_custom_call" | custom-call | flops 10000000 | bytes 1000000 | tf_op jit(solution)/shard_map/pallas_call | solution.py:464
  27.6 0.0 collective-permute-done.r0.c0
  27.7 0.0 collective-permute-done.1.r1.c1
  27.7 0.1 collective-permute-done.2.r2.c2
  27.8 0.0 collective-permute-done.3.r3.c3
  27.8 0.8 %shard_map.39 = (f32[640,128]{1,0:T(8,128)S(1)}, f32[240,128]{1,0:T(8,128)S(1)}, f32[240,128]{1,0:T(8,128)S(1)}, f32[240,128]{1,0:T(8,128)S(1)}, f32[240,128]{1,0:T(8,128)S(1)}) custom-call(f32[640,128]{1,0:T(8,128)S(1)} %bitcast.6, f32[200,128]{1,0:T(8,128)S(1)} %copy-done.1, f32[640,128]{1,0:T(8,128)S(1)} %get-tuple-element.18.acc, ...), custom_call_target="tpu_custom_call" | custom-call | flops 1000000 | bytes 1000000 | tf_op jit(solution)/shard_map/pallas_call | solution.py:464
  28.6 3.9 %collective-permute-start.4 = (f32[240,128]{1,0:T(8,128)S(1)}, f32[240,128]{1,0:T(8,128)S(1)}, u32[]{:S(2)}, u32[]{:S(2)}) collective-permute-start(f32[240,128]{1,0:T(8,128)S(1)} %get-tuple-element.25), channel_id=1, source_target_pairs={{4,8},{8,4},{12,16},{16,12},{20,24},{24,20},{28,32},{32,28},{36,40... | collective-permute-start | bytes 368648 | tf_op jit(solution)/shard_map/ppermute | solution.py:496
  32.5 5.4 %collective-permute-start.5 = (f32[240,128]{1,0:T(8,128)S(1)}, f32[240,128]{1,0:T(8,128)S(1)}, u32[]{:S(2)}, u32[]{:S(2)}) collective-permute-start(f32[240,128]{1,0:T(8,128)S(1)} %get-tuple-element.26), channel_id=1, source_target_pairs={{1,2},{2,1},{0,0},{3,3},{5,6},{6,5},{4,4},{7,7},{9,10},{10,9},{8,8... | collective-permute-start | bytes 368648 | tf_op jit(solution)/shard_map/ppermute | solution.py:496
  38.0 1.9 %collective-permute-start.6 = (f32[240,128]{1,0:T(8,128)S(1)}, f32[240,128]{1,0:T(8,128)S(1)}, u32[]{:S(2)}, u32[]{:S(2)}) collective-permute-start(f32[240,128]{1,0:T(8,128)S(1)} %get-tuple-element.27), channel_id=1, source_target_pairs={{0,4},{4,0},{8,12},{12,8},{16,20},{20,16},{24,28},{28,24},{32,36},... | collective-permute-start | bytes 368648 | tf_op jit(solution)/shard_map/ppermute | solution.py:496
  39.9 1.9 %collective-permute-start.7 = (f32[240,128]{1,0:T(8,128)S(1)}, f32[240,128]{1,0:T(8,128)S(1)}, u32[]{:S(2)}, u32[]{:S(2)}) collective-permute-start(f32[240,128]{1,0:T(8,128)S(1)} %get-tuple-element.28), channel_id=1, source_target_pairs={{0,1},{1,0},{2,3},{3,2},{4,5},{5,4},{6,7},{7,6},{8,9},{9,8},{10,11... | collective-permute-start | bytes 368648 | tf_op jit(solution)/shard_map/ppermute | solution.py:496
  41.8 0.8 %shard_map.40.acc = f32[640,128]{1,0:T(8,128)S(1)} custom-call(f32[640,128]{1,0:T(8,128)S(1)} %get-tuple-element.23.s_ref, f32[200,128]{1,0:T(8,128)S(1)} %copy-done.1, bf16[256,256]{1,0:T(8,128)(2,1)S(1)} %get-tuple-element.24.wm_ref), custom_call_target="tpu_custom_call" | custom-call | flops 10000000 | bytes 1000000 | tf_op jit(solution)/shard_map/pallas_call | solution.py:464
  42.6 0.0 collective-permute-done.4.r0
  42.6 1.3 %collective-permute-done.5.r1 = f32[240,128]{1,0:T(8,128)S(1)} collective-permute-done((f32[240,128]{1,0:T(8,128)S(1)}, f32[240,128]{1,0:T(8,128)S(1)}, u32[]{:S(2)}, u32[]{:S(2)}) %collective-permute-start.5) | collective-permute-done | bytes 122912 | tf_op jit(solution)/shard_map/ppermute | solution.py:496
  43.9 0.0 collective-permute-done.6.r2
  43.9 0.0 collective-permute-done.7.r3
  43.9 1.3 %shard_map.41 = f32[640,128]{1,0:T(8,128)} custom-call(f32[640,128]{1,0:T(8,128)S(1)} %bitcast.7, f32[640,128]{1,0:T(8,128)S(1)} %get-tuple-element.23.s_ref, f32[200,128]{1,0:T(8,128)S(1)} %copy-done.1, f32[640,128]{1,0:T(8,128)S(1)} %shard_map.40.acc, f32[272,128]{1,0:T(8,128)S(1)} %collective-permute-done.r0.c0, ...), custom_call_target="tpu_custom_call" | custom-call | flops 1000000 | bytes 1000000 | tf_op jit(solution)/shard_map/pallas_call | solution.py:464
Async XLA Ops:
  0.0 25.6 %copy-start = (f32[8,5,4,4,128]{4,3,2,1,0:T(4,128)S(1)}, f32[8,5,4,4,128]{4,3,2,1,0:T(4,128)}, u32[]{:S(2)}) copy-start(f32[8,5,4,4,128]{4,3,2,1,0:T(4,128)} %param.3) | copy-start | bytes 983044
  2.2 25.5 %collective-permute-start = (f32[272,128]{1,0:T(8,128)}, f32[272,128]{1,0:T(8,128)S(1)}, u32[]{:S(2)}, u32[]{:S(2)}) collective-permute-start(f32[272,128]{1,0:T(8,128)} %get-tuple-element.19), channel_id=1, source_target_pairs={{4,8},{8,4},{12,16},{16,12},{20,24},{24,20},{28,32},{32,28},{36,40... | collective-permute-start | bytes 417800 | tf_op jit(solution)/shard_map/ppermute | solution.py:496
  16.2 11.5 %collective-permute-start.1 = (f32[272,128]{1,0:T(8,128)}, f32[272,128]{1,0:T(8,128)S(1)}, u32[]{:S(2)}, u32[]{:S(2)}) collective-permute-start(f32[272,128]{1,0:T(8,128)} %get-tuple-element.20), channel_id=1, source_target_pairs={{1,2},{2,1},{0,0},{3,3},{5,6},{6,5},{4,4},{7,7},{9,10},{10,9},{8,8... | collective-permute-start | bytes 417800 | tf_op jit(solution)/shard_map/ppermute | solution.py:496
  21.8 6.0 %collective-permute-start.2 = (f32[272,128]{1,0:T(8,128)}, f32[272,128]{1,0:T(8,128)S(1)}, u32[]{:S(2)}, u32[]{:S(2)}) collective-permute-start(f32[272,128]{1,0:T(8,128)} %get-tuple-element.21), channel_id=1, source_target_pairs={{0,4},{4,0},{8,12},{12,8},{16,20},{20,16},{24,28},{28,24},{32,36},... | collective-permute-start | bytes 417800 | tf_op jit(solution)/shard_map/ppermute | solution.py:496
  23.7 4.1 %collective-permute-start.3 = (f32[272,128]{1,0:T(8,128)}, f32[272,128]{1,0:T(8,128)S(1)}, u32[]{:S(2)}, u32[]{:S(2)}) collective-permute-start(f32[272,128]{1,0:T(8,128)} %get-tuple-element.22), channel_id=1, source_target_pairs={{0,1},{1,0},{2,3},{3,2},{4,5},{5,4},{6,7},{7,6},{8,9},{9,8},{10,11... | collective-permute-start | bytes 417800 | tf_op jit(solution)/shard_map/ppermute | solution.py:496
  25.6 0.9 %copy-start.1 = (f32[200,128]{1,0:T(8,128)S(1)}, f32[200,128]{1,0:T(8,128)}, u32[]{:S(2)}) copy-start(f32[200,128]{1,0:T(8,128)} %get-tuple-element.17.coef_ref) | copy-start | bytes 307204
  28.6 14.0 %collective-permute-start.4 = (f32[240,128]{1,0:T(8,128)S(1)}, f32[240,128]{1,0:T(8,128)S(1)}, u32[]{:S(2)}, u32[]{:S(2)}) collective-permute-start(f32[240,128]{1,0:T(8,128)S(1)} %get-tuple-element.25), channel_id=1, source_target_pairs={{4,8},{8,4},{12,16},{16,12},{20,24},{24,20},{28,32},{32,28},{36,40... | collective-permute-start | bytes 368648 | tf_op jit(solution)/shard_map/ppermute | solution.py:496
  32.5 11.4 %collective-permute-start.5 = (f32[240,128]{1,0:T(8,128)S(1)}, f32[240,128]{1,0:T(8,128)S(1)}, u32[]{:S(2)}, u32[]{:S(2)}) collective-permute-start(f32[240,128]{1,0:T(8,128)S(1)} %get-tuple-element.26), channel_id=1, source_target_pairs={{1,2},{2,1},{0,0},{3,3},{5,6},{6,5},{4,4},{7,7},{9,10},{10,9},{8,8... | collective-permute-start | bytes 368648 | tf_op jit(solution)/shard_map/ppermute | solution.py:496
  38.0 6.0 %collective-permute-start.6 = (f32[240,128]{1,0:T(8,128)S(1)}, f32[240,128]{1,0:T(8,128)S(1)}, u32[]{:S(2)}, u32[]{:S(2)}) collective-permute-start(f32[240,128]{1,0:T(8,128)S(1)} %get-tuple-element.27), channel_id=1, source_target_pairs={{0,4},{4,0},{8,12},{12,8},{16,20},{20,16},{24,28},{28,24},{32,36},... | collective-permute-start | bytes 368648 | tf_op jit(solution)/shard_map/ppermute | solution.py:496
  39.9 4.1 %collective-permute-start.7 = (f32[240,128]{1,0:T(8,128)S(1)}, f32[240,128]{1,0:T(8,128)S(1)}, u32[]{:S(2)}, u32[]{:S(2)}) collective-permute-start(f32[240,128]{1,0:T(8,128)S(1)} %get-tuple-element.28), channel_id=1, source_target_pairs={{0,1},{1,0},{2,3},{3,2},{4,5},{5,4},{6,7},{7,6},{8,9},{9,8},{10,11... | collective-permute-start | bytes 368648 | tf_op jit(solution)/shard_map/ppermute | solution.py:496

commit v6 on v5

--- a/solution.py
+++ b/solution.py
@@ -257,7 +257,7 @@
     return out
 
 
-def volume(load, coef_ref, wm_ref, acc, ops, aux):
+def volume(load, coef_ref, wm_ref, acc, ops, aux, result):
     top_lane = lax.broadcasted_iota(jnp.int32, (COLS, LANES), 1) % 4 == 3
     chunk = 128
 
@@ -333,6 +333,8 @@
                             top_lane, pltpu.roll(tt[i], LANES - 1, 1), pltpu.roll(tt[i], 1, 1)
                         )
                         total = total + coef(coef_ref, SZ, x, y) * (other - tt[i])
+                    else:
+                        total = result(f, x, y, tt[i], total)
                     acc[r : r + 8, :] = total
 
 
@@ -345,7 +347,7 @@
     return total
 
 
-def add_faces(load, coef_ref, recv, coef_recv, odd_x, odd_y, acc, work, wide, finish):
+def add_faces(load, coef_ref, recv, coef_recv, odd_x, odd_y, acc, work, wide, scale, finish):
     for face in range(4):
         r = COEF_AT + 28
         chosen = selection(coef_recv[face][r : r + 1, :])
@@ -367,7 +369,7 @@
 
         for n in range(4):
             line = [(k, n) if axis == 0 else (n, k) for k in range(4)]
-            nu3 = 3.0 * coef(coef_ref, NU, *line[0])
+            nu3 = (3.0 * scale) * coef(coef_ref, NU, *line[0])
             shift, extra = [], []
             for low in (True, False):
                 place = line[0] if low else line[3]
@@ -378,7 +380,7 @@
                     dp = dp - (0.4 * v[d]) * far_t[1 + d]
                 far_g = flux(axis, far_t, v, dp, far_t[4] + dp, pick_coef(low, 4, n))
                 far_nu = pick_coef(low, 5, n)
-                s3 = 3.0 * jnp.maximum(
+                s3 = (3.0 * scale) * jnp.maximum(
                     coef(coef_ref, SX + axis, *place), pick_coef(low, 6, n)
                 )
                 moved, added = [], []
@@ -388,7 +390,7 @@
                     b = wide[wide_at(2 * axis + 1, f, n)]
                     far_d = jnp.where(odd, a, b) if low else jnp.where(odd, b, a)
                     far_q = far_d - 3.0 * gap if low else far_d + 3.0 * gap
-                    value = 3.0 * (far_nu * far_q - far_g[f])
+                    value = (3.0 * scale) * (far_nu * far_q - far_g[f])
                     added.append(s3 * gap - value if low else s3 * gap + value)
                     moved.append(-(nu3 * far_t[f]) if low else nu3 * far_t[f])
                 shift.append(moved)
@@ -421,11 +423,17 @@
 
 def first_volume(t_ref, coef_ref, acc, wm_ref, ops, aux):
     span_table(wm_ref)
-    volume(lambda f, x, y: tan_in(t_ref, f, x, y), coef_ref, wm_ref, acc, ops, aux)
-
-
-def second_volume(s_ref, coef_ref, wm_ref, acc, ops, aux):
-    volume(loader(s_ref), coef_ref, wm_ref, acc, ops, aux)
+    volume(
+        lambda f, x, y: tan_in(t_ref, f, x, y), coef_ref, wm_ref, acc, ops, aux,
+        lambda f, x, y, t, total: t + STEP * total,
+    )
+
+
+def second_volume(t_ref, s_ref, coef_ref, wm_ref, acc, ops, aux):
+    def result(f, x, y, s, total):
+        return 0.5 * tan_in(t_ref, f, x, y) + (0.5 * s + (0.5 * STEP) * total)
+
+    volume(loader(s_ref), coef_ref, wm_ref, acc, ops, aux, result)
 
 
 def first_faces(t_ref, coef_ref, acc, r0, r1, r2, r3, s_ref, m0, m1, m2, m3, work, wide):
@@ -435,28 +443,27 @@
 
     def finish(f, x, y, total):
         r = row(f, x, y)
-        s_ref[r : r + 8, :] = load(f, x, y) + STEP * total
+        s_ref[r : r + 8, :] = total
 
     faces = by_face((r0, r1, r2, r3), ORDER_1)
-    add_faces(load, coef_ref, faces, faces, odd_x, odd_y, acc, work, wide, finish)
+    add_faces(load, coef_ref, faces, faces, odd_x, odd_y, acc, work, wide, STEP, finish)
     sent = by_face((m0, m1, m2, m3), ORDER_2)
     pack_faces(loader(s_ref), coef_ref, sent, odd_x, odd_y, wide)
 
 
 def second_faces(
-    t_ref, s_ref, coef_ref, acc, c0, c1, c2, c3, r0, r1, r2, r3, out_ref, work, wide
+    s_ref, coef_ref, acc, c0, c1, c2, c3, r0, r1, r2, r3, out_ref, work, wide
 ):
     odd_x = lax.axis_index("gx") % 2 == 1
     odd_y = lax.axis_index("gy") % 2 == 1
     load = loader(s_ref)
 
     def finish(f, x, y, total):
-        value = 0.5 * tan_in(t_ref, f, x, y) + (0.5 * load(f, x, y) + (0.5 * STEP) * total)
-        out_ref[pl.ds(f * 16 + x * 4 + y, COLS, stride=80), :] = value
+        out_ref[pl.ds(f * 16 + x * 4 + y, COLS, stride=80), :] = total
 
     add_faces(
         load, coef_ref, by_face((r0, r1, r2, r3), ORDER_2),
-        by_face((c0, c1, c2, c3), ORDER_1), odd_x, odd_y, acc, work, wide, finish,
+        by_face((c0, c1, c2, c3), ORDER_1), odd_x, odd_y, acc, work, wide, 0.5 * STEP, finish,
     )
 
 
@@ -529,8 +536,8 @@
         first_faces, [whole] + [short] * 4, work, [t, coefs, inner, *got], 1000000
     )
     again = exchange(faces, ORDER_2)
-    (inner,) = call(second_volume, [whole], volume_scratch, [s, coefs, wm], 10000000)
-    (out,) = call(second_faces, [whole], work, [t, s, coefs, inner, *got, *again], 1000000)
+    (inner,) = call(second_volume, [whole], volume_scratch, [t, s, coefs, wm], 10000000)
+    (out,) = call(second_faces, [whole], work, [s, coefs, inner, *got, *again], 1000000)
     return out.reshape(tangent.shape)
 
 

time: 45.6 us -> 45.5 us (level)
  no operation moved by 1% of the time
where the time goes in v6:
time: 45.5 us; the launch traced here: 45.1 us
  starting transfers between devices  36.6 us (80%)
  Pallas kernels  6.2 us (14%)
  waiting for transfers between devices  1.33 us (3%)
  local copies, waits for them, and re-layouts  0.89 us (2%)
    ppermute x8, starting transfers between devices, exchange(): return [lax.ppermute(m, *plan[face]) for m, face in zip(messages, order)]  36.6 us
    pallas_call x5, Pallas kernels, call(): pl.pallas_call(kernel, out_shape=[s if hasattr(s, 'dtype') else jax.Shape...  6.2 us
    ppermute x8, waiting for transfers between devices, exchange(): return [lax.ppermute(m, *plan[face]) for m, face in zip(messages, order)]  1.33 us
  transfers between devices with their start and end apart: 8, of which 2 were waited for; matrix products, arithmetic and copies ran while one was open for 0% of the time, Pallas kernels for 4%

profile of v6, /device:TPU:7, one launch (start us, length us, event | category | flops | bytes accessed | tf_op | source)
XLA Modules:
  0.0 45.1 jit_solution(4043957793123867956)
XLA Ops:
  0.0 0.0 copy-start
  0.0 2.2 %shard_map.37 = (f32[200,128]{1,0:T(8,128)}, f32[272,128]{1,0:T(8,128)}, f32[272,128]{1,0:T(8,128)}, f32[272,128]{1,0:T(8,128)}, f32[272,128]{1,0:T(8,128)}) custom-call(f32[640,128]{1,0:T(8,128)} %bitcast.4, f32[80,128]{1,0:T(8,128)} %bitcast.8, s32[1,32]{1,0:T(1,128)} %bitcast.9), custom_call_target="tpu_custom_call" | custom-call | flops 1000000 | bytes 1000000 | tf_op jit(solution)/shard_map/pallas_call | solution.py:471
  2.2 14.0 %collective-permute-start = (f32[272,128]{1,0:T(8,128)}, f32[272,128]{1,0:T(8,128)S(1)}, u32[]{:S(2)}, u32[]{:S(2)}) collective-permute-start(f32[272,128]{1,0:T(8,128)} %get-tuple-element.19), channel_id=1, source_target_pairs={{4,8},{8,4},{12,16},{16,12},{20,24},{24,20},{28,32},{32,28},{36,40... | collective-permute-start | bytes 417800 | tf_op jit(solution)/shard_map/ppermute | solution.py:503
  16.2 5.6 %collective-permute-start.1 = (f32[272,128]{1,0:T(8,128)}, f32[272,128]{1,0:T(8,128)S(1)}, u32[]{:S(2)}, u32[]{:S(2)}) collective-permute-start(f32[272,128]{1,0:T(8,128)} %get-tuple-element.20), channel_id=1, source_target_pairs={{1,2},{2,1},{0,0},{3,3},{5,6},{6,5},{4,4},{7,7},{9,10},{10,9},{8,8... | collective-permute-start | bytes 417800 | tf_op jit(solution)/shard_map/ppermute | solution.py:503
  21.8 1.9 %collective-permute-start.2 = (f32[272,128]{1,0:T(8,128)}, f32[272,128]{1,0:T(8,128)S(1)}, u32[]{:S(2)}, u32[]{:S(2)}) collective-permute-start(f32[272,128]{1,0:T(8,128)} %get-tuple-element.21), channel_id=1, source_target_pairs={{0,4},{4,0},{8,12},{12,8},{16,20},{20,16},{24,28},{28,24},{32,36},... | collective-permute-start | bytes 417800 | tf_op jit(solution)/shard_map/ppermute | solution.py:503
  23.7 1.9 %collective-permute-start.3 = (f32[272,128]{1,0:T(8,128)}, f32[272,128]{1,0:T(8,128)S(1)}, u32[]{:S(2)}, u32[]{:S(2)}) collective-permute-start(f32[272,128]{1,0:T(8,128)} %get-tuple-element.22), channel_id=1, source_target_pairs={{0,1},{1,0},{2,3},{3,2},{4,5},{5,4},{6,7},{7,6},{8,9},{9,8},{10,11... | collective-permute-start | bytes 417800 | tf_op jit(solution)/shard_map/ppermute | solution.py:503
  25.6 0.0 copy-done
  25.6 0.0 copy-start.1
  25.6 0.9 %copy-done.1 = f32[200,128]{1,0:T(8,128)S(1)} copy-done((f32[200,128]{1,0:T(8,128)S(1)}, f32[200,128]{1,0:T(8,128)}, u32[]{:S(2)}) %copy-start.1) | copy-done | bytes 102424
  26.5 1.1 %shard_map.38 = (f32[640,128]{1,0:T(8,128)S(1)}, bf16[256,256]{1,0:T(8,128)(2,1)S(1)}) custom-call(f32[640,128]{1,0:T(8,128)S(1)} %bitcast.5, f32[200,128]{1,0:T(8,128)S(1)} %copy-done.1), custom_call_target="tpu_custom_call" | custom-call | flops 10000000 | bytes 1000000 | tf_op jit(solution)/shard_map/pallas_call | solution.py:471
  27.7 0.0 collective-permute-done.r0.c0
  27.7 0.0 collective-permute-done.1.r1.c1
  27.7 0.1 collective-permute-done.2.r2.c2
  27.8 0.0 collective-permute-done.3.r3.c3
  27.8 0.8 %shard_map.39 = (f32[640,128]{1,0:T(8,128)S(1)}, f32[240,128]{1,0:T(8,128)S(1)}, f32[240,128]{1,0:T(8,128)S(1)}, f32[240,128]{1,0:T(8,128)S(1)}, f32[240,128]{1,0:T(8,128)S(1)}) custom-call(f32[640,128]{1,0:T(8,128)S(1)} %bitcast.6, f32[200,128]{1,0:T(8,128)S(1)} %copy-done.1, f32[640,128]{1,0:T(8,128)S(1)} %get-tuple-element.18.acc, ...), custom_call_target="tpu_custom_call" | custom-call | flops 1000000 | bytes 1000000 | tf_op jit(solution)/shard_map/pallas_call | solution.py:471
  28.6 4.0 %collective-permute-start.4 = (f32[240,128]{1,0:T(8,128)S(1)}, f32[240,128]{1,0:T(8,128)S(1)}, u32[]{:S(2)}, u32[]{:S(2)}) collective-permute-start(f32[240,128]{1,0:T(8,128)S(1)} %get-tuple-element.25), channel_id=1, source_target_pairs={{4,8},{8,4},{12,16},{16,12},{20,24},{24,20},{28,32},{32,28},{36,40... | collective-permute-start | bytes 368648 | tf_op jit(solution)/shard_map/ppermute | solution.py:503
  32.5 5.4 %collective-permute-start.5 = (f32[240,128]{1,0:T(8,128)S(1)}, f32[240,128]{1,0:T(8,128)S(1)}, u32[]{:S(2)}, u32[]{:S(2)}) collective-permute-start(f32[240,128]{1,0:T(8,128)S(1)} %get-tuple-element.26), channel_id=1, source_target_pairs={{1,2},{2,1},{0,0},{3,3},{5,6},{6,5},{4,4},{7,7},{9,10},{10,9},{8,8... | collective-permute-start | bytes 368648 | tf_op jit(solution)/shard_map/ppermute | solution.py:503
  37.9 1.9 %collective-permute-start.6 = (f32[240,128]{1,0:T(8,128)S(1)}, f32[240,128]{1,0:T(8,128)S(1)}, u32[]{:S(2)}, u32[]{:S(2)}) collective-permute-start(f32[240,128]{1,0:T(8,128)S(1)} %get-tuple-element.27), channel_id=1, source_target_pairs={{0,4},{4,0},{8,12},{12,8},{16,20},{20,16},{24,28},{28,24},{32,36},... | collective-permute-start | bytes 368648 | tf_op jit(solution)/shard_map/ppermute | solution.py:503
  39.8 1.9 %collective-permute-start.7 = (f32[240,128]{1,0:T(8,128)S(1)}, f32[240,128]{1,0:T(8,128)S(1)}, u32[]{:S(2)}, u32[]{:S(2)}) collective-permute-start(f32[240,128]{1,0:T(8,128)S(1)} %get-tuple-element.28), channel_id=1, source_target_pairs={{0,1},{1,0},{2,3},{3,2},{4,5},{5,4},{6,7},{7,6},{8,9},{9,8},{10,11... | collective-permute-start | bytes 368648 | tf_op jit(solution)/shard_map/ppermute | solution.py:503
  41.8 0.9 %shard_map.40.acc = f32[640,128]{1,0:T(8,128)S(1)} custom-call(f32[640,128]{1,0:T(8,128)S(1)} %bitcast.7, f32[640,128]{1,0:T(8,128)S(1)} %get-tuple-element.23.s_ref, f32[200,128]{1,0:T(8,128)S(1)} %copy-done.1, bf16[256,256]{1,0:T(8,128)(2,1)S(1)} %get-tuple-element.24.wm_ref), custom_call_target="tpu_custom_call" | custom-call | flops 10000000 | bytes 1000000 | tf_op jit(solution)/shard_map/pallas_call | solution.py:471
  42.7 0.0 collective-permute-done.4.r0
  42.7 1.2 %collective-permute-done.5.r1 = f32[240,128]{1,0:T(8,128)S(1)} collective-permute-done((f32[240,128]{1,0:T(8,128)S(1)}, f32[240,128]{1,0:T(8,128)S(1)}, u32[]{:S(2)}, u32[]{:S(2)}) %collective-permute-start.5) | collective-permute-done | bytes 122912 | tf_op jit(solution)/shard_map/ppermute | solution.py:503
  43.9 0.0 collective-permute-done.6.r2
  43.9 0.0 collective-permute-done.7.r3
  43.9 1.2 %shard_map.41 = f32[640,128]{1,0:T(8,128)} custom-call(f32[640,128]{1,0:T(8,128)S(1)} %get-tuple-element.23.s_ref, f32[200,128]{1,0:T(8,128)S(1)} %copy-done.1, f32[640,128]{1,0:T(8,128)S(1)} %shard_map.40.acc, f32[272,128]{1,0:T(8,128)S(1)} %collective-permute-done.r0.c0, f32[272,128]{1,0:T(8,128)S(1)} %collective-permute-done.1.r1.c1, ...), custom_call_target="tpu_custom_call" | custom-call | flops 1000000 | bytes 1000000 | tf_op jit(solution)/shard_map/pallas_call | solution.py:471
Async XLA Ops:
  0.0 25.6 %copy-start = (f32[8,5,4,4,128]{4,3,2,1,0:T(4,128)S(1)}, f32[8,5,4,4,128]{4,3,2,1,0:T(4,128)}, u32[]{:S(2)}) copy-start(f32[8,5,4,4,128]{4,3,2,1,0:T(4,128)} %param.3) | copy-start | bytes 983044
  2.2 25.5 %collective-permute-start = (f32[272,128]{1,0:T(8,128)}, f32[272,128]{1,0:T(8,128)S(1)}, u32[]{:S(2)}, u32[]{:S(2)}) collective-permute-start(f32[272,128]{1,0:T(8,128)} %get-tuple-element.19), channel_id=1, source_target_pairs={{4,8},{8,4},{12,16},{16,12},{20,24},{24,20},{28,32},{32,28},{36,40... | collective-permute-start | bytes 417800 | tf_op jit(solution)/shard_map/ppermute | solution.py:503
  16.2 11.5 %collective-permute-start.1 = (f32[272,128]{1,0:T(8,128)}, f32[272,128]{1,0:T(8,128)S(1)}, u32[]{:S(2)}, u32[]{:S(2)}) collective-permute-start(f32[272,128]{1,0:T(8,128)} %get-tuple-element.20), channel_id=1, source_target_pairs={{1,2},{2,1},{0,0},{3,3},{5,6},{6,5},{4,4},{7,7},{9,10},{10,9},{8,8... | collective-permute-start | bytes 417800 | tf_op jit(solution)/shard_map/ppermute | solution.py:503
  21.8 6.0 %collective-permute-start.2 = (f32[272,128]{1,0:T(8,128)}, f32[272,128]{1,0:T(8,128)S(1)}, u32[]{:S(2)}, u32[]{:S(2)}) collective-permute-start(f32[272,128]{1,0:T(8,128)} %get-tuple-element.21), channel_id=1, source_target_pairs={{0,4},{4,0},{8,12},{12,8},{16,20},{20,16},{24,28},{28,24},{32,36},... | collective-permute-start | bytes 417800 | tf_op jit(solution)/shard_map/ppermute | solution.py:503
  23.7 4.1 %collective-permute-start.3 = (f32[272,128]{1,0:T(8,128)}, f32[272,128]{1,0:T(8,128)S(1)}, u32[]{:S(2)}, u32[]{:S(2)}) collective-permute-start(f32[272,128]{1,0:T(8,128)} %get-tuple-element.22), channel_id=1, source_target_pairs={{0,1},{1,0},{2,3},{3,2},{4,5},{5,4},{6,7},{7,6},{8,9},{9,8},{10,11... | collective-permute-start | bytes 417800 | tf_op jit(solution)/shard_map/ppermute | solution.py:503
  25.6 0.9 %copy-start.1 = (f32[200,128]{1,0:T(8,128)S(1)}, f32[200,128]{1,0:T(8,128)}, u32[]{:S(2)}) copy-start(f32[200,128]{1,0:T(8,128)} %get-tuple-element.17.coef_ref) | copy-start | bytes 307204
  28.6 14.1 %collective-permute-start.4 = (f32[240,128]{1,0:T(8,128)S(1)}, f32[240,128]{1,0:T(8,128)S(1)}, u32[]{:S(2)}, u32[]{:S(2)}) collective-permute-start(f32[240,128]{1,0:T(8,128)S(1)} %get-tuple-element.25), channel_id=1, source_target_pairs={{4,8},{8,4},{12,16},{16,12},{20,24},{24,20},{28,32},{32,28},{36,40... | collective-permute-start | bytes 368648 | tf_op jit(solution)/shard_map/ppermute | solution.py:503
  32.5 11.4 %collective-permute-start.5 = (f32[240,128]{1,0:T(8,128)S(1)}, f32[240,128]{1,0:T(8,128)S(1)}, u32[]{:S(2)}, u32[]{:S(2)}) collective-permute-start(f32[240,128]{1,0:T(8,128)S(1)} %get-tuple-element.26), channel_id=1, source_target_pairs={{1,2},{2,1},{0,0},{3,3},{5,6},{6,5},{4,4},{7,7},{9,10},{10,9},{8,8... | collective-permute-start | bytes 368648 | tf_op jit(solution)/shard_map/ppermute | solution.py:503
  37.9 6.0 %collective-permute-start.6 = (f32[240,128]{1,0:T(8,128)S(1)}, f32[240,128]{1,0:T(8,128)S(1)}, u32[]{:S(2)}, u32[]{:S(2)}) collective-permute-start(f32[240,128]{1,0:T(8,128)S(1)} %get-tuple-element.27), channel_id=1, source_target_pairs={{0,4},{4,0},{8,12},{12,8},{16,20},{20,16},{24,28},{28,24},{32,36},... | collective-permute-start | bytes 368648 | tf_op jit(solution)/shard_map/ppermute | solution.py:503
  39.8 4.1 %collective-permute-start.7 = (f32[240,128]{1,0:T(8,128)S(1)}, f32[240,128]{1,0:T(8,128)S(1)}, u32[]{:S(2)}, u32[]{:S(2)}) collective-permute-start(f32[240,128]{1,0:T(8,128)S(1)} %get-tuple-element.28), channel_id=1, source_target_pairs={{0,1},{1,0},{2,3},{3,2},{4,5},{5,4},{6,7},{7,6},{8,9},{9,8},{10,11... | collective-permute-start | bytes 368648 | tf_op jit(solution)/shard_map/ppermute | solution.py:503

commit v7 on v6

--- a/solution.py
+++ b/solution.py
@@ -18,7 +18,7 @@
 COEF_ROWS = 32
 COEF_AT = FACE + HALF
 PLACE_AT = 12 * 16
-ORDER_1 = (1, 3, 0, 2)
+ORDER_1 = (0, 1, 3, 2)
 ORDER_2 = (1, 3, 0, 2)
 
 

time: 45.5 us -> 45.5 us (level)
  starting transfers between devices: 36.6 us -> 37.1 us
  waiting for transfers between devices: 1.33 us -> 0.87 us
    ppermute x8, starting transfers between devices: 36.6 us -> 37.1 us  [exchange(): return [lax.ppermute(m, *plan[face]) for m, face in zip(messages, order)]]
    ppermute x8, waiting for transfers between devices: 1.33 us -> 0.87 us  [exchange(): return [lax.ppermute(m, *plan[face]) for m, face in zip(messages, order)]]
  transfers between devices with their start and end apart: 8 -> 8, of which waited for: 2 -> 1; matrix products, arithmetic and copies ran while one was open for 0% -> 0% of each run, Pallas kernels for 4% -> 4%
where the time goes in v7:
time: 45.5 us; the launch traced here: 45.2 us
  starting transfers between devices  37.1 us (82%)
  Pallas kernels  6.22 us (14%)
  local copies, waits for them, and re-layouts  0.89 us (2%)
  waiting for transfers between devices  0.87 us (2%)
    ppermute x8, starting transfers between devices, exchange(): return [lax.ppermute(m, *plan[face]) for m, face in zip(messages, order)]  37.1 us
    pallas_call x5, Pallas kernels, call(): pl.pallas_call(kernel, out_shape=[s if hasattr(s, 'dtype') else jax.Shape...  6.22 us
  transfers between devices with their start and end apart: 8, of which 1 were waited for; matrix products, arithmetic and copies ran while one was open for 0% of the time, Pallas kernels for 4%

profile of v7, /device:TPU:7, one launch (start us, length us, event | category | flops | bytes accessed | tf_op | source)
XLA Modules:
  0.0 45.2 jit_solution(12783657835911850783)
XLA Ops:
  0.0 0.0 copy-start
  0.0 2.2 %shard_map.37 = (f32[200,128]{1,0:T(8,128)}, f32[272,128]{1,0:T(8,128)}, f32[272,128]{1,0:T(8,128)}, f32[272,128]{1,0:T(8,128)}, f32[272,128]{1,0:T(8,128)}) custom-call(f32[640,128]{1,0:T(8,128)} %bitcast.4, f32[80,128]{1,0:T(8,128)} %bitcast.8, s32[1,32]{1,0:T(1,128)} %bitcast.9), custom_call_target="tpu_custom_call" | custom-call | flops 1000000 | bytes 1000000 | tf_op jit(solution)/shard_map/pallas_call | solution.py:471
  2.2 3.2 %collective-permute-start = (f32[272,128]{1,0:T(8,128)}, f32[272,128]{1,0:T(8,128)S(1)}, u32[]{:S(2)}, u32[]{:S(2)}) collective-permute-start(f32[272,128]{1,0:T(8,128)} %get-tuple-element.19), channel_id=1, source_target_pairs={{0,4},{4,0},{8,12},{12,8},{16,20},{20,16},{24,28},{28,24},{32,36},... | collective-permute-start | bytes 417800 | tf_op jit(solution)/shard_map/ppermute | solution.py:503
  5.4 12.8 %collective-permute-start.1 = (f32[272,128]{1,0:T(8,128)}, f32[272,128]{1,0:T(8,128)S(1)}, u32[]{:S(2)}, u32[]{:S(2)}) collective-permute-start(f32[272,128]{1,0:T(8,128)} %get-tuple-element.20), channel_id=1, source_target_pairs={{4,8},{8,4},{12,16},{16,12},{20,24},{24,20},{28,32},{32,28},{36,40... | collective-permute-start | bytes 417800 | tf_op jit(solution)/shard_map/ppermute | solution.py:503
  18.3 6.8 %collective-permute-start.2 = (f32[272,128]{1,0:T(8,128)}, f32[272,128]{1,0:T(8,128)S(1)}, u32[]{:S(2)}, u32[]{:S(2)}) collective-permute-start(f32[272,128]{1,0:T(8,128)} %get-tuple-element.21), channel_id=1, source_target_pairs={{1,2},{2,1},{0,0},{3,3},{5,6},{6,5},{4,4},{7,7},{9,10},{10,9},{8,8... | collective-permute-start | bytes 417800 | tf_op jit(solution)/shard_map/ppermute | solution.py:503
  25.1 1.9 %collective-permute-start.3 = (f32[272,128]{1,0:T(8,128)}, f32[272,128]{1,0:T(8,128)S(1)}, u32[]{:S(2)}, u32[]{:S(2)}) collective-permute-start(f32[272,128]{1,0:T(8,128)} %get-tuple-element.22), channel_id=1, source_target_pairs={{0,1},{1,0},{2,3},{3,2},{4,5},{5,4},{6,7},{7,6},{8,9},{9,8},{10,11... | collective-permute-start | bytes 417800 | tf_op jit(solution)/shard_map/ppermute | solution.py:503
  27.0 0.0 copy-done
  27.0 0.0 copy-start.1
  27.0 0.9 %copy-done.1 = f32[200,128]{1,0:T(8,128)S(1)} copy-done((f32[200,128]{1,0:T(8,128)S(1)}, f32[200,128]{1,0:T(8,128)}, u32[]{:S(2)}) %copy-start.1) | copy-done | bytes 102424
  27.9 1.1 %shard_map.38 = (f32[640,128]{1,0:T(8,128)S(1)}, bf16[256,256]{1,0:T(8,128)(2,1)S(1)}) custom-call(f32[640,128]{1,0:T(8,128)S(1)} %bitcast.5, f32[200,128]{1,0:T(8,128)S(1)} %copy-done.1), custom_call_target="tpu_custom_call" | custom-call | flops 10000000 | bytes 1000000 | tf_op jit(solution)/shard_map/pallas_call | solution.py:471
  29.0 0.0 collective-permute-done.r0.c0
  29.0 0.0 collective-permute-done.1.r1.c1
  29.1 0.0 collective-permute-done.2.r2.c2
  29.1 0.0 collective-permute-done.3.r3.c3
  29.1 0.8 %shard_map.39 = (f32[640,128]{1,0:T(8,128)S(1)}, f32[240,128]{1,0:T(8,128)S(1)}, f32[240,128]{1,0:T(8,128)S(1)}, f32[240,128]{1,0:T(8,128)S(1)}, f32[240,128]{1,0:T(8,128)S(1)}) custom-call(f32[640,128]{1,0:T(8,128)S(1)} %bitcast.6, f32[200,128]{1,0:T(8,128)S(1)} %copy-done.1, f32[640,128]{1,0:T(8,128)S(1)} %get-tuple-element.18.acc, ...), custom_call_target="tpu_custom_call" | custom-call | flops 1000000 | bytes 1000000 | tf_op jit(solution)/shard_map/pallas_call | solution.py:471
  29.8 1.9 %collective-permute-start.4 = (f32[240,128]{1,0:T(8,128)S(1)}, f32[240,128]{1,0:T(8,128)S(1)}, u32[]{:S(2)}, u32[]{:S(2)}) collective-permute-start(f32[240,128]{1,0:T(8,128)S(1)} %get-tuple-element.25), channel_id=1, source_target_pairs={{4,8},{8,4},{12,16},{16,12},{20,24},{24,20},{28,32},{32,28},{36,40... | collective-permute-start | bytes 368648 | tf_op jit(solution)/shard_map/ppermute | solution.py:503
  31.8 6.6 %collective-permute-start.5 = (f32[240,128]{1,0:T(8,128)S(1)}, f32[240,128]{1,0:T(8,128)S(1)}, u32[]{:S(2)}, u32[]{:S(2)}) collective-permute-start(f32[240,128]{1,0:T(8,128)S(1)} %get-tuple-element.26), channel_id=1, source_target_pairs={{1,2},{2,1},{0,0},{3,3},{5,6},{6,5},{4,4},{7,7},{9,10},{10,9},{8,8... | collective-permute-start | bytes 368648 | tf_op jit(solution)/shard_map/ppermute | solution.py:503
  38.4 1.9 %collective-permute-start.6 = (f32[240,128]{1,0:T(8,128)S(1)}, f32[240,128]{1,0:T(8,128)S(1)}, u32[]{:S(2)}, u32[]{:S(2)}) collective-permute-start(f32[240,128]{1,0:T(8,128)S(1)} %get-tuple-element.27), channel_id=1, source_target_pairs={{0,4},{4,0},{8,12},{12,8},{16,20},{20,16},{24,28},{28,24},{32,36},... | collective-permute-start | bytes 368648 | tf_op jit(solution)/shard_map/ppermute | solution.py:503
  40.3 1.9 %collective-permute-start.7 = (f32[240,128]{1,0:T(8,128)S(1)}, f32[240,128]{1,0:T(8,128)S(1)}, u32[]{:S(2)}, u32[]{:S(2)}) collective-permute-start(f32[240,128]{1,0:T(8,128)S(1)} %get-tuple-element.28), channel_id=1, source_target_pairs={{0,1},{1,0},{2,3},{3,2},{4,5},{5,4},{6,7},{7,6},{8,9},{9,8},{10,11... | collective-permute-start | bytes 368648 | tf_op jit(solution)/shard_map/ppermute | solution.py:503
  42.2 0.9 %shard_map.40.acc = f32[640,128]{1,0:T(8,128)S(1)} custom-call(f32[640,128]{1,0:T(8,128)S(1)} %bitcast.7, f32[640,128]{1,0:T(8,128)S(1)} %get-tuple-element.23.s_ref, f32[200,128]{1,0:T(8,128)S(1)} %copy-done.1, bf16[256,256]{1,0:T(8,128)(2,1)S(1)} %get-tuple-element.24.wm_ref), custom_call_target="tpu_custom_call" | custom-call | flops 10000000 | bytes 1000000 | tf_op jit(solution)/shard_map/pallas_call | solution.py:471
  43.1 0.0 collective-permute-done.4.r0
  43.1 0.0 collective-permute-done.5.r1
  43.1 0.8 %collective-permute-done.6.r2 = f32[240,128]{1,0:T(8,128)S(1)} collective-permute-done((f32[240,128]{1,0:T(8,128)S(1)}, f32[240,128]{1,0:T(8,128)S(1)}, u32[]{:S(2)}, u32[]{:S(2)}) %collective-permute-start.6) | collective-permute-done | bytes 122912 | tf_op jit(solution)/shard_map/ppermute | solution.py:503
  44.0 0.0 collective-permute-done.7.r3
  44.0 1.2 %shard_map.41 = f32[640,128]{1,0:T(8,128)} custom-call(f32[640,128]{1,0:T(8,128)S(1)} %get-tuple-element.23.s_ref, f32[200,128]{1,0:T(8,128)S(1)} %copy-done.1, f32[640,128]{1,0:T(8,128)S(1)} %shard_map.40.acc, f32[272,128]{1,0:T(8,128)S(1)} %collective-permute-done.r0.c0, f32[272,128]{1,0:T(8,128)S(1)} %collective-permute-done.1.r1.c1, ...), custom_call_target="tpu_custom_call" | custom-call | flops 1000000 | bytes 1000000 | tf_op jit(solution)/shard_map/pallas_call | solution.py:471
Async XLA Ops:
  0.0 27.0 %copy-start = (f32[8,5,4,4,128]{4,3,2,1,0:T(4,128)S(1)}, f32[8,5,4,4,128]{4,3,2,1,0:T(4,128)}, u32[]{:S(2)}) copy-start(f32[8,5,4,4,128]{4,3,2,1,0:T(4,128)} %param.3) | copy-start | bytes 983044
  2.2 26.8 %collective-permute-start = (f32[272,128]{1,0:T(8,128)}, f32[272,128]{1,0:T(8,128)S(1)}, u32[]{:S(2)}, u32[]{:S(2)}) collective-permute-start(f32[272,128]{1,0:T(8,128)} %get-tuple-element.19), channel_id=1, source_target_pairs={{0,4},{4,0},{8,12},{12,8},{16,20},{20,16},{24,28},{28,24},{32,36},... | collective-permute-start | bytes 417800 | tf_op jit(solution)/shard_map/ppermute | solution.py:503
  5.4 23.6 %collective-permute-start.1 = (f32[272,128]{1,0:T(8,128)}, f32[272,128]{1,0:T(8,128)S(1)}, u32[]{:S(2)}, u32[]{:S(2)}) collective-permute-start(f32[272,128]{1,0:T(8,128)} %get-tuple-element.20), channel_id=1, source_target_pairs={{4,8},{8,4},{12,16},{16,12},{20,24},{24,20},{28,32},{32,28},{36,40... | collective-permute-start | bytes 417800 | tf_op jit(solution)/shard_map/ppermute | solution.py:503
  18.3 10.8 %collective-permute-start.2 = (f32[272,128]{1,0:T(8,128)}, f32[272,128]{1,0:T(8,128)S(1)}, u32[]{:S(2)}, u32[]{:S(2)}) collective-permute-start(f32[272,128]{1,0:T(8,128)} %get-tuple-element.21), channel_id=1, source_target_pairs={{1,2},{2,1},{0,0},{3,3},{5,6},{6,5},{4,4},{7,7},{9,10},{10,9},{8,8... | collective-permute-start | bytes 417800 | tf_op jit(solution)/shard_map/ppermute | solution.py:503
  25.1 4.0 %collective-permute-start.3 = (f32[272,128]{1,0:T(8,128)}, f32[272,128]{1,0:T(8,128)S(1)}, u32[]{:S(2)}, u32[]{:S(2)}) collective-permute-start(f32[272,128]{1,0:T(8,128)} %get-tuple-element.22), channel_id=1, source_target_pairs={{0,1},{1,0},{2,3},{3,2},{4,5},{5,4},{6,7},{7,6},{8,9},{9,8},{10,11... | collective-permute-start | bytes 417800 | tf_op jit(solution)/shard_map/ppermute | solution.py:503
  27.0 0.9 %copy-start.1 = (f32[200,128]{1,0:T(8,128)S(1)}, f32[200,128]{1,0:T(8,128)}, u32[]{:S(2)}) copy-start(f32[200,128]{1,0:T(8,128)} %get-tuple-element.17.coef_ref) | copy-start | bytes 307204
  29.8 13.3 %collective-permute-start.4 = (f32[240,128]{1,0:T(8,128)S(1)}, f32[240,128]{1,0:T(8,128)S(1)}, u32[]{:S(2)}, u32[]{:S(2)}) collective-permute-start(f32[240,128]{1,0:T(8,128)S(1)} %get-tuple-element.25), channel_id=1, source_target_pairs={{4,8},{8,4},{12,16},{16,12},{20,24},{24,20},{28,32},{32,28},{36,40... | collective-permute-start | bytes 368648 | tf_op jit(solution)/shard_map/ppermute | solution.py:503
  31.8 11.4 %collective-permute-start.5 = (f32[240,128]{1,0:T(8,128)S(1)}, f32[240,128]{1,0:T(8,128)S(1)}, u32[]{:S(2)}, u32[]{:S(2)}) collective-permute-start(f32[240,128]{1,0:T(8,128)S(1)} %get-tuple-element.26), channel_id=1, source_target_pairs={{1,2},{2,1},{0,0},{3,3},{5,6},{6,5},{4,4},{7,7},{9,10},{10,9},{8,8... | collective-permute-start | bytes 368648 | tf_op jit(solution)/shard_map/ppermute | solution.py:503
  38.4 5.6 %collective-permute-start.6 = (f32[240,128]{1,0:T(8,128)S(1)}, f32[240,128]{1,0:T(8,128)S(1)}, u32[]{:S(2)}, u32[]{:S(2)}) collective-permute-start(f32[240,128]{1,0:T(8,128)S(1)} %get-tuple-element.27), channel_id=1, source_target_pairs={{0,4},{4,0},{8,12},{12,8},{16,20},{20,16},{24,28},{28,24},{32,36},... | collective-permute-start | bytes 368648 | tf_op jit(solution)/shard_map/ppermute | solution.py:503
  40.3 3.7 %collective-permute-start.7 = (f32[240,128]{1,0:T(8,128)S(1)}, f32[240,128]{1,0:T(8,128)S(1)}, u32[]{:S(2)}, u32[]{:S(2)}) collective-permute-start(f32[240,128]{1,0:T(8,128)S(1)} %get-tuple-element.28), channel_id=1, source_target_pairs={{0,1},{1,0},{2,3},{3,2},{4,5},{5,4},{6,7},{7,6},{8,9},{9,8},{10,11... | collective-permute-start | bytes 368648 | tf_op jit(solution)/shard_map/ppermute | solution.py:503
